TPU v7x, 128 devices: a whole 4x4x4 slice. The times are simulated.
128 devices in a mesh: grid: 16 (over z, x_hi, core), rec: 8 (over y, x_lo).
Axes of the slice: x: 4 (x_hi: 2, x_lo: 2; x = x_hi * 2 + x_lo), y: 4, z: 4, core: 2. Of those that a mesh axis runs over, the one named last changes fastest.
Arguments:
- adjoint: float32 [4096, 128, 256], P('rec', 'grid'), may hold values from -26 to 26, as said below
- courant: float32 [4, 128, 256], P(None, 'grid'), may hold values from 0.02 to 0.22
- detector: int32 [4096], P('rec'), may hold values from 0 to 32767
- sources: int32 [32768], P('grid'), may hold values from 0 to 32767, as said below
- emission: float32 [32768], P('grid'), may hold values from 0.3 to 3
Outputs:
- advanced: float32 [4096, 128, 256], P('rec', 'grid')
- gram: float32 [4096, 4096], P('grid', 'rec')
Inputs may be any that keep to these rules, and one draw needn't show every extreme that they name: `adjoint`: each receptor's field is rough from cell to cell; the fields of different receptors need not be independent of one another. The sources of the j-th run of 2048 entries are distinct cells of grid rows j * 8 to (j + 1) * 8 - 1, so each run is an ordering of all cells of those rows.
All inputs are finite; a program needn't handle non-finite values.
Results may differ from a plain program's by a relative error of at most 0.0008.
Values may be sent and summed in bfloat16 or wider, within the bound.
No kernel may reach another device: no remote copies, remote signals or barrier semaphores. Data moves between devices by JAX's collectives and lax.ppermute only.
A program may use at most 128 MiB of HBM per device.

v0:
```python
import jax
import jax.numpy as jnp
from jax import lax
from jax.sharding import PartitionSpec as P

STEPS = 2


def padded_2(block, sides, width):
    for axis, dim in sides:
        count = lax.axis_size(axis)
        forward = [(i, i + 1) for i in range(count - 1)]
        backward = [(target, source) for source, target in forward]
        low = lax.ppermute(
            lax.slice_in_dim(block, block.shape[dim] - width, None, axis=dim), axis, forward
        )
        high = lax.ppermute(lax.slice_in_dim(block, 0, width, axis=dim), axis, backward)
        block = jnp.concatenate([low, block, high], axis=dim)
    return block


def advance(extended, coef, pulses):
    center = extended[:, 1:-1]
    north = extended[:, 2:]
    south = extended[:, :-2]
    padded = jnp.pad(center, ((0, 0), (0, 0), (1, 1)))
    east = padded[:, :, 2:]
    west = padded[:, :, :-2]
    fresh = (
        center
        + coef[0] * (north - center)
        + coef[1] * (south - center)
        + coef[2] * (east - center)
        + coef[3] * (west - center)
    )
    return fresh + pulses


def pulse_mask(detector, first_row, rows, width):
    row_ids = first_row + jnp.arange(rows, dtype=jnp.int32)
    col_ids = jnp.arange(width, dtype=jnp.int32)
    det_row = detector // width
    det_col = detector % width
    hit = (det_row[:, None, None] == row_ids[None, :, None]) & (
        det_col[:, None, None] == col_ids[None, None, :]
    )
    return hit.astype(jnp.float32)


def contract(left, right):
    return lax.dot_general(
        left, right, (((1,), (1,)), ((), ())), preferred_element_type=jnp.float32
    )


def body(adjoint, courant, detector, sources, emission):
    groups, rows, width = adjoint.shape
    first_row = lax.axis_index("grid") * rows
    field = adjoint
    pulses = pulse_mask(detector, first_row, rows, width)
    for step in range(STEPS):
        extended = padded_2(field, (("grid", 1),), 1)
        field = advance(extended, courant, pulses)
    local_cells = sources - first_row * width
    picked = jnp.take(field.reshape(groups, rows * width), local_cells, axis=1)
    footprint = (picked * emission[None, :]).astype(jnp.bfloat16)
    n_grid = lax.axis_size("grid")
    total_sources = sources.shape[0] * n_grid
    gathered = lax.all_gather(footprint, "rec", axis=0, tiled=True)
    summed = lax.psum_scatter(
        contract(gathered, footprint), "grid", scatter_dimension=0, tiled=True
    )
    gram = summed / jnp.float32(total_sources)
    return (field, gram)


def solution(mesh):
    in_specs = (P("rec", "grid", None), P(None, "grid", None), P("rec"), P("grid"), P("grid"))
    out_specs = (P("rec", "grid", None), P("grid", "rec"))
    return jax.shard_map(body, mesh=mesh, in_specs=in_specs, out_specs=out_specs, check_vma=False)
```

profile of v0, /device:TPU:56, one launch (start us, length us, event | category | flops | bytes accessed | tf_op | source)
XLA Modules:
  0.0 545.4 jit_solution(16735223309082242095)
XLA Ops:
  7.2 3.5 copy.11
  10.8 2.0 copy-done
  12.9 3.9 collective-permute-start
  16.8 1.9 collective-permute-start.1
  18.8 0.1 broadcast_compare_fusion
  18.8 0.1 iota_compare_fusion
  19.0 7.7 %collective-permute-done = f32[512,1,256]{2,0,1:T(8,128)S(1)} collective-permute-done((f32[512,1,256]{2,0,1:T(8,128)S(1)}, f32[512,1,256]{2,0,1:T(8,128)S(1)}, u32[]{:S(2)}, u32[]{:S(2)}) %collective-permute-start) | collective-permute-done | bytes 524320 | tf_op jit(solution)/shard_map/ppermute | solution.py:17
  26.6 3.5 collective-permute-done.1
  30.1 9.3 %convert_add_fusion.1 = f32[512,8,256]{2,0,1:T(8,128)S(1)} fusion(f32[512,8,256]{2,0,1:T(8,128)} %copy-done, f32[512,1,256]{2,0,1:T(8,128)S(1)} %collective-permute-done.1, f32[512,1,256]{2,0,1:T(8,128)S(1)} %collective-permute-done, f32[8,256]{1,0:T(8,128)S(1)} %get-tuple-element.10, f32[8,256]{1,0:T(8,128)S(1)} %get-tuple-element.11, ...), kind=kLoop, calls=%fused_computation.6 | loop fusion | flops 17825792 | bytes 9605120 | tf_op jit(solution)/shard_map/add | solution.py:36
  39.5 2.0 copy-done.1
  41.5 2.8 collective-permute-start.2
  44.3 1.9 collective-permute-start.3
  46.3 6.8 %collective-permute-done.2 = f32[512,1,256]{2,0,1:T(8,128)S(1)} collective-permute-done((f32[512,1,256]{2,0,1:T(8,128)S(1)}, f32[512,1,256]{2,0,1:T(8,128)S(1)}, u32[]{:S(2)}, u32[]{:S(2)}) %collective-permute-start.2) | collective-permute-done | bytes 524320 | tf_op jit(solution)/shard_map/ppermute | solution.py:17
  53.1 4.1 collective-permute-done.3
  57.2 11.1 %convert_add_fusion = f32[512,8,256]{2,0,1:T(8,128)} fusion(f32[512,8,256]{2,0,1:T(8,128)} %copy-done.1, f32[512,1,256]{2,0,1:T(8,128)S(1)} %collective-permute-done.3, f32[512,1,256]{2,0,1:T(8,128)S(1)} %collective-permute-done.2, f32[8,256]{1,0:T(8,128)S(1)} %get-tuple-element.10, f32[8,256]{1,0:T(8,128)S(1)} %get-tuple-element.11, ...), kind=kLoop, calls=%fused_computation.5 | loop fusion | flops 17825792 | bytes 9605120 | tf_op jit(solution)/shard_map/add | solution.py:36
  68.3 5.3 copy.18
  73.6 11.7 %gather_fusion = f32[2048,512]{1,0:T(8,128)} fusion(f32[512,2048]{0,1:T(8,128)} %bitcast.12, s32[2048]{0:T(1024)S(1)} %fusion.24), kind=kCustom, calls=%fused_computation | custom fusion | bytes 8396800 | tf_op jit(solution)/shard_map/jit(_take)/gather | solution.py:65
  85.4 3.5 fusion.27
  88.9 0.2 reduce-scatter.2.cloned.1.call-start
  89.2 328.2 %all-gather.2.cloned.1.call-done = bf16[4096,2048]{0,1:T(8,128)(2,1)} async-done(((bf16[512,2048]{0,1:T(8,128)(2,1)}), bf16[4096,2048]{0,1:T(8,128)(2,1)}) %all-gather.2.cloned.1.call-update) | async-done | bytes 16777232 | tf_op jit(solution)/shard_map/all_gather | solution.py:69
  417.4 15.9 %fusion.26 = f32[4096,512]{1,0:T(8,128)} fusion(bf16[4096,2048]{0,1:T(8,128)(2,1)} %all-gather.2.cloned.1.call-done, f32[2048,512]{1,0:T(8,128)} %gather_fusion, f32[2048]{0:T(1024)S(1)} %copy-done.4, pred[2048]{0:T(1024)(128)(4,1)S(1)} %compare_and_fusion), kind=kOutput, calls=%fused_computation.55 | convolution fusion | flops 8593080320 | bytes 29370368 | tf_op jit(solution)/shard_map/dot_general | solution.py:51
  433.3 6.6 %copy.19 = f32[512,8,256]{2,1,0:T(8,128)} copy(f32[512,8,256]{2,0,1:T(8,128)} %convert_add_fusion) | data formatting | bytes 8388608
  440.0 96.7 %reduce-scatter.2.cloned.1.call-done = f32[256,512]{1,0:T(8,128)} async-done(((f32[4096,512]{1,0:T(8,128)}), f32[256,512]{1,0:T(8,128)}) %reduce-scatter.2.cloned.1.call-update) | async-done | bytes 524304 | tf_op jit(solution)/shard_map/reduce_scatter | solution.py:70
  536.6 1.9 broadcast_multiply_fusion
  (20 shorter events, 0.3 us)
Async XLA Ops:
  7.2 11.6 %copy-start.5 = (s32[512]{0:T(512)S(1)}, s32[512]{0:T(512)}, u32[]{:S(2)}) copy-start(s32[512]{0:T(512)} %param.7) | copy-start | bytes 6148
  7.2 11.7 %copy-start.2 = (f32[4,8,256]{2,1,0:T(8,128)S(1)}, f32[4,8,256]{2,1,0:T(8,128)}, u32[]{:S(2)}) copy-start(f32[4,8,256]{2,1,0:T(8,128)} %param.6) | copy-start | bytes 98308
  7.2 410.2 %all-gather.2.cloned.1.call-start = ((), (), s32[]{:S(2)}) async-start(), calls=%async_computation.1 | async-start | bytes 18874368 | tf_op jit(solution)/shard_map/all_gather | solution.py:69
  10.8 2.0 copy-start
  12.9 13.8 %collective-permute-start = (f32[512,1,256]{2,0,1:T(8,128)S(1)}, f32[512,1,256]{2,0,1:T(8,128)S(1)}, u32[]{:S(2)}, u32[]{:S(2)}) collective-permute-start(f32[512,1,256]{2,0,1:T(8,128)S(1)} %get-tuple-element.6), channel_id=1, source_target_pairs={{8,0},{16,8},{24,16},{32,24},{40,32},{48,40},{56,48},{64,56},{72,6... | collective-permute-start | bytes 1572872 | tf_op jit(solution)/shard_map/ppermute | solution.py:17
  16.8 13.3 %collective-permute-start.1 = (f32[512,1,256]{2,0,1:T(8,128)S(1)}, f32[512,1,256]{2,0,1:T(8,128)S(1)}, u32[]{:S(2)}, u32[]{:S(2)}) collective-permute-start(f32[512,1,256]{2,0,1:T(8,128)S(1)} %get-tuple-element.7), channel_id=1, source_target_pairs={{0,8},{8,16},{16,24},{24,32},{32,40},{40,48},{48,56},{56,64},{64,7... | collective-permute-start | bytes 1572872 | tf_op jit(solution)/shard_map/ppermute | solution.py:14
  30.1 16.2 %copy-start.3 = (s32[2048]{0:T(1024)S(1)}, s32[2048]{0:T(1024)}, u32[]{:S(2)}) copy-start(s32[2048]{0:T(1024)} %param.8) | copy-start | bytes 24580
  39.5 2.0 copy-start.1
  41.5 11.5 %collective-permute-start.2 = (f32[512,1,256]{2,0,1:T(8,128)S(1)}, f32[512,1,256]{2,0,1:T(8,128)S(1)}, u32[]{:S(2)}, u32[]{:S(2)}) collective-permute-start(f32[512,1,256]{2,0,1:T(8,128)S(1)} %get-tuple-element.4), channel_id=1, source_target_pairs={{8,0},{16,8},{24,16},{32,24},{40,32},{48,40},{56,48},{64,56},{72,6... | collective-permute-start | bytes 1572872 | tf_op jit(solution)/shard_map/ppermute | solution.py:17
  44.3 12.9 %collective-permute-start.3 = (f32[512,1,256]{2,0,1:T(8,128)S(1)}, f32[512,1,256]{2,0,1:T(8,128)S(1)}, u32[]{:S(2)}, u32[]{:S(2)}) collective-permute-start(f32[512,1,256]{2,0,1:T(8,128)S(1)} %get-tuple-element.5), channel_id=1, source_target_pairs={{0,8},{8,16},{16,24},{24,32},{32,40},{40,48},{48,56},{56,64},{64,7... | collective-permute-start | bytes 1572872 | tf_op jit(solution)/shard_map/ppermute | solution.py:14
  73.6 11.7 %copy-start.4 = (f32[2048]{0:T(1024)S(1)}, f32[2048]{0:T(1024)}, u32[]{:S(2)}) copy-start(f32[2048]{0:T(1024)} %param.9) | copy-start | bytes 24580
  88.9 447.7 %reduce-scatter.2.cloned.1.call-start = ((), (), s32[]{:S(2)}) async-start(), calls=%async_computation.2 | async-start | bytes 8912896 | tf_op jit(solution)/shard_map/reduce_scatter | solution.py:70
Sparse Core Ops, SparseCore 0:
  89.1 328.2 all-gather.1
  433.5 103.1 reduce-scatter.1
where the time goes:
time: 547 us; the launch traced here: 545 us
  waiting for transfers between devices  447 us (82%)
  local copies, waits for them, and re-layouts  31.4 us (6%)
  other arithmetic  26.1 us (5%)
  matrix products  15.9 us (3%)
  between operations  14.2 us (3%)
  starting transfers between devices  10.8 us (2%)
    all_gather x1, waiting for transfers between devices, body(): gathered = lax.all_gather(footprint, 'rec', axis=0, tiled=True)  328 us
    reduce_scatter x1, waiting for transfers between devices, body(): lax.psum_scatter(contract(gathered, footprint), 'grid', scatter_dimension...  96.7 us
    add x2, other arithmetic, advance(): return fresh + pulses  20.4 us
    dot_general x1, matrix products, contract(): lax.dot_general(left, right, (((1,), (1,)), ((), ())), preferred_element_...  15.9 us
    ppermute x2, waiting for transfers between devices, padded_2(): lax.ppermute(lax.slice_in_dim(block, 0, width, axis=dim), axis, backward)  14.5 us
    unnamed x14, local copies, waits for them, and re-layouts  14.2 us
    gather x1, local copies, waits for them, and re-layouts, body(): picked = jnp.take(field.reshape(groups, rows * width), local_cells, axis=1)  11.7 us
  transfers between devices with their start and end apart: 6, of which 6 were waited for; matrix products, arithmetic and copies ran while one was open for 1% of the time, Pallas kernels for 0%

commit v1 on v0

v1 whole, which is shorter than its diff:
```python
import jax
import jax.numpy as jnp
from jax import lax
from jax.experimental import pallas as pl
from jax.experimental.pallas import tpu as pltpu
from jax.sharding import Mesh, PartitionSpec as P

GRID = ("z", "xh", "core")
PLANE = ("z", "xh", "xl")
BF = jnp.bfloat16
VMEM_LIMIT = 48 * 1024 * 1024


def swap(axis):
    return [(0, 1), (1, 0)]


def edge_kernel(x_ref, top_ref, bot_ref):
    top_ref[0] = x_ref[:, 0, :].astype(BF)
    top_ref[1] = x_ref[:, 1, :].astype(BF)
    bot_ref[0] = x_ref[:, 6, :].astype(BF)
    bot_ref[1] = x_ref[:, 7, :].astype(BF)


def edges(field):
    groups, rows, width = field.shape
    block = 64
    shape = jax.ShapeDtypeStruct((2, groups, width), BF)
    spec = pl.BlockSpec((2, block, width), lambda i: (0, i, 0))
    return pl.pallas_call(
        edge_kernel,
        grid=(groups // block,),
        in_specs=[pl.BlockSpec((block, rows, width), lambda i: (i, 0, 0))],
        out_specs=[spec, spec],
        out_shape=[shape, shape],
        compiler_params=pltpu.CompilerParams(vmem_limit_bytes=VMEM_LIMIT),
    )(field)


def stencil_kernel(info, x_ref, up_ref, down_ref, coef_ref, emis_ref, det_ref, adv_ref, keep_ref, send_ref):
    block = x_ref.shape[0]
    width = x_ref.shape[2]
    own_first = info[1] == 0
    first_cell = info[2]

    def group(g, carry):
        at = pl.ds(pl.multiple_of(g * 16, 16), 16)
        delta = det_ref[at, :] - first_cell - lax.broadcasted_iota(jnp.int32, (16, width), 1)

        def value(r):
            if r < 0:
                return up_ref[r + 2, at, :].astype(jnp.float32)
            if r > 7:
                return down_ref[r - 8, at, :].astype(jnp.float32)
            return x_ref[at, r, :]

        def step(r, south, center, north):
            east = pltpu.roll(center, width - 1, 1)
            west = pltpu.roll(center, 1, 1)
            c = [coef_ref[k, r + 1:r + 2, :] for k in range(5)]
            pulse = jnp.where(delta == r * width, 1.0, 0.0)
            return c[4] * center + c[0] * north + c[1] * south + c[2] * east + c[3] * west + pulse

        v = {r: value(r) for r in (-2, -1)}
        first = {}
        prints = {}
        for r in range(-1, 9):
            v[r + 1] = value(r + 1)
            first[r] = step(r, v[r - 1], v[r], v[r + 1])
            if r >= 1:
                q = r - 1
                out = step(q, first[q - 1], first[q], first[q + 1])
                adv_ref[at, q, :] = out
                prints[q] = (out * emis_ref[q:q + 1, :])
                if q >= 4:
                    p = q - 4
                    cols = pl.ds(p * width, width)
                    keep_ref[at, cols] = jnp.where(own_first, prints[p], prints[q]).astype(BF)
                    send_ref[at, cols] = jnp.where(own_first, prints[q], prints[p]).astype(BF)
        return carry

    lax.fori_loop(0, block // 16, group, 0)


def stencil(info, field, up, down, coef, emis, det):
    groups, rows, width = field.shape
    block = 64
    count = groups // block
    half = count // 2

    def turned(i, info):
        return lax.rem(i + info[0] * half, count)

    cells = rows * width // 2
    return pl.pallas_call(
        stencil_kernel,
        grid_spec=pltpu.PrefetchScalarGridSpec(
            num_scalar_prefetch=1,
            grid=(count,),
            in_specs=[
                pl.BlockSpec((block, rows, width), lambda i, info: (turned(i, info), 0, 0)),
                pl.BlockSpec((2, block, width), lambda i, info: (0, turned(i, info), 0)),
                pl.BlockSpec((2, block, width), lambda i, info: (0, turned(i, info), 0)),
                pl.BlockSpec((5, rows + 2, width), lambda i, info: (0, 0, 0)),
                pl.BlockSpec((rows, width), lambda i, info: (0, 0)),
                pl.BlockSpec((block, 1), lambda i, info: (turned(i, info), 0)),
            ],
            out_specs=[
                pl.BlockSpec((block, rows, width), lambda i, info: (turned(i, info), 0, 0)),
                pl.BlockSpec((block, cells), lambda i, info: (i, 0)),
                pl.BlockSpec((block, cells), lambda i, info: (i, 0)),
            ],
        ),
        out_shape=[
            jax.ShapeDtypeStruct(field.shape, jnp.float32),
            jax.ShapeDtypeStruct((groups, cells), BF),
            jax.ShapeDtypeStruct((groups, cells), BF),
        ],
        compiler_params=pltpu.CompilerParams(vmem_limit_bytes=VMEM_LIMIT),
    )(info, field, up, down, coef, emis, det)


def gram_kernel(info, a0, a1, a2, a3, o_ref, os_ref, q_ref, qs_ref, out_ref):
    i = pl.program_id(0)
    core, xl, y = info[0], info[1], info[3]
    half = o_ref.shape[1]
    rows = a0.shape[1]
    for d, a_ref in enumerate((a0, a1, a2, a3)):
        for j, (b_own, b_sib) in enumerate(((o_ref, os_ref), (q_ref, qs_ref))):
            slot = lax.rem(y + d, 4) * 4 + lax.rem(i + xl, 2) * 2 + lax.rem(j + xl, 2)
            for m in range(2):
                mine = pl.ds(m * rows, rows)
                sib = pl.ds((1 - m) * rows, rows)
                dims = (((1,), (1,)), ((), ()))
                total = lax.dot_general(
                    a_ref[0, :, :half], b_own[mine, :], dims, preferred_element_type=jnp.float32
                ) + lax.dot_general(
                    a_ref[0, :, half:], b_sib[sib, :], dims, preferred_element_type=jnp.float32
                )
                cols = pl.ds(pl.multiple_of(lax.rem(core + m, 2) * rows, rows), rows)
                out_ref[slot, :, cols] = total.astype(BF)


def partial_gram(info, lefts, rights):
    rows = lefts[0].shape[1]
    depth = lefts[0].shape[2]
    cols = rights[0].shape[0]
    left = pl.BlockSpec((1, rows, depth), lambda i, info: (i, 0, 0))
    right = pl.BlockSpec(rights[0].shape, lambda i, info: (0, 0))
    return pl.pallas_call(
        gram_kernel,
        grid_spec=pltpu.PrefetchScalarGridSpec(
            num_scalar_prefetch=1,
            grid=(2,),
            in_specs=[left] * 4 + [right] * 4,
            out_specs=pl.BlockSpec((16, rows, cols), lambda i, info: (0, 0, 0)),
        ),
        out_shape=jax.ShapeDtypeStruct((16, rows, cols), BF),
        compiler_params=pltpu.CompilerParams(vmem_limit_bytes=VMEM_LIMIT),
    )(info, *lefts, *rights)


def body(adjoint, courant, detector, sources, emission):
    groups, rows, width = adjoint.shape
    core = lax.axis_index("core")
    xl = lax.axis_index("xl")
    y = lax.axis_index("y")
    tile = lax.axis_index(GRID)
    first_cell = tile * rows * width
    info = jnp.stack([core, xl, first_cell, y]).astype(jnp.int32)

    count = lax.axis_size(GRID)
    forward = [(i, i + 1) for i in range(count - 1)]
    backward = [(i + 1, i) for i in range(count - 1)]
    top, bottom = edges(adjoint)
    up = lax.ppermute(bottom, GRID, forward)
    down = lax.ppermute(top, GRID, backward)
    coef_up = lax.ppermute(courant[:, rows - 1:], GRID, forward)
    coef_down = lax.ppermute(courant[:, :1], GRID, backward)
    coef = jnp.concatenate([coef_up, courant, coef_down], axis=1)
    columns = jnp.arange(width)
    coef = jnp.stack([
        coef[0],
        coef[1],
        jnp.where(columns == width - 1, 0.0, coef[2]),
        jnp.where(columns == 0, 0.0, coef[3]),
        1.0 - (coef[0] + coef[1] + coef[2] + coef[3]),
    ])

    local = sources - first_cell
    by_row = jnp.where(
        (local // width)[None, :] == jnp.arange(rows)[:, None], emission[None, :], 0.0
    )
    by_col = ((local % width)[:, None] == columns[None, :]).astype(jnp.float32)
    emis = jnp.dot(by_row, by_col, precision=lax.Precision.HIGHEST)

    field, keep, send = stencil(info, adjoint, up, down, coef, emis, detector[:, None])

    part = groups // 2
    other = lax.ppermute(send, "xl", swap("xl"))
    keep_s = lax.ppermute(keep, "core", swap("core"))
    other_s = lax.ppermute(other, "core", swap("core"))
    own = jnp.stack([
        jnp.concatenate([keep[:part], keep_s[part:]], axis=1),
        jnp.concatenate([other[:part], other_s[part:]], axis=1),
    ])
    lefts = [own] + [
        lax.ppermute(own, "y", [((i + d) % 4, i) for i in range(4)]) for d in (1, 2, 3)
    ]
    partial = partial_gram(info, lefts, (keep, keep_s, other, other_s))
    pieces = lax.all_to_all(partial, PLANE, 0, 0, tiled=True)
    total_sources = sources.shape[0] * count
    gram = jnp.sum(pieces.astype(jnp.float32), axis=0) / jnp.float32(total_sources)
    return field, gram


def solution(mesh):
    fine = Mesh(mesh.devices.reshape(4, 2, 2, 4, 2), ("z", "xh", "core", "y", "xl"))
    rec = ("y", "xl")
    in_specs = (P(rec, GRID, None), P(None, GRID, None), P(rec), P(GRID), P(GRID))
    out_specs = (P(rec, GRID, None), P(GRID, rec))
    return jax.shard_map(body, mesh=fine, in_specs=in_specs, out_specs=out_specs, check_vma=False)
```

time: 547 us -> 244 us (0.45)
  waiting for transfers between devices: 447 us -> 120 us
  blocking collectives: 0 us -> 56.2 us
  Pallas kernels: 0 us -> 29.5 us
  local copies, waits for them, and re-layouts: 31.4 us -> 4.71 us
  other arithmetic: 26.1 us -> 1.91 us
  matrix products: 15.9 us -> 0.79 us
  starting transfers between devices: 10.8 us -> 24.9 us
  between operations: 14.2 us -> 0.88 us
    all_gather x1 -> x0, waiting for transfers between devices: 328 us -> none  [body(): gathered = lax.all_gather(footprint, 'rec', axis=0, tiled=True)]
    ppermute x4 -> x10, waiting for transfers between devices: 22 us -> 120 us  [the longest x3 91.6 us: body(): lax.ppermute(own, 'y', [((i + d) % 4, i) for i in range(4)])]
    reduce_scatter x1 -> x0, waiting for transfers between devices: 96.7 us -> none  [body(): lax.psum_scatter(contract(gathered, footprint), 'grid', scatter_dimension...]
    all_to_all x0 -> x1, blocking collectives: none -> 56.2 us  [body(): pieces = lax.all_to_all(partial, PLANE, 0, 0, tiled=True)]
    pallas_call x0 -> x3, Pallas kernels: none -> 29.5 us  [the longest x1 13.8 us: partial_gram(): pl.pallas_call(gram_kernel, grid_spec=pltpu.PrefetchScalarGridSpec(num_sc...]
    add x3 -> x0, other arithmetic: 20.4 us -> none  [the longest x2 20.4 us: advance(): return fresh + pulses]
    dot_general x1, matrix products: 15.9 us -> 0.79 us  [body(): emis = jnp.dot(by_row, by_col, precision=lax.Precision.HIGHEST)]
    ppermute x4 -> x10, starting transfers between devices: 10.5 us -> 24.9 us  [the longest x1 6.05 us: body(): coef_down = lax.ppermute(courant[:, :1], GRID, backward)]
  transfers between devices with their start and end apart: 6 -> 10, of which waited for: 6 -> 7; matrix products, arithmetic and copies ran while one was open for 1% -> 1% of each run, Pallas kernels for 0% -> 1%
where the time goes in v1:
time: 244 us; the launch traced here: 239 us
  waiting for transfers between devices  120 us (49%)
  blocking collectives  56.2 us (23%)
  Pallas kernels  29.5 us (12%)
  starting transfers between devices  24.9 us (10%)
  local copies, waits for them, and re-layouts  4.71 us (2%)
    ppermute x3, waiting for transfers between devices, body(): lax.ppermute(own, 'y', [((i + d) % 4, i) for i in range(4)])  91.6 us
    all_to_all x1, blocking collectives, body(): pieces = lax.all_to_all(partial, PLANE, 0, 0, tiled=True)  56.2 us
    ppermute x1, waiting for transfers between devices, body(): other = lax.ppermute(send, 'xl', swap('xl'))  19.9 us
    pallas_call x1, Pallas kernels, partial_gram(): pl.pallas_call(gram_kernel, grid_spec=pltpu.PrefetchScalarGridSpec(num_sc...  13.8 us
    pallas_call x1, Pallas kernels, stencil(): pl.pallas_call(stencil_kernel, grid_spec=pltpu.PrefetchScalarGridSpec(num...  13.4 us
    ppermute x1, waiting for transfers between devices, body(): up = lax.ppermute(bottom, GRID, forward)  6.28 us
    ppermute x1, starting transfers between devices, body(): coef_down = lax.ppermute(courant[:, :1], GRID, backward)  6.05 us
    ppermute x1, starting transfers between devices, body(): down = lax.ppermute(top, GRID, backward)  6.05 us
  transfers between devices with their start and end apart: 10, of which 7 were waited for; matrix products, arithmetic and copies ran while one was open for 1% of the time, Pallas kernels for 1%

profile of v1, /device:TPU:56, one launch (start us, length us, event | category | flops | bytes accessed | tf_op | source)
XLA Modules:
  0.0 238.9 jit_solution(17724171964321686427)
XLA Ops:
  0.6 0.8 fusion.12
  1.5 1.9 collective-permute-start.2
  3.4 6.0 %collective-permute-start.3 = (f32[4,1,256]{2,1,0:T(1,128)S(1)}, f32[4,1,256]{2,1,0:T(1,128)S(1)}, u32[]{:S(2)}, u32[]{:S(2)}) collective-permute-start(f32[4,1,256]{2,1,0:T(1,128)S(1)} %get-tuple-element.16), channel_id=1, source_target_pairs={{8,0},{16,8},{24,16},{32,24},{40,32},{48,40},{56,48},{64,56},{72,6... | collective-permute-start | bytes 12296 | tf_op jit(solution)/shard_map/ppermute | solution.py:179
  9.5 2.2 copy-done
  11.6 2.3 shard_map.68
  13.9 1.9 collective-permute-start
  15.8 6.0 %collective-permute-start.1 = (bf16[2,512,256]{2,1,0:T(8,128)(2,1)S(1)}, bf16[2,512,256]{2,1,0:T(8,128)(2,1)S(1)}, u32[]{:S(2)}, u32[]{:S(2)}) collective-permute-start(bf16[2,512,256]{2,1,0:T(8,128)(2,1)S(1)} %get-tuple-element.8), channel_id=1, source_target_pairs={{8,0},{16,8},{24,16},{32,24},{40,32},{48,40},{56,48},{64,56},{72,6... | collective-permute-start | bytes 1572872 | tf_op jit(solution)/shard_map/ppermute | solution.py:177
  22.0 0.8 fusion.emis_ref
  23.1 6.3 %collective-permute-done.up_ref = bf16[2,512,256]{2,1,0:T(8,128)(2,1)S(1)} collective-permute-done((bf16[2,512,256]{2,1,0:T(8,128)(2,1)S(1)}, bf16[2,512,256]{2,1,0:T(8,128)(2,1)S(1)}, u32[]{:S(2)}, u32[]{:S(2)}) %collective-permute-start) | collective-permute-done | bytes 524320 | tf_op jit(solution)/shard_map/ppermute | solution.py:176
  29.7 13.4 %shard_map.69 = (f32[512,8,256]{2,1,0:T(8,128)}, bf16[512,1024]{1,0:T(8,128)(2,1)S(1)}, bf16[512,1024]{1,0:T(8,128)(2,1)S(1)}) custom-call(s32[4]{0:T(128)S(1)} %pad_add_fusion.info, f32[512,8,256]{2,1,0:T(8,128)} %x_ref.3, bf16[2,512,256]{2,1,0:T(8,128)(2,1)S(1)} %collective-permute-done.up_ref, bf16[2,512,256]{2,1,0:T(8,128)(2,1)S(1)} %collective-permute-done.1.down_ref, ...), custom_call_target="tpu_custom_call" | custom-call | tf_op jit(solution)/shard_map/pallas_call | solution.py:95
  43.1 2.1 collective-permute-start.5
  45.2 2.1 collective-permute-start.4
  47.3 19.9 %collective-permute-done.5.q_ref = bf16[512,1024]{1,0:T(8,128)(2,1)S(1)} collective-permute-done((bf16[512,1024]{1,0:T(8,128)(2,1)S(1)}, bf16[512,1024]{1,0:T(8,128)(2,1)S(1)}, u32[]{:S(2)}, u32[]{:S(2)}) %collective-permute-start.5) | collective-permute-done | bytes 1048608 | tf_op jit(solution)/shard_map/ppermute | solution.py:200
  67.2 1.8 collective-permute-start.6
  69.2 2.1 collective-permute-done.6.qs_ref
  71.9 2.6 %collective-permute-start.8 = (bf16[2,256,2048]{2,1,0:T(8,128)(2,1)S(1)}, bf16[2,256,2048]{2,1,0:T(8,128)(2,1)S(1)}, u32[]{:S(2)}, u32[]{:S(2)}) collective-permute-start(bf16[2,256,2048]{2,1,0:T(8,128)(2,1)S(1)} %pad_maximum_fusion.a0), channel_id=1, source_target_pairs={{4,0},{6,2},{0,4},{2,6},{5,1},{7,3},{1,5},{3,7},{12,8},{14,10},{8,... | collective-permute-start | bytes 6291464 | tf_op jit(solution)/shard_map/ppermute | solution.py:208
  74.5 45.6 %collective-permute-done.9.a3 = bf16[2,256,2048]{2,1,0:T(8,128)(2,1)S(1)} collective-permute-done((bf16[2,256,2048]{2,1,0:T(8,128)(2,1)S(1)}, bf16[2,256,2048]{2,1,0:T(8,128)(2,1)S(1)}, u32[]{:S(2)}, u32[]{:S(2)}) %collective-permute-start.9) | collective-permute-done | bytes 2097184 | tf_op jit(solution)/shard_map/ppermute | solution.py:208
  120.2 1.8 collective-permute-done.8.a2
  121.9 44.2 %collective-permute-done.7.a1 = bf16[2,256,2048]{2,1,0:T(8,128)(2,1)S(1)} collective-permute-done((bf16[2,256,2048]{2,1,0:T(8,128)(2,1)S(1)}, bf16[2,256,2048]{2,1,0:T(8,128)(2,1)S(1)}, u32[]{:S(2)}, u32[]{:S(2)}) %collective-permute-start.7) | collective-permute-done | bytes 2097184 | tf_op jit(solution)/shard_map/ppermute | solution.py:208
  166.2 1.4 copy-done.4
  167.5 13.8 %shard_map.70 = bf16[16,256,512]{2,1,0:T(8,128)(2,1)} custom-call(s32[4]{0:T(128)S(1)} %pad_add_fusion.info, bf16[2,256,2048]{2,1,0:T(8,128)(2,1)} %copy-done.1, bf16[2,256,2048]{2,1,0:T(8,128)(2,1)} %copy-done.4, bf16[2,256,2048]{2,1,0:T(8,128)(2,1)} %copy-done.3, bf16[2,256,2048]{2,1,0:T(8,128)(2,1)} %copy-done.2, ...), custom_call_target="tpu_custom_call" | custom-call | tf_op jit(solution)/shard_map/pallas_call | solution.py:150
  181.3 56.2 %all_to_all.5 = bf16[16,256,512]{2,1,0:T(8,128)(2,1)S(1)} all-to-all(bf16[16,256,512]{2,1,0:T(8,128)(2,1)} %shard_map.70), channel_id=1, replica_groups=mesh['z'=4,'xh'=2,'core'=2,'y'=4,'xl'=2] {'z','xh','xl'}, dimensions={0} | all-to-all | bytes 8388608 | tf_op jit(solution)/shard_map/all_to_all | solution.py:211
  237.5 0.6 convert_reduce_fusion
  238.1 0.8 broadcast_multiply_fusion
  (37 shorter events, 1.4 us)
Async XLA Ops:
  1.5 21.5 %collective-permute-start.2 = (f32[4,1,256]{2,1,0:T(1,128)S(1)}, f32[4,1,256]{2,1,0:T(1,128)S(1)}, u32[]{:S(2)}, u32[]{:S(2)}) collective-permute-start(f32[4,1,256]{2,1,0:T(1,128)S(1)} %get-tuple-element.15), channel_id=1, source_target_pairs={{0,8},{8,16},{16,24},{24,32},{32,40},{40,48},{48,56},{56,64},{64,7... | collective-permute-start | bytes 12296 | tf_op jit(solution)/shard_map/ppermute | solution.py:178
  3.4 19.6 %collective-permute-start.3 = (f32[4,1,256]{2,1,0:T(1,128)S(1)}, f32[4,1,256]{2,1,0:T(1,128)S(1)}, u32[]{:S(2)}, u32[]{:S(2)}) collective-permute-start(f32[4,1,256]{2,1,0:T(1,128)S(1)} %get-tuple-element.16), channel_id=1, source_target_pairs={{8,0},{16,8},{24,16},{32,24},{40,32},{48,40},{56,48},{64,56},{72,6... | collective-permute-start | bytes 12296 | tf_op jit(solution)/shard_map/ppermute | solution.py:179
  9.4 2.2 copy-start
  11.6 10.3 %copy-start.6 = (s32[2048]{0:T(1024)S(1)}, s32[2048]{0:T(1024)}, u32[]{:S(2)}) copy-start(s32[2048]{0:T(1024)} %param.8) | copy-start | bytes 24580
  11.6 10.3 %copy-start.8 = (f32[2048]{0:T(1024)S(1)}, f32[2048]{0:T(1024)}, u32[]{:S(2)}) copy-start(f32[2048]{0:T(1024)} %param.9) | copy-start | bytes 24580
  11.6 11.2 %copy-start.7 = (s32[512]{0:T(512)S(1)}, s32[512]{0:T(512)}, u32[]{:S(2)}) copy-start(s32[512]{0:T(512)} %param.7) | copy-start | bytes 6148
  11.6 11.4 %copy-start.5 = (f32[4,8,256]{2,1,0:T(8,128)S(1)}, f32[4,8,256]{2,1,0:T(8,128)}, u32[]{:S(2)}) copy-start(f32[4,8,256]{2,1,0:T(8,128)} %param.6) | copy-start | bytes 98308
  13.9 15.5 %collective-permute-start = (bf16[2,512,256]{2,1,0:T(8,128)(2,1)S(1)}, bf16[2,512,256]{2,1,0:T(8,128)(2,1)S(1)}, u32[]{:S(2)}, u32[]{:S(2)}) collective-permute-start(bf16[2,512,256]{2,1,0:T(8,128)(2,1)S(1)} %get-tuple-element.7), channel_id=1, source_target_pairs={{0,8},{8,16},{16,24},{24,32},{32,40},{40,48},{48,56},{56,64},{64,7... | collective-permute-start | bytes 1572872 | tf_op jit(solution)/shard_map/ppermute | solution.py:176
  15.8 13.8 %collective-permute-start.1 = (bf16[2,512,256]{2,1,0:T(8,128)(2,1)S(1)}, bf16[2,512,256]{2,1,0:T(8,128)(2,1)S(1)}, u32[]{:S(2)}, u32[]{:S(2)}) collective-permute-start(bf16[2,512,256]{2,1,0:T(8,128)(2,1)S(1)} %get-tuple-element.8), channel_id=1, source_target_pairs={{8,0},{16,8},{24,16},{32,24},{40,32},{48,40},{56,48},{64,56},{72,6... | collective-permute-start | bytes 1572872 | tf_op jit(solution)/shard_map/ppermute | solution.py:177
  43.1 24.1 %collective-permute-start.5 = (bf16[512,1024]{1,0:T(8,128)(2,1)S(1)}, bf16[512,1024]{1,0:T(8,128)(2,1)S(1)}, u32[]{:S(2)}, u32[]{:S(2)}) collective-permute-start(bf16[512,1024]{1,0:T(8,128)(2,1)S(1)} %get-tuple-element.11), channel_id=1, source_target_pairs={{0,1},{1,0},{2,3},{3,2},{4,5},{5,4},{6,7},{7,6},{8,9},{9,8},{10,11... | collective-permute-start | bytes 3145736 | tf_op jit(solution)/shard_map/ppermute | solution.py:200
  45.2 23.9 %collective-permute-start.4 = (bf16[512,1024]{1,0:T(8,128)(2,1)S(1)}, bf16[512,1024]{1,0:T(8,128)(2,1)S(1)}, u32[]{:S(2)}, u32[]{:S(2)}) collective-permute-start(bf16[512,1024]{1,0:T(8,128)(2,1)S(1)} %get-tuple-element.10.o_ref), channel_id=1, source_target_pairs={{0,8},{8,0},{1,9},{9,1},{2,10},{10,2},{3,11},{11,3},{4,12},{12,4},... | collective-permute-start | bytes 3145736 | tf_op jit(solution)/shard_map/ppermute | solution.py:201
  67.2 4.1 %collective-permute-start.6 = (bf16[512,1024]{1,0:T(8,128)(2,1)S(1)}, bf16[512,1024]{1,0:T(8,128)(2,1)S(1)}, u32[]{:S(2)}, u32[]{:S(2)}) collective-permute-start(bf16[512,1024]{1,0:T(8,128)(2,1)S(1)} %collective-permute-done.5.q_ref), channel_id=1, source_target_pairs={{0,8},{8,0},{1,9},{9,1},{2,10},{10,2},{3,11},{11,3},{4,12},{12,4},... | collective-permute-start | bytes 3145736 | tf_op jit(solution)/shard_map/ppermute | solution.py:202
  71.6 94.5 %copy-start.1 = (bf16[2,256,2048]{2,1,0:T(8,128)(2,1)}, bf16[2,256,2048]{2,1,0:T(8,128)(2,1)S(1)}, u32[]{:S(2)}) copy-start(bf16[2,256,2048]{2,1,0:T(8,128)(2,1)S(1)} %pad_maximum_fusion.a0) | copy-start | bytes 6291460
  71.6 48.5 %collective-permute-start.9 = (bf16[2,256,2048]{2,1,0:T(8,128)(2,1)S(1)}, bf16[2,256,2048]{2,1,0:T(8,128)(2,1)S(1)}, u32[]{:S(2)}, u32[]{:S(2)}) collective-permute-start(bf16[2,256,2048]{2,1,0:T(8,128)(2,1)S(1)} %pad_maximum_fusion.a0), channel_id=1, source_target_pairs={{6,0},{0,2},{2,4},{4,6},{7,1},{1,3},{3,5},{5,7},{14,8},{8,10},{10,... | collective-permute-start | bytes 6291464 | tf_op jit(solution)/shard_map/ppermute | solution.py:208
  71.9 50.0 %collective-permute-start.8 = (bf16[2,256,2048]{2,1,0:T(8,128)(2,1)S(1)}, bf16[2,256,2048]{2,1,0:T(8,128)(2,1)S(1)}, u32[]{:S(2)}, u32[]{:S(2)}) collective-permute-start(bf16[2,256,2048]{2,1,0:T(8,128)(2,1)S(1)} %pad_maximum_fusion.a0), channel_id=1, source_target_pairs={{4,0},{6,2},{0,4},{2,6},{5,1},{7,3},{1,5},{3,7},{12,8},{14,10},{8,... | collective-permute-start | bytes 6291464 | tf_op jit(solution)/shard_map/ppermute | solution.py:208
  74.5 91.6 %collective-permute-start.7 = (bf16[2,256,2048]{2,1,0:T(8,128)(2,1)S(1)}, bf16[2,256,2048]{2,1,0:T(8,128)(2,1)S(1)}, u32[]{:S(2)}, u32[]{:S(2)}) collective-permute-start(bf16[2,256,2048]{2,1,0:T(8,128)(2,1)S(1)} %pad_maximum_fusion.a0), channel_id=1, source_target_pairs={{2,0},{4,2},{6,4},{0,6},{3,1},{5,3},{7,5},{1,7},{10,8},{12,10},{14... | collective-permute-start | bytes 6291464 | tf_op jit(solution)/shard_map/ppermute | solution.py:208
  120.2 46.0 %copy-start.2 = (bf16[2,256,2048]{2,1,0:T(8,128)(2,1)}, bf16[2,256,2048]{2,1,0:T(8,128)(2,1)S(1)}, u32[]{:S(2)}) copy-start(bf16[2,256,2048]{2,1,0:T(8,128)(2,1)S(1)} %collective-permute-done.9.a3) | copy-start | bytes 6291460
  121.9 44.2 %copy-start.3 = (bf16[2,256,2048]{2,1,0:T(8,128)(2,1)}, bf16[2,256,2048]{2,1,0:T(8,128)(2,1)S(1)}, u32[]{:S(2)}) copy-start(bf16[2,256,2048]{2,1,0:T(8,128)(2,1)S(1)} %collective-permute-done.8.a2) | copy-start | bytes 6291460
  166.2 1.4 copy-start.4

commit v2 on v1

v2 whole, which is shorter than its diff:
```python
import jax
import jax.numpy as jnp
from jax import lax
from jax.experimental import pallas as pl
from jax.experimental.pallas import tpu as pltpu
from jax.sharding import Mesh, PartitionSpec as P

GRID = ("z", "xh", "core")
PLANE = ("z", "xh", "xl")
BF = jnp.bfloat16
VMEM_LIMIT = 40 * 1024 * 1024
LIFT = 1.0 / 256
SWAP = [(0, 1), (1, 0)]


def params():
    return pltpu.CompilerParams(vmem_limit_bytes=VMEM_LIMIT)


def cost(flops, moved):
    return pl.CostEstimate(flops=flops, bytes_accessed=moved, transcendentals=0)


def edge_kernel(x_ref, top_ref, bot_ref):
    top_ref[0] = x_ref[:, 0, :].astype(BF)
    top_ref[1] = x_ref[:, 1, :].astype(BF)
    bot_ref[0] = x_ref[:, 6, :].astype(BF)
    bot_ref[1] = x_ref[:, 7, :].astype(BF)


def edges(field):
    groups, rows, width = field.shape
    block = 64
    shape = jax.ShapeDtypeStruct((2, groups, width), BF)
    spec = pl.BlockSpec((2, block, width), lambda i: (0, i, 0))
    return pl.pallas_call(
        edge_kernel,
        grid=(groups // block,),
        in_specs=[pl.BlockSpec((block, rows, width), lambda i: (i, 0, 0))],
        out_specs=[spec, spec],
        out_shape=[shape, shape],
        cost_estimate=cost(1000, 6 << 20),
        compiler_params=params(),
    )(field)


def stepper(coef_ref, offset, delta, width):
    def step(r, south, center, north):
        east = pltpu.roll(center, width - 1, 1)
        west = pltpu.roll(center, 1, 1)
        at = r + offset
        c = [coef_ref[k, at:at + 1, :] for k in range(5)]
        pulse = jnp.where(delta == r * width, 1.0, 0.0)
        return c[4] * center + c[0] * north + c[1] * south + c[2] * east + c[3] * west + pulse

    return step


def offsets(det_ref, at, first_cell, width):
    return det_ref[at, :] - first_cell - lax.broadcasted_iota(jnp.int32, (16, width), 1)


def put(keep_ref, send_ref, at, p, own_first, low, high):
    width = low.shape[1]
    cols = pl.ds(p * width, width)
    keep_ref[at, cols] = jnp.where(own_first, low, high).astype(BF)
    send_ref[at, cols] = jnp.where(own_first, high, low).astype(BF)


def inner_kernel(info, x_ref, coef_ref, emis_ref, det_ref, adv_ref, keep_ref, send_ref):
    block, _, width = x_ref.shape
    own_first = info[1] == 0

    def group(g, carry):
        at = pl.ds(pl.multiple_of(g * 16, 16), 16)
        step = stepper(coef_ref, 0, offsets(det_ref, at, info[2], width), width)
        v = {r: x_ref[at, r, :] for r in (0, 1)}
        first = {}
        prints = {}
        for r in range(1, 7):
            v[r + 1] = x_ref[at, r + 1, :]
            first[r] = step(r, v[r - 1], v[r], v[r + 1])
            if r >= 3:
                q = r - 1
                out = step(q, first[q - 1], first[q], first[q + 1])
                adv_ref[at, q, :] = out
                prints[q] = out * emis_ref[q:q + 1, :]
                if q >= 4:
                    put(keep_ref, send_ref, at, q - 4, own_first, prints[q - 2], prints[q])
        return carry

    lax.fori_loop(0, block // 16, group, 0)


def outer_kernel(info, x_ref, up_ref, down_ref, coef_ref, emis_ref, det_ref, mid_ref, adv_ref, keep_ref, send_ref):
    block, _, width = x_ref.shape
    own_first = info[1] == 0

    def group(g, carry):
        at = pl.ds(pl.multiple_of(g * 16, 16), 16)
        step = stepper(coef_ref, 1, offsets(det_ref, at, info[2], width), width)

        def value(r):
            if r < 0:
                return up_ref[r + 2, at, :].astype(jnp.float32)
            if r > 7:
                return down_ref[r - 8, at, :].astype(jnp.float32)
            return x_ref[at, r, :]

        prints = {}
        for base in (-1, 5):
            v = {r: value(r) for r in (base - 1, base)}
            first = {}
            for r in range(base, base + 4):
                v[r + 1] = value(r + 1)
                first[r] = step(r, v[r - 1], v[r], v[r + 1])
                if r >= base + 2:
                    q = r - 1
                    out = step(q, first[q - 1], first[q], first[q + 1])
                    adv_ref[at, q, :] = out
                    prints[q] = out * emis_ref[q:q + 1, :]
        for r in range(2, 6):
            adv_ref[at, r, :] = mid_ref[at, r, :]
        for p in range(2):
            put(keep_ref, send_ref, at, p, own_first, prints[p], prints[p + 6])
        return carry

    lax.fori_loop(0, block // 16, group, 0)


def stencil(kernel, info, field, halos, coef, emis, det, mid, work):
    groups, rows, width = field.shape
    block = 64
    count = groups // block
    half = count // 2
    cells = 2 * width

    def turned(i, info):
        return lax.rem(i + info[0] * half, count)

    fields = pl.BlockSpec((block, rows, width), lambda i, info: (turned(i, info), 0, 0))
    halo = pl.BlockSpec((2, block, width), lambda i, info: (0, turned(i, info), 0))
    prints = pl.BlockSpec((block, cells), lambda i, info: (i, 0))
    print_shape = jax.ShapeDtypeStruct((groups, cells), BF)
    operands = [field, *halos, coef, emis, det, *mid]
    return pl.pallas_call(
        kernel,
        grid_spec=pltpu.PrefetchScalarGridSpec(
            num_scalar_prefetch=1,
            grid=(count,),
            in_specs=[
                fields,
                *([halo] * len(halos)),
                pl.BlockSpec(coef.shape, lambda i, info: (0, 0, 0)),
                pl.BlockSpec((rows, width), lambda i, info: (0, 0)),
                pl.BlockSpec((block, 1), lambda i, info: (turned(i, info), 0)),
                *([fields] * len(mid)),
            ],
            out_specs=[fields, prints, prints],
        ),
        out_shape=[jax.ShapeDtypeStruct(field.shape, jnp.float32), print_shape, print_shape],
        input_output_aliases={len(operands): 0} if mid else {},
        cost_estimate=cost(work, 8 << 20),
        compiler_params=params(),
    )(info, *operands)


NT = (((1,), (1,)), ((), ()))


def dot(left, right):
    return lax.dot_general(left, right, NT, preferred_element_type=jnp.float32)


def gram_kernel(grows, info, *refs):
    out_ref = refs[-1]
    acc_ref = refs[-2] if grows else None
    own, nxt, last, last_s, mine, theirs = (refs[2 * k:2 * k + 2] for k in range(6))
    core, xl = info[0], info[1]
    rows, depth = own[0].shape
    half = depth // 2
    at = [pl.multiple_of(lax.rem(core + m, 2) * rows, rows) for m in range(2)]
    e, i = pl.program_id(0), pl.program_id(1)

    def put_block(a_ref, pair):
        for j in range(2):
            slot = lax.rem(j + xl, 2)
            first, second = pair(j, a_ref)
            for m, value in enumerate((first, second)):
                where = (0, 0, slot, slice(None), pl.ds(at[m], rows))
                out_ref[where] = (value if acc_ref is None else value + acc_ref[where])

    def here(j, a):
        return dot(a[...], own[j][...]), (
            dot(a[:, :half], mine[j][rows:, :]) + dot(a[:, half:], theirs[j][:rows, :])
        )

    def far(j, a):
        return dot(a[...], last[j][...]), (
            dot(a[:, :half], last_s[j][:, half:]) + dot(a[:, half:], last_s[j][:, :half])
        )

    for step, (lefts, pair) in enumerate(((own, here), (nxt, here), (nxt, far), (last, here))):
        for owner in range(2):
            @pl.when((e == step) & (i == owner))
            def _():
                put_block(lefts[owner], pair)


def partial_gram(info, operands, acc):
    rows = operands[0].shape[0]
    cols = 2 * rows
    whole = pl.BlockSpec(memory_space=pltpu.VMEM)
    block = pl.BlockSpec(
        (1, 1, 2, rows, cols),
        lambda e, i, info: (lax.rem(info[3] + e, 4), lax.rem(i + info[1], 2), 0, 0, 0),
    )
    return pl.pallas_call(
        lambda *refs: gram_kernel(bool(acc), *refs),
        grid_spec=pltpu.PrefetchScalarGridSpec(
            num_scalar_prefetch=1,
            grid=(4, 2),
            in_specs=[whole] * len(operands) + [block] * len(acc),
            out_specs=block,
        ),
        out_shape=jax.ShapeDtypeStruct((4, 2, 2, rows, cols), jnp.float32),
        cost_estimate=cost(16 * 2 * rows * cols * operands[0].shape[1], 20 << 20),
        compiler_params=params(),
    )(info, *operands, *acc)


def spread(keep, send):
    part = keep.shape[0] // 2
    result = []
    for mine in (keep, lax.ppermute(send, "xl", SWAP)):
        theirs = lax.ppermute(mine, "core", SWAP)
        own = jnp.concatenate([mine[:part], theirs[part:]], axis=1)
        nxt = lax.ppermute(own, "y", [((i + 1) % 4, i) for i in range(4)])
        last = lax.ppermute(own, "y", [(i, (i + 1) % 4) for i in range(4)])
        last_s = lax.ppermute(last, "core", SWAP)
        result.append((own, nxt, last, last_s, mine, theirs))
    return [array for pair in zip(*result) for array in pair]


def body(adjoint, courant, detector, sources, emission):
    groups, rows, width = adjoint.shape
    core = lax.axis_index("core")
    xl = lax.axis_index("xl")
    y = lax.axis_index("y")
    z = lax.axis_index("z")
    tile = lax.axis_index(GRID)
    first_cell = tile * rows * width
    info = jnp.stack([core, xl, first_cell, y]).astype(jnp.int32)
    count = lax.axis_size(GRID)
    forward = [(i, i + 1) for i in range(count - 1)]
    backward = [(i + 1, i) for i in range(count - 1)]

    top, bottom = edges(adjoint)
    up = lax.ppermute(bottom, GRID, forward)
    down = lax.ppermute(top, GRID, backward)
    coef_up = lax.ppermute(courant[:, rows - 1:], GRID, forward)
    coef_down = lax.ppermute(courant[:, :1], GRID, backward)
    columns = jnp.arange(width)

    def weights(c):
        return jnp.stack([
            c[0],
            c[1],
            jnp.where(columns == width - 1, 0.0, c[2]),
            jnp.where(columns == 0, 0.0, c[3]),
            1.0 - (c[0] + c[1] + c[2] + c[3]),
        ])

    local = sources - first_cell
    by_row = jnp.where(
        (local // width)[None, :] == jnp.arange(rows)[:, None], emission[None, :], 0.0
    )
    by_col = ((local % width)[:, None] == columns[None, :]).astype(jnp.float32)
    emis = jnp.dot(by_row, by_col, precision=lax.Precision.HIGHEST)
    det = detector[:, None]

    mid, keep, send = stencil(
        inner_kernel, info, adjoint, [], weights(courant), emis, det, [], 8 << 20
    )
    parts = spread(keep, send)
    total = partial_gram(info, parts, [])

    extended = jnp.concatenate([coef_up, courant, coef_down], axis=1)
    field, keep, send = stencil(
        outer_kernel, info, adjoint, [up, down], weights(extended), emis, det, [mid], 8 << 20
    )
    parts = spread(keep, send)
    total = partial_gram(info, parts, [total])

    half = jnp.float16
    packed = (total * LIFT).astype(half).reshape(16, groups // 2, groups)
    pieces = lax.all_to_all(packed, PLANE, 0, 0, tiled=True)
    summed = jnp.sum(pieces.astype(jnp.float32), axis=0)
    moves = [((i + 2) % 4 * 4 + i, (i + 1) % 4 * 4 + (i + 3) % 4) for i in range(4)]
    moved = lax.ppermute((summed * (1.0 / 16)).astype(half), ("z", "y"), moves)
    moved = moved.astype(jnp.float32) * 16.0
    summed = jnp.where(lax.rem(y + 2, 4) == z, moved, summed)
    total_sources = sources.shape[0] * count
    return field, summed * jnp.float32(1.0 / (LIFT * total_sources))


def solution(mesh):
    fine = Mesh(mesh.devices.reshape(4, 2, 2, 4, 2), ("z", "xh", "core", "y", "xl"))
    rec = ("y", "xl")
    in_specs = (P(rec, GRID, None), P(None, GRID, None), P(rec), P(GRID), P(GRID))
    out_specs = (P(rec, GRID, None), P(GRID, rec))
    return jax.shard_map(body, mesh=fine, in_specs=in_specs, out_specs=out_specs, check_vma=False)
```

time: 244 us -> 196 us (0.80); the launches traced: 239 us -> 195 us
  waiting for transfers between devices: 120 us -> 55.9 us
  Pallas kernels: 29.5 us -> 43.1 us
  starting transfers between devices: 24.9 us -> 29.7 us
  other arithmetic: 1.91 us -> 6.57 us
  blocking collectives: 56.2 us -> 52.6 us
    ppermute x6 -> x19, waiting for transfers between devices: 114 us -> 55.9 us  [the longest x4 19.7 us: spread(): last = lax.ppermute(own, 'y', [(i, (i + 1) % 4) for i in range(4)])]
    pallas_call x2 -> x4, Pallas kernels: 27.2 us -> 40.9 us  [the longest x2 20.6 us: partial_gram(): pl.pallas_call(lambda *refs: gram_kernel(bool(acc), *refs), grid_spec=plt...]
    ppermute x1, waiting for transfers between devices: 6.28 us -> 0.01 us  [body(): up = lax.ppermute(bottom, GRID, forward)]
    ppermute x6 -> x19, starting transfers between devices: 8.94 us -> 13.8 us  [the longest x4 6.14 us: spread(): last = lax.ppermute(own, 'y', [(i, (i + 1) % 4) for i in range(4)])]
    convert_element_type x0 -> x2, other arithmetic: none -> 4.74 us  [the longest x1 4.69 us: body(): packed = (total * LIFT).astype(half).reshape(16, groups // 2, groups)]
    all_to_all x1, blocking collectives: 56.2 us -> 52.6 us  [body(): pieces = lax.all_to_all(packed, PLANE, 0, 0, tiled=True)]
  transfers between devices with their start and end apart: 10 -> 23, of which waited for: 7 -> 6; matrix products, arithmetic and copies ran while one was open for 1% -> 1% of each run, Pallas kernels for 1% -> 16%
where the time goes in v2:
time: 196 us; the launch traced here: 195 us
  waiting for transfers between devices  55.9 us (29%)
  blocking collectives  52.6 us (27%)
  Pallas kernels  43.1 us (22%)
  starting transfers between devices  29.7 us (15%)
  other arithmetic  6.57 us (3%)
  local copies, waits for them, and re-layouts  5.54 us (3%)
    all_to_all x1, blocking collectives, body(): pieces = lax.all_to_all(packed, PLANE, 0, 0, tiled=True)  52.6 us
    pallas_call x2, Pallas kernels, partial_gram(): pl.pallas_call(lambda *refs: gram_kernel(bool(acc), *refs), grid_spec=plt...  20.6 us
    pallas_call x2, Pallas kernels, stencil(): pl.pallas_call(kernel, grid_spec=pltpu.PrefetchScalarGridSpec(num_scalar_...  20.3 us
    ppermute x4, waiting for transfers between devices, spread(): last = lax.ppermute(own, 'y', [(i, (i + 1) % 4) for i in range(4)])  19.7 us
    ppermute x4, waiting for transfers between devices, spread(): nxt = lax.ppermute(own, 'y', [((i + 1) % 4, i) for i in range(4)])  15.4 us
    ppermute x2, waiting for transfers between devices, spread(): lax.ppermute(send, 'xl', SWAP)  12.8 us
    ppermute x1, waiting for transfers between devices, body(): moved = lax.ppermute((summed * (1.0 / 16)).astype(half), ('z', 'y'), moves)  8 us
    ppermute x4, starting transfers between devices, spread(): last = lax.ppermute(own, 'y', [(i, (i + 1) % 4) for i in range(4)])  6.14 us
  transfers between devices with their start and end apart: 23, of which 6 were waited for; matrix products, arithmetic and copies ran while one was open for 1% of the time, Pallas kernels for 16%

profile of v2, /device:TPU:56, one launch (start us, length us, event | category | flops | bytes accessed | tf_op | source)
XLA Modules:
  0.0 195.2 jit_solution(3528599212006351652)
XLA Ops:
  1.5 1.9 collective-permute-start.2
  3.4 6.0 %collective-permute-start.3 = (f32[4,1,256]{2,1,0:T(1,128)S(1)}, f32[4,1,256]{2,1,0:T(1,128)S(1)}, u32[]{:S(2)}, u32[]{:S(2)}) collective-permute-start(f32[4,1,256]{2,1,0:T(1,128)S(1)} %get-tuple-element.25), channel_id=1, source_target_pairs={{8,0},{16,8},{24,16},{32,24},{40,32},{48,40},{56,48},{64,56},{72,6... | collective-permute-start | bytes 12296 | tf_op jit(solution)/shard_map/ppermute | solution.py:262
  9.5 2.2 %copy-done = f32[512,8,256]{2,1,0:T(8,128)S(1)} copy-done((f32[512,8,256]{2,1,0:T(8,128)S(1)}, f32[512,8,256]{2,1,0:T(8,128)}, u32[]{:S(2)}) %copy-start) | copy-done | bytes 4194328
  11.7 2.2 %shard_map.68 = (bf16[2,512,256]{2,1,0:T(8,128)(2,1)S(1)}, bf16[2,512,256]{2,1,0:T(8,128)(2,1)S(1)}) custom-call(f32[512,8,256]{2,1,0:T(8,128)S(1)} %copy-done), custom_call_target="tpu_custom_call" | custom-call | flops 1000 | bytes 6291456 | tf_op jit(solution)/shard_map/pallas_call | solution.py:36
  13.9 1.9 collective-permute-start
  15.8 6.0 %collective-permute-start.1 = (bf16[2,512,256]{2,1,0:T(8,128)(2,1)S(1)}, bf16[2,512,256]{2,1,0:T(8,128)(2,1)S(1)}, u32[]{:S(2)}, u32[]{:S(2)}) collective-permute-start(bf16[2,512,256]{2,1,0:T(8,128)(2,1)S(1)} %get-tuple-element.11), channel_id=1, source_target_pairs={{8,0},{16,8},{24,16},{32,24},{40,32},{48,40},{56,48},{64,56},{72,6... | collective-permute-start | bytes 1572872 | tf_op jit(solution)/shard_map/ppermute | solution.py:260
  23.1 2.2 %copy-done.1 = f32[512,8,256]{2,1,0:T(8,128)S(1)} copy-done((f32[512,8,256]{2,1,0:T(8,128)S(1)}, f32[512,8,256]{2,1,0:T(8,128)}, u32[]{:S(2)}) %copy-start.1) | copy-done | bytes 4194328
  25.2 8.9 %shard_map.69 = (f32[512,8,256]{2,1,0:T(8,128)}, bf16[512,512]{1,0:T(8,128)(2,1)S(1)}, bf16[512,512]{1,0:T(8,128)(2,1)S(1)}) custom-call(s32[4]{0:T(128)S(1)} %pad_add_fusion.info.refs_0_, f32[512,8,256]{2,1,0:T(8,128)S(1)} %copy-done.1, f32[5,8,256]{2,1,0:T(8,128)S(1)} %pad_maximum_fusion.6.coef_ref, f32[8,256]{1,0:T(8,128)S(1)} %fusion.emis_ref, ...), custom_call_target="tpu_custom_call" | custom-call | flops 8388608 | bytes 8388608 | tf_op jit(solution)/shard_map/pallas_call | solution.py:146
  34.1 1.5 collective-permute-start.14
  35.7 11.4 %shard_map.70 = (f32[512,8,256]{2,1,0:T(8,128)}, bf16[512,512]{1,0:T(8,128)(2,1)S(1)}, bf16[512,512]{1,0:T(8,128)(2,1)S(1)}) custom-call(s32[4]{0:T(128)S(1)} %pad_add_fusion.info.refs_0_, f32[512,8,256]{2,1,0:T(8,128)S(1)} %copy-done.1, bf16[2,512,256]{2,1,0:T(8,128)(2,1)S(1)} %collective-permute-done.up_ref, ...), custom_call_target="tpu_custom_call", output_to_operand_aliasing={{0}: (7, {})} | custom-call | flops 8388608 | bytes 8388608 | tf_op jit(solution)/shard_map/pallas_call | solution.py:146
  48.6 12.8 %collective-permute-done.5.refs_10_ = bf16[512,512]{1,0:T(8,128)(2,1)S(1)} collective-permute-done((bf16[512,512]{1,0:T(8,128)(2,1)S(1)}, bf16[512,512]{1,0:T(8,128)(2,1)S(1)}, u32[]{:S(2)}, u32[]{:S(2)}) %collective-permute-start.5) | collective-permute-done | bytes 524320 | tf_op jit(solution)/shard_map/ppermute | solution.py:235
  62.3 2.6 %collective-permute-start.19 = (bf16[256,1024]{1,0:T(8,128)(2,1)S(1)}, bf16[256,1024]{1,0:T(8,128)(2,1)S(1)}, u32[]{:S(2)}, u32[]{:S(2)}) collective-permute-start(bf16[256,1024]{1,0:T(8,128)(2,1)S(1)} %pad_maximum_fusion.3.refs_2_), channel_id=1, source_target_pairs={{0,2},{2,4},{4,6},{6,0},{1,3},{3,5},{5,7},{7,1},{8,10},{10,12},{12... | collective-permute-start | bytes 1572872 | tf_op jit(solution)/shard_map/ppermute | solution.py:239
  65.1 3.3 %collective-permute-start.9 = (bf16[256,1024]{1,0:T(8,128)(2,1)S(1)}, bf16[256,1024]{1,0:T(8,128)(2,1)S(1)}, u32[]{:S(2)}, u32[]{:S(2)}) collective-permute-start(bf16[256,1024]{1,0:T(8,128)(2,1)S(1)} %pad_maximum_fusion.refs_1_), channel_id=1, source_target_pairs={{0,2},{2,4},{4,6},{6,0},{1,3},{3,5},{5,7},{7,1},{8,10},{10,12},{12... | collective-permute-start | bytes 1572872 | tf_op jit(solution)/shard_map/ppermute | solution.py:239
  68.5 8.9 %collective-permute-done.16.refs_3_ = bf16[256,1024]{1,0:T(8,128)(2,1)S(1)} collective-permute-done((bf16[256,1024]{1,0:T(8,128)(2,1)S(1)}, bf16[256,1024]{1,0:T(8,128)(2,1)S(1)}, u32[]{:S(2)}, u32[]{:S(2)}) %collective-permute-start.16) | collective-permute-done | bytes 524320 | tf_op jit(solution)/shard_map/ppermute | solution.py:238
  77.4 11.0 %collective-permute-done.9.refs_5_ = bf16[256,1024]{1,0:T(8,128)(2,1)S(1)} collective-permute-done((bf16[256,1024]{1,0:T(8,128)(2,1)S(1)}, bf16[256,1024]{1,0:T(8,128)(2,1)S(1)}, u32[]{:S(2)}, u32[]{:S(2)}) %collective-permute-start.9) | collective-permute-done | bytes 524320 | tf_op jit(solution)/shard_map/ppermute | solution.py:239
  88.8 1.4 collective-permute-start.8
  90.2 8.7 %collective-permute-done.10.refs_6_ = bf16[256,1024]{1,0:T(8,128)(2,1)S(1)} collective-permute-done((bf16[256,1024]{1,0:T(8,128)(2,1)S(1)}, bf16[256,1024]{1,0:T(8,128)(2,1)S(1)}, u32[]{:S(2)}, u32[]{:S(2)}) %collective-permute-start.10) | collective-permute-done | bytes 524320 | tf_op jit(solution)/shard_map/ppermute | solution.py:239
  98.9 8.6 %shard_map.71.refs_13_ = f32[4,2,2,256,512]{4,3,2,1,0:T(8,128)} custom-call(s32[4]{0:T(128)S(1)} %pad_add_fusion.info.refs_0_, bf16[256,1024]{1,0:T(8,128)(2,1)S(1)} %pad_maximum_fusion.2.refs_1_, bf16[256,1024]{1,0:T(8,128)(2,1)S(1)} %pad_maximum_fusion.3.refs_2_, bf16[256,1024]{1,0:T(8,128)(2,1)S(1)} %collective-permute-done.16.refs_3_, ...), custom_call_target="tpu_custom_call" | custom-call | flops 4294967296 | bytes 20971520 | tf_op jit(solution)/shard_map/pallas_call | solution.py:218
  107.5 6.5 %collective-permute-done.8.refs_4_ = bf16[256,1024]{1,0:T(8,128)(2,1)S(1)} collective-permute-done((bf16[256,1024]{1,0:T(8,128)(2,1)S(1)}, bf16[256,1024]{1,0:T(8,128)(2,1)S(1)}, u32[]{:S(2)}, u32[]{:S(2)}) %collective-permute-start.8) | collective-permute-done | bytes 524320 | tf_op jit(solution)/shard_map/ppermute | solution.py:238
  114.1 12.0 %shard_map.72 = f32[4,2,2,256,512]{4,3,2,1,0:T(8,128)} custom-call(s32[4]{0:T(128)S(1)} %pad_add_fusion.info.refs_0_, bf16[256,1024]{1,0:T(8,128)(2,1)S(1)} %pad_maximum_fusion.refs_1_, bf16[256,1024]{1,0:T(8,128)(2,1)S(1)} %pad_maximum_fusion.1.refs_2_, bf16[256,1024]{1,0:T(8,128)(2,1)S(1)} %collective-permute-done.7.refs_3_, ...), custom_call_target="tpu_custom_call" | custom-call | flops 4294967296 | bytes 20971520 | tf_op jit(solution)/shard_map/pallas_call | solution.py:218
  126.1 4.7 %multiply_convert_fusion = f16[4,2,2,256,512]{4,3,2,1,0:T(8,128)(2,1)S(1)} fusion(f32[4,2,2,256,512]{4,3,2,1,0:T(8,128)} %shard_map.72), kind=kLoop, calls=%fused_computation.1 | loop fusion | flops 4194304 | bytes 12582912 | tf_op jit(solution)/shard_map/convert_element_type | solution.py:296
  130.8 52.6 %all_to_all.5 = f16[16,256,512]{2,1,0:T(8,128)(2,1)S(1)} all-to-all(f16[16,256,512]{2,1,0:T(8,128)(2,1)S(1)} %bitcast.6), channel_id=1, replica_groups=mesh['z'=4,'xh'=2,'core'=2,'y'=4,'xl'=2] {'z','xh','xl'}, dimensions={0} | all-to-all | bytes 8388608 | tf_op jit(solution)/shard_map/all_to_all | solution.py:297
  183.9 2.4 %collective-permute-start.22 = (f16[256,512]{1,0:T(8,128)(2,1)S(1)}, f16[256,512]{1,0:T(8,128)(2,1)S(1)}, u32[]{:S(2)}, u32[]{:S(2)}) collective-permute-start(f16[256,512]{1,0:T(8,128)(2,1)S(1)} %multiply_convert_fusion.1), channel_id=1, source_target_pairs={{64,38},{98,64},{4,98},{38,4},{65,39},{99,65},{5,99},{39,5},{72,46... | collective-permute-start | bytes 786440 | tf_op jit(solution)/shard_map/ppermute | solution.py:300
  186.3 8.0 %collective-permute-done.22 = f16[256,512]{1,0:T(8,128)(2,1)S(1)} collective-permute-done((f16[256,512]{1,0:T(8,128)(2,1)S(1)}, f16[256,512]{1,0:T(8,128)(2,1)S(1)}, u32[]{:S(2)}, u32[]{:S(2)}) %collective-permute-start.22) | collective-permute-done | bytes 262176 | tf_op jit(solution)/shard_map/ppermute | solution.py:300
  (70 shorter events, 6.6 us)
Async XLA Ops:
  0.6 22.2 %copy-start.4 = (s32[512]{0:T(512)S(1)}, s32[512]{0:T(512)}, u32[]{:S(2)}) copy-start(s32[512]{0:T(512)} %param.7) | copy-start | bytes 6148
  1.5 34.1 %collective-permute-start.2 = (f32[4,1,256]{2,1,0:T(1,128)S(1)}, f32[4,1,256]{2,1,0:T(1,128)S(1)}, u32[]{:S(2)}, u32[]{:S(2)}) collective-permute-start(f32[4,1,256]{2,1,0:T(1,128)S(1)} %get-tuple-element.24), channel_id=1, source_target_pairs={{0,8},{8,16},{16,24},{24,32},{32,40},{40,48},{48,56},{56,64},{64,7... | collective-permute-start | bytes 12296 | tf_op jit(solution)/shard_map/ppermute | solution.py:261
  3.4 32.2 %collective-permute-start.3 = (f32[4,1,256]{2,1,0:T(1,128)S(1)}, f32[4,1,256]{2,1,0:T(1,128)S(1)}, u32[]{:S(2)}, u32[]{:S(2)}) collective-permute-start(f32[4,1,256]{2,1,0:T(1,128)S(1)} %get-tuple-element.25), channel_id=1, source_target_pairs={{8,0},{16,8},{24,16},{32,24},{40,32},{48,40},{56,48},{64,56},{72,6... | collective-permute-start | bytes 12296 | tf_op jit(solution)/shard_map/ppermute | solution.py:262
  13.9 21.8 %collective-permute-start = (bf16[2,512,256]{2,1,0:T(8,128)(2,1)S(1)}, bf16[2,512,256]{2,1,0:T(8,128)(2,1)S(1)}, u32[]{:S(2)}, u32[]{:S(2)}) collective-permute-start(bf16[2,512,256]{2,1,0:T(8,128)(2,1)S(1)} %get-tuple-element.10), channel_id=1, source_target_pairs={{0,8},{8,16},{16,24},{24,32},{32,40},{40,48},{48,56},{56,64},{64,7... | collective-permute-start | bytes 1572872 | tf_op jit(solution)/shard_map/ppermute | solution.py:259
  15.8 19.9 %collective-permute-start.1 = (bf16[2,512,256]{2,1,0:T(8,128)(2,1)S(1)}, bf16[2,512,256]{2,1,0:T(8,128)(2,1)S(1)}, u32[]{:S(2)}, u32[]{:S(2)}) collective-permute-start(bf16[2,512,256]{2,1,0:T(8,128)(2,1)S(1)} %get-tuple-element.11), channel_id=1, source_target_pairs={{8,0},{16,8},{24,16},{32,24},{40,32},{48,40},{56,48},{64,56},{72,6... | collective-permute-start | bytes 1572872 | tf_op jit(solution)/shard_map/ppermute | solution.py:260
  34.1 13.5 %collective-permute-start.14 = (bf16[512,512]{1,0:T(8,128)(2,1)S(1)}, bf16[512,512]{1,0:T(8,128)(2,1)S(1)}, u32[]{:S(2)}, u32[]{:S(2)}) collective-permute-start(bf16[512,512]{1,0:T(8,128)(2,1)S(1)} %get-tuple-element.17), channel_id=1, source_target_pairs={{0,1},{1,0},{2,3},{3,2},{4,5},{5,4},{6,7},{7,6},{8,9},{9,8},{10,11... | collective-permute-start | bytes 1572872 | tf_op jit(solution)/shard_map/ppermute | solution.py:235
  35.6 12.6 %collective-permute-start.13 = (bf16[512,512]{1,0:T(8,128)(2,1)S(1)}, bf16[512,512]{1,0:T(8,128)(2,1)S(1)}, u32[]{:S(2)}, u32[]{:S(2)}) collective-permute-start(bf16[512,512]{1,0:T(8,128)(2,1)S(1)} %get-tuple-element.16.refs_9_), channel_id=1, source_target_pairs={{0,8},{8,0},{1,9},{9,1},{2,10},{10,2},{3,11},{11,3},{4,12},{12,4},... | collective-permute-start | bytes 1572872 | tf_op jit(solution)/shard_map/ppermute | solution.py:236
  47.1 14.3 %collective-permute-start.5 = (bf16[512,512]{1,0:T(8,128)(2,1)S(1)}, bf16[512,512]{1,0:T(8,128)(2,1)S(1)}, u32[]{:S(2)}, u32[]{:S(2)}) collective-permute-start(bf16[512,512]{1,0:T(8,128)(2,1)S(1)} %get-tuple-element.15), channel_id=1, source_target_pairs={{0,1},{1,0},{2,3},{3,2},{4,5},{5,4},{6,7},{7,6},{8,9},{9,8},{10,11... | collective-permute-start | bytes 1572872 | tf_op jit(solution)/shard_map/ppermute | solution.py:235
  47.6 14.6 %collective-permute-start.15 = (bf16[512,512]{1,0:T(8,128)(2,1)S(1)}, bf16[512,512]{1,0:T(8,128)(2,1)S(1)}, u32[]{:S(2)}, u32[]{:S(2)}) collective-permute-start(bf16[512,512]{1,0:T(8,128)(2,1)S(1)} %collective-permute-done.14.refs_10_), channel_id=1, source_target_pairs={{0,8},{8,0},{1,9},{9,1},{2,10},{10,2},{3,11},{11,3},{4,12},{12,4},... | collective-permute-start | bytes 1572872 | tf_op jit(solution)/shard_map/ppermute | solution.py:236
  47.9 17.0 %collective-permute-start.4 = (bf16[512,512]{1,0:T(8,128)(2,1)S(1)}, bf16[512,512]{1,0:T(8,128)(2,1)S(1)}, u32[]{:S(2)}, u32[]{:S(2)}) collective-permute-start(bf16[512,512]{1,0:T(8,128)(2,1)S(1)} %get-tuple-element.14.refs_9_), channel_id=1, source_target_pairs={{0,8},{8,0},{1,9},{9,1},{2,10},{10,2},{3,11},{11,3},{4,12},{12,4},... | collective-permute-start | bytes 1572872 | tf_op jit(solution)/shard_map/ppermute | solution.py:236
  48.3 16.8 %collective-permute-start.18 = (bf16[256,1024]{1,0:T(8,128)(2,1)S(1)}, bf16[256,1024]{1,0:T(8,128)(2,1)S(1)}, u32[]{:S(2)}, u32[]{:S(2)}) collective-permute-start(bf16[256,1024]{1,0:T(8,128)(2,1)S(1)} %pad_maximum_fusion.2.refs_1_), channel_id=1, source_target_pairs={{0,2},{2,4},{4,6},{6,0},{1,3},{3,5},{5,7},{7,1},{8,10},{10,12},{12... | collective-permute-start | bytes 1572872 | tf_op jit(solution)/shard_map/ppermute | solution.py:239
  61.4 7.0 %collective-permute-start.6 = (bf16[512,512]{1,0:T(8,128)(2,1)S(1)}, bf16[512,512]{1,0:T(8,128)(2,1)S(1)}, u32[]{:S(2)}, u32[]{:S(2)}) collective-permute-start(bf16[512,512]{1,0:T(8,128)(2,1)S(1)} %collective-permute-done.5.refs_10_), channel_id=1, source_target_pairs={{0,8},{8,0},{1,9},{9,1},{2,10},{10,2},{3,11},{11,3},{4,12},{12,4},... | collective-permute-start | bytes 1572872 | tf_op jit(solution)/shard_map/ppermute | solution.py:236
  61.4 15.9 %collective-permute-start.16 = (bf16[256,1024]{1,0:T(8,128)(2,1)S(1)}, bf16[256,1024]{1,0:T(8,128)(2,1)S(1)}, u32[]{:S(2)}, u32[]{:S(2)}) collective-permute-start(bf16[256,1024]{1,0:T(8,128)(2,1)S(1)} %pad_maximum_fusion.2.refs_1_), channel_id=1, source_target_pairs={{2,0},{4,2},{6,4},{0,6},{3,1},{5,3},{7,5},{1,7},{10,8},{12,10},{14... | collective-permute-start | bytes 1572872 | tf_op jit(solution)/shard_map/ppermute | solution.py:238
  62.3 15.1 %collective-permute-start.19 = (bf16[256,1024]{1,0:T(8,128)(2,1)S(1)}, bf16[256,1024]{1,0:T(8,128)(2,1)S(1)}, u32[]{:S(2)}, u32[]{:S(2)}) collective-permute-start(bf16[256,1024]{1,0:T(8,128)(2,1)S(1)} %pad_maximum_fusion.3.refs_2_), channel_id=1, source_target_pairs={{0,2},{2,4},{4,6},{6,0},{1,3},{3,5},{5,7},{7,1},{8,10},{10,12},{12... | collective-permute-start | bytes 1572872 | tf_op jit(solution)/shard_map/ppermute | solution.py:239
  64.9 23.9 %collective-permute-start.17 = (bf16[256,1024]{1,0:T(8,128)(2,1)S(1)}, bf16[256,1024]{1,0:T(8,128)(2,1)S(1)}, u32[]{:S(2)}, u32[]{:S(2)}) collective-permute-start(bf16[256,1024]{1,0:T(8,128)(2,1)S(1)} %pad_maximum_fusion.3.refs_2_), channel_id=1, source_target_pairs={{2,0},{4,2},{6,4},{0,6},{3,1},{5,3},{7,5},{1,7},{10,8},{12,10},{14... | collective-permute-start | bytes 1572872 | tf_op jit(solution)/shard_map/ppermute | solution.py:238
  65.1 23.3 %collective-permute-start.9 = (bf16[256,1024]{1,0:T(8,128)(2,1)S(1)}, bf16[256,1024]{1,0:T(8,128)(2,1)S(1)}, u32[]{:S(2)}, u32[]{:S(2)}) collective-permute-start(bf16[256,1024]{1,0:T(8,128)(2,1)S(1)} %pad_maximum_fusion.refs_1_), channel_id=1, source_target_pairs={{0,2},{2,4},{4,6},{6,0},{1,3},{3,5},{5,7},{7,1},{8,10},{10,12},{12... | collective-permute-start | bytes 1572872 | tf_op jit(solution)/shard_map/ppermute | solution.py:239
  68.4 21.8 %collective-permute-start.20 = (bf16[256,1024]{1,0:T(8,128)(2,1)S(1)}, bf16[256,1024]{1,0:T(8,128)(2,1)S(1)}, u32[]{:S(2)}, u32[]{:S(2)}) collective-permute-start(bf16[256,1024]{1,0:T(8,128)(2,1)S(1)} %collective-permute-done.18.refs_5_), channel_id=1, source_target_pairs={{0,8},{8,0},{1,9},{9,1},{2,10},{10,2},{3,11},{11,3},{4,12},{12,4},... | collective-permute-start | bytes 1572872 | tf_op jit(solution)/shard_map/ppermute | solution.py:240
  77.4 21.5 %collective-permute-start.10 = (bf16[256,1024]{1,0:T(8,128)(2,1)S(1)}, bf16[256,1024]{1,0:T(8,128)(2,1)S(1)}, u32[]{:S(2)}, u32[]{:S(2)}) collective-permute-start(bf16[256,1024]{1,0:T(8,128)(2,1)S(1)} %pad_maximum_fusion.1.refs_2_), channel_id=1, source_target_pairs={{0,2},{2,4},{4,6},{6,0},{1,3},{3,5},{5,7},{7,1},{8,10},{10,12},{12... | collective-permute-start | bytes 1572872 | tf_op jit(solution)/shard_map/ppermute | solution.py:239
  77.4 21.5 %collective-permute-start.21 = (bf16[256,1024]{1,0:T(8,128)(2,1)S(1)}, bf16[256,1024]{1,0:T(8,128)(2,1)S(1)}, u32[]{:S(2)}, u32[]{:S(2)}) collective-permute-start(bf16[256,1024]{1,0:T(8,128)(2,1)S(1)} %collective-permute-done.19.refs_6_), channel_id=1, source_target_pairs={{0,8},{8,0},{1,9},{9,1},{2,10},{10,2},{3,11},{11,3},{4,12},{12,4},... | collective-permute-start | bytes 1572872 | tf_op jit(solution)/shard_map/ppermute | solution.py:240
  88.4 19.2 %collective-permute-start.7 = (bf16[256,1024]{1,0:T(8,128)(2,1)S(1)}, bf16[256,1024]{1,0:T(8,128)(2,1)S(1)}, u32[]{:S(2)}, u32[]{:S(2)}) collective-permute-start(bf16[256,1024]{1,0:T(8,128)(2,1)S(1)} %pad_maximum_fusion.refs_1_), channel_id=1, source_target_pairs={{2,0},{4,2},{6,4},{0,6},{3,1},{5,3},{7,5},{1,7},{10,8},{12,10},{14... | collective-permute-start | bytes 1572872 | tf_op jit(solution)/shard_map/ppermute | solution.py:238
  88.8 25.3 %collective-permute-start.8 = (bf16[256,1024]{1,0:T(8,128)(2,1)S(1)}, bf16[256,1024]{1,0:T(8,128)(2,1)S(1)}, u32[]{:S(2)}, u32[]{:S(2)}) collective-permute-start(bf16[256,1024]{1,0:T(8,128)(2,1)S(1)} %pad_maximum_fusion.1.refs_2_), channel_id=1, source_target_pairs={{2,0},{4,2},{6,4},{0,6},{3,1},{5,3},{7,5},{1,7},{10,8},{12,10},{14... | collective-permute-start | bytes 1572872 | tf_op jit(solution)/shard_map/ppermute | solution.py:238
  90.2 23.9 %collective-permute-start.11 = (bf16[256,1024]{1,0:T(8,128)(2,1)S(1)}, bf16[256,1024]{1,0:T(8,128)(2,1)S(1)}, u32[]{:S(2)}, u32[]{:S(2)}) collective-permute-start(bf16[256,1024]{1,0:T(8,128)(2,1)S(1)} %collective-permute-done.9.refs_5_), channel_id=1, source_target_pairs={{0,8},{8,0},{1,9},{9,1},{2,10},{10,2},{3,11},{11,3},{4,12},{12,4},... | collective-permute-start | bytes 1572872 | tf_op jit(solution)/shard_map/ppermute | solution.py:240
  98.9 15.2 %collective-permute-start.12 = (bf16[256,1024]{1,0:T(8,128)(2,1)S(1)}, bf16[256,1024]{1,0:T(8,128)(2,1)S(1)}, u32[]{:S(2)}, u32[]{:S(2)}) collective-permute-start(bf16[256,1024]{1,0:T(8,128)(2,1)S(1)} %collective-permute-done.10.refs_6_), channel_id=1, source_target_pairs={{0,8},{8,0},{1,9},{9,1},{2,10},{10,2},{3,11},{11,3},{4,12},{12,4},... | collective-permute-start | bytes 1572872 | tf_op jit(solution)/shard_map/ppermute | solution.py:240
  183.9 10.4 %collective-permute-start.22 = (f16[256,512]{1,0:T(8,128)(2,1)S(1)}, f16[256,512]{1,0:T(8,128)(2,1)S(1)}, u32[]{:S(2)}, u32[]{:S(2)}) collective-permute-start(f16[256,512]{1,0:T(8,128)(2,1)S(1)} %multiply_convert_fusion.1), channel_id=1, source_target_pairs={{64,38},{98,64},{4,98},{38,4},{65,39},{99,65},{5,99},{39,5},{72,46... | collective-permute-start | bytes 786440 | tf_op jit(solution)/shard_map/ppermute | solution.py:300
  (6 other events, 57.4 us)

commit v3 on v2

--- a/solution.py
+++ b/solution.py
@@ -6,11 +6,14 @@
 from jax.sharding import Mesh, PartitionSpec as P
 
 GRID = ("z", "xh", "core")
-PLANE = ("z", "xh", "xl")
+XS = ("xh", "xl")
+HALF = jnp.float16
 BF = jnp.bfloat16
-VMEM_LIMIT = 40 * 1024 * 1024
+VMEM_LIMIT = 16 * 1024 * 1024
 LIFT = 1.0 / 256
 SWAP = [(0, 1), (1, 0)]
+INNER = 100 << 20
+OUTER = 20 << 20
 
 
 def params():
@@ -89,7 +92,7 @@
                     put(keep_ref, send_ref, at, q - 4, own_first, prints[q - 2], prints[q])
         return carry
 
-    lax.fori_loop(0, block // 16, group, 0)
+    lax.fori_loop(0, block // 16, group, 0, unroll=2)
 
 
 def outer_kernel(info, x_ref, up_ref, down_ref, coef_ref, emis_ref, det_ref, mid_ref, adv_ref, keep_ref, send_ref):
@@ -125,7 +128,7 @@
             put(keep_ref, send_ref, at, p, own_first, prints[p], prints[p + 6])
         return carry
 
-    lax.fori_loop(0, block // 16, group, 0)
+    lax.fori_loop(0, block // 16, group, 0, unroll=2)
 
 
 def stencil(kernel, info, field, halos, coef, emis, det, mid, work):
@@ -160,7 +163,7 @@
         ),
         out_shape=[jax.ShapeDtypeStruct(field.shape, jnp.float32), print_shape, print_shape],
         input_output_aliases={len(operands): 0} if mid else {},
-        cost_estimate=cost(work, 8 << 20),
+        cost_estimate=cost(1000, work),
         compiler_params=params(),
     )(info, *operands)
 
@@ -173,73 +176,92 @@
 
 
 def gram_kernel(grows, info, *refs):
-    out_ref = refs[-1]
-    acc_ref = refs[-2] if grows else None
-    own, nxt, last, last_s, mine, theirs = (refs[2 * k:2 * k + 2] for k in range(6))
-    core, xl = info[0], info[1]
-    rows, depth = own[0].shape
-    half = depth // 2
-    at = [pl.multiple_of(lax.rem(core + m, 2) * rows, rows) for m in range(2)]
-    e, i = pl.program_id(0), pl.program_id(1)
-
-    def put_block(a_ref, pair):
-        for j in range(2):
-            slot = lax.rem(j + xl, 2)
-            first, second = pair(j, a_ref)
-            for m, value in enumerate((first, second)):
-                where = (0, 0, slot, slice(None), pl.ds(at[m], rows))
-                out_ref[where] = (value if acc_ref is None else value + acc_ref[where])
-
-    def here(j, a):
-        return dot(a[...], own[j][...]), (
-            dot(a[:, :half], mine[j][rows:, :]) + dot(a[:, half:], theirs[j][:rows, :])
-        )
-
-    def far(j, a):
-        return dot(a[...], last[j][...]), (
-            dot(a[:, :half], last_s[j][:, half:]) + dot(a[:, half:], last_s[j][:, :half])
-        )
-
-    for step, (lefts, pair) in enumerate(((own, here), (nxt, here), (nxt, far), (last, here))):
-        for owner in range(2):
-            @pl.when((e == step) & (i == owner))
-            def _():
-                put_block(lefts[owner], pair)
+    stack, outs = refs[-1], refs[-3:-1]
+    accs = refs[12:14] if grows else None
+    own, own_s, nxt, nxt_s, last, last_s = (refs[2 * k:2 * k + 2] for k in range(6))
+    core, xl, y, xpos = info[0], info[1], info[3], info[4]
+    rows = nxt_s[0].shape[0]
+    half = own[0].shape[1]
+    part = rows // 2
+    lefts = []
+    for e, tile, sibling, first in ((1, nxt, nxt_s, 0), (0, own, own_s, rows), (3, last, last_s, rows)):
+        for i in range(2):
+            at = pl.ds(len(lefts) * rows, rows)
+            stack[at, :half] = tile[i][:rows, :]
+            stack[at, half:] = sibling[i][first:first + rows, :]
+            lefts.append((e, i))
+
+    for j in range(2):
+        for m in range(2):
+            mine = slice(m * rows, (m + 1) * rows)
+            theirs = slice((1 - m) * rows, (2 - m) * rows)
+            here = dot(stack[:, :half], own[j][mine, :]) + dot(stack[:, half:], own_s[j][theirs, :])
+            far = dot(stack[:2 * rows, :half], last[j][mine, :]) + dot(
+                stack[:2 * rows, half:], last_s[j][theirs, :]
+            )
+            cols = pl.ds(pl.multiple_of(lax.rem(core + m, 2) * rows, rows), rows)
+            values = [(e, i, here[k * rows:(k + 1) * rows]) for k, (e, i) in enumerate(lefts)]
+            values += [(2, i, far[i * rows:(i + 1) * rows]) for i in range(2)]
+            for e, i, value in values:
+                at_z = lax.rem(y + e, 4)
+                at_x = lax.rem(lax.rem(i + xl, 2) * 2 + lax.rem(j + xl, 2) + 4 - xpos, 4)
+                for upper, slot in enumerate((at_z * 4 + at_x, at_x * 4 + at_z)):
+                    piece = value[upper * part:(upper + 1) * part]
+                    if accs is not None:
+                        piece = piece + accs[upper][slot, :, cols]
+                    outs[upper][slot, :, cols] = piece
 
 
 def partial_gram(info, operands, acc):
-    rows = operands[0].shape[0]
-    cols = 2 * rows
+    rows, half = operands[0].shape
+    rows = rows // 2
     whole = pl.BlockSpec(memory_space=pltpu.VMEM)
-    block = pl.BlockSpec(
-        (1, 1, 2, rows, cols),
-        lambda e, i, info: (lax.rem(info[3] + e, 4), lax.rem(i + info[1], 2), 0, 0, 0),
-    )
+    shape = jax.ShapeDtypeStruct((16, rows // 2, 2 * rows), jnp.float32)
     return pl.pallas_call(
         lambda *refs: gram_kernel(bool(acc), *refs),
-        grid_spec=pltpu.PrefetchScalarGridSpec(
-            num_scalar_prefetch=1,
-            grid=(4, 2),
-            in_specs=[whole] * len(operands) + [block] * len(acc),
-            out_specs=block,
-        ),
-        out_shape=jax.ShapeDtypeStruct((4, 2, 2, rows, cols), jnp.float32),
-        cost_estimate=cost(16 * 2 * rows * cols * operands[0].shape[1], 20 << 20),
+        in_specs=[pl.BlockSpec(memory_space=pltpu.SMEM)] + [whole] * (len(operands) + len(acc)),
+        out_specs=[whole, whole],
+        out_shape=[shape, shape],
+        scratch_shapes=[pltpu.VMEM((6 * rows, 2 * half), BF)],
+        cost_estimate=cost(1000, 8 << 20),
         compiler_params=params(),
     )(info, *operands, *acc)
 
 
-def spread(keep, send):
-    part = keep.shape[0] // 2
-    result = []
-    for mine in (keep, lax.ppermute(send, "xl", SWAP)):
-        theirs = lax.ppermute(mine, "core", SWAP)
-        own = jnp.concatenate([mine[:part], theirs[part:]], axis=1)
-        nxt = lax.ppermute(own, "y", [((i + 1) % 4, i) for i in range(4)])
-        last = lax.ppermute(own, "y", [(i, (i + 1) % 4) for i in range(4)])
-        last_s = lax.ppermute(last, "core", SWAP)
-        result.append((own, nxt, last, last_s, mine, theirs))
-    return [array for pair in zip(*result) for array in pair]
+def to_four(pieces, axis):
+    total = pieces[0].astype(jnp.float32)
+    for d in (1, 2, 3):
+        came = lax.ppermute(pieces[d], axis, [(i, (i + d) % 4) for i in range(4)])
+        total = total + came.astype(jnp.float32)
+    return total * 0.25
+
+
+def after(value, *others):
+    return lax.optimization_barrier((value, others))[0]
+
+
+def along_y(own):
+    nxt = lax.ppermute(own, "y", [((i + 1) % 4, i) for i in range(4)])
+    last = lax.ppermute(own, "y", [(i, (i + 1) % 4) for i in range(4)])
+    return nxt, last
+
+
+def siblings(own, nxt, last):
+    part = own.shape[0] // 2
+    own_s = lax.ppermute(own, "core", SWAP)
+    nxt_s = lax.ppermute(nxt[part:], "core", SWAP)
+    last_s = lax.ppermute(last, "core", SWAP)
+    return own, own_s, nxt, nxt_s, last, last_s
+
+
+def gram_operands(keep, keep_y, other, other_y):
+    return [
+        array for pair in zip(siblings(keep, *keep_y), siblings(other, *other_y)) for array in pair
+    ]
+
+
+def mean_of_four(pieces):
+    return jnp.sum(pieces.astype(jnp.float32), axis=0) * 0.25
 
 
 def body(adjoint, courant, detector, sources, emission):
@@ -250,7 +272,8 @@
     z = lax.axis_index("z")
     tile = lax.axis_index(GRID)
     first_cell = tile * rows * width
-    info = jnp.stack([core, xl, first_cell, y]).astype(jnp.int32)
+    xpos = lax.axis_index(XS)
+    info = jnp.stack([core, xl, first_cell, y, xpos]).astype(jnp.int32)
     count = lax.axis_size(GRID)
     forward = [(i, i + 1) for i in range(count - 1)]
     backward = [(i + 1, i) for i in range(count - 1)]
@@ -258,8 +281,9 @@
     top, bottom = edges(adjoint)
     up = lax.ppermute(bottom, GRID, forward)
     down = lax.ppermute(top, GRID, backward)
-    coef_up = lax.ppermute(courant[:, rows - 1:], GRID, forward)
-    coef_down = lax.ppermute(courant[:, :1], GRID, backward)
+    near = after(courant, top)
+    coef_up = lax.ppermute(near[:, rows - 1:], GRID, forward)
+    coef_down = lax.ppermute(near[:, :1], GRID, backward)
     columns = jnp.arange(width)
 
     def weights(c):
@@ -279,29 +303,39 @@
     emis = jnp.dot(by_row, by_col, precision=lax.Precision.HIGHEST)
     det = detector[:, None]
 
+    weights_in = weights(courant)
     mid, keep, send = stencil(
-        inner_kernel, info, adjoint, [], weights(courant), emis, det, [], 8 << 20
+        inner_kernel, after(info, top, bottom), adjoint, [], weights_in, emis, det, [], INNER
     )
-    parts = spread(keep, send)
-    total = partial_gram(info, parts, [])
+    other = lax.ppermute(send, "xl", SWAP)
+    keep_y = along_y(after(keep, up, down))
+    other_y = along_y(after(other, keep_y))
+    totals = partial_gram(info, gram_operands(keep, keep_y, other, other_y), [])
 
     extended = jnp.concatenate([coef_up, courant, coef_down], axis=1)
     field, keep, send = stencil(
-        outer_kernel, info, adjoint, [up, down], weights(extended), emis, det, [mid], 8 << 20
+        outer_kernel, after(info, keep_y), adjoint, [up, down], weights(extended), emis, det,
+        [mid], OUTER
     )
-    parts = spread(keep, send)
-    total = partial_gram(info, parts, [total])
-
-    half = jnp.float16
-    packed = (total * LIFT).astype(half).reshape(16, groups // 2, groups)
-    pieces = lax.all_to_all(packed, PLANE, 0, 0, tiled=True)
-    summed = jnp.sum(pieces.astype(jnp.float32), axis=0)
+    other = lax.ppermute(send, "xl", SWAP)
+    keep_y = along_y(keep)
+    other_y = along_y(after(other, keep_y, totals))
+    totals = partial_gram(info, gram_operands(keep, keep_y, other, other_y), totals)
+
+    along_z, along_x = [
+        (total * LIFT).astype(HALF).reshape(4, 4, groups // 4, groups) for total in totals
+    ]
+    along_z = lax.all_to_all(along_z, "z", 0, 0, tiled=True)
+    along_x = after(to_four(along_x, XS).astype(HALF), along_z)
+    along_z = mean_of_four(along_z).astype(HALF)
+    along_x = mean_of_four(lax.all_to_all(along_x, "z", 0, 0, tiled=True))
+    along_z = to_four(along_z, XS)
+    summed = jnp.concatenate([along_z, along_x], axis=0)
     moves = [((i + 2) % 4 * 4 + i, (i + 1) % 4 * 4 + (i + 3) % 4) for i in range(4)]
-    moved = lax.ppermute((summed * (1.0 / 16)).astype(half), ("z", "y"), moves)
-    moved = moved.astype(jnp.float32) * 16.0
+    moved = lax.ppermute(summed.astype(HALF), ("z", "y"), moves).astype(jnp.float32)
     summed = jnp.where(lax.rem(y + 2, 4) == z, moved, summed)
     total_sources = sources.shape[0] * count
-    return field, summed * jnp.float32(1.0 / (LIFT * total_sources))
+    return field, summed * jnp.float32(16.0 / (LIFT * total_sources))
 
 
 def solution(mesh):

time: 196 us -> 171 us (0.87)
  blocking collectives: 52.6 us -> 0 us
  waiting for transfers between devices: 55.9 us -> 75.9 us
  starting transfers between devices: 29.7 us -> 47 us
  Pallas kernels: 43.1 us -> 31.2 us
    all_to_all x1 -> x0, blocking collectives: 52.6 us -> none  [body(): pieces = lax.all_to_all(packed, PLANE, 0, 0, tiled=True)]
    ppermute x21 -> x31, waiting for transfers between devices: 55.9 us -> 75.9 us  [the longest x6 26.7 us: to_four(): came = lax.ppermute(pieces[d], axis, [(i, (i + d) % 4) for i in range(4)])]
    pallas_call x2, Pallas kernels: 20.6 us -> 10.7 us  [partial_gram(): pl.pallas_call(lambda *refs: gram_kernel(bool(acc), *refs), in_specs=[pl....]
    all_to_all x0 -> x2, starting transfers between devices: none -> 9.77 us  [the longest x1 4.96 us: body(): along_z = lax.all_to_all(along_z, 'z', 0, 0, tiled=True)]
    ppermute x21 -> x31, starting transfers between devices: 21.7 us -> 29.3 us  [the longest x6 9.54 us: to_four(): came = lax.ppermute(pieces[d], axis, [(i, (i + d) % 4) for i in range(4)])]
    pallas_call x2, Pallas kernels: 20.3 us -> 18.2 us  [stencil(): pl.pallas_call(kernel, grid_spec=pltpu.PrefetchScalarGridSpec(num_scalar_...]
    unnamed x12 -> x14, local copies, waits for them, and re-layouts: 4.39 us -> 6.35 us
    convert_element_type x2 -> x5, other arithmetic: 4.74 us -> 6.1 us  [the longest x2 4.8 us: body(): (total * LIFT).astype(HALF).reshape(4, 4, groups // 4, groups)]
  transfers between devices with their start and end apart: 23 -> 35, of which waited for: 6 -> 19; matrix products, arithmetic and copies ran while one was open for 1% -> 3% of each run, Pallas kernels for 16% -> 14%
where the time goes in v3:
time: 171 us
  waiting for transfers between devices  75.9 us (44%)
  starting transfers between devices  47 us (27%)
  Pallas kernels  31.2 us (18%)
  other arithmetic  7.56 us (4%)
  local copies, waits for them, and re-layouts  7.1 us (4%)
    ppermute x6, waiting for transfers between devices, to_four(): came = lax.ppermute(pieces[d], axis, [(i, (i + d) % 4) for i in range(4)])  26.7 us
    pallas_call x2, Pallas kernels, stencil(): pl.pallas_call(kernel, grid_spec=pltpu.PrefetchScalarGridSpec(num_scalar_...  18.2 us
    ppermute x2, waiting for transfers between devices, body(): other = lax.ppermute(send, 'xl', SWAP)  13.7 us
    ppermute x4, waiting for transfers between devices, along_y(): last = lax.ppermute(own, 'y', [(i, (i + 1) % 4) for i in range(4)])  12.4 us
    pallas_call x2, Pallas kernels, partial_gram(): pl.pallas_call(lambda *refs: gram_kernel(bool(acc), *refs), in_specs=[pl....  10.7 us
    ppermute x6, starting transfers between devices, to_four(): came = lax.ppermute(pieces[d], axis, [(i, (i + d) % 4) for i in range(4)])  9.54 us
    ppermute x1, waiting for transfers between devices, body(): lax.ppermute(summed.astype(HALF), ('z', 'y'), moves).astype(jnp.float32)  8.44 us
    unnamed x14, local copies, waits for them, and re-layouts  6.35 us
  transfers between devices with their start and end apart: 35, of which 19 were waited for; matrix products, arithmetic and copies ran while one was open for 3% of the time, Pallas kernels for 14%

profile of v3, /device:TPU:56, one launch (start us, length us, event | category | flops | bytes accessed | tf_op | source)
XLA Modules:
  0.0 170.5 jit_solution(2474506018944258203)
XLA Ops:
  0.6 2.2 %copy-done = f32[512,8,256]{2,1,0:T(8,128)S(1)} copy-done((f32[512,8,256]{2,1,0:T(8,128)S(1)}, f32[512,8,256]{2,1,0:T(8,128)}, u32[]{:S(2)}) %copy-start) | copy-done | bytes 4194328
  2.8 2.3 %shard_map.68 = (bf16[2,512,256]{2,1,0:T(8,128)(2,1)S(1)}, bf16[2,512,256]{2,1,0:T(8,128)(2,1)S(1)}) custom-call(f32[512,8,256]{2,1,0:T(8,128)S(1)} %copy-done), custom_call_target="tpu_custom_call" | custom-call | flops 1000 | bytes 6291456 | tf_op jit(solution)/shard_map/pallas_call | solution.py:39
  7.0 6.0 %collective-permute-start.1 = (bf16[2,512,256]{2,1,0:T(8,128)(2,1)S(1)}, bf16[2,512,256]{2,1,0:T(8,128)(2,1)S(1)}, u32[]{:S(2)}, u32[]{:S(2)}) collective-permute-start(bf16[2,512,256]{2,1,0:T(8,128)(2,1)S(1)} %get-tuple-element.21), channel_id=1, source_target_pairs={{8,0},{16,8},{24,16},{32,24},{40,32},{48,40},{56,48},{64,56},{72,6... | collective-permute-start | bytes 1572872 | tf_op jit(solution)/shard_map/ppermute | solution.py:283
  14.3 2.2 %copy-done.1 = f32[512,8,256]{2,1,0:T(8,128)S(1)} copy-done((f32[512,8,256]{2,1,0:T(8,128)S(1)}, f32[512,8,256]{2,1,0:T(8,128)}, u32[]{:S(2)}) %copy-start.1) | copy-done | bytes 4194328
  16.5 7.3 %shard_map.69 = (f32[512,8,256]{2,1,0:T(8,128)}, bf16[512,512]{1,0:T(8,128)(2,1)S(1)}, bf16[512,512]{1,0:T(8,128)(2,1)S(1)}) custom-call(s32[5]{0:T(128)S(1)} %stack.35.info.refs_0_, f32[512,8,256]{2,1,0:T(8,128)S(1)} %copy-done.1, f32[5,8,256]{2,1,0:T(8,128)S(1)} %pad_maximum_fusion.3.coef_ref, f32[8,256]{1,0:T(8,128)S(1)} %fusion.emis_ref, ...), custom_call_target="tpu_custom_call" | custom-call | flops 1000 | bytes 104857600 | tf_op jit(solution)/shard_map/pallas_call | solution.py:149
  27.3 9.3 %collective-permute-done.11.refs_2_ = bf16[512,512]{1,0:T(8,128)(2,1)S(1)} collective-permute-done((bf16[512,512]{1,0:T(8,128)(2,1)S(1)}, bf16[512,512]{1,0:T(8,128)(2,1)S(1)}, u32[]{:S(2)}, u32[]{:S(2)}) %collective-permute-start.11) | collective-permute-done | bytes 524320 | tf_op jit(solution)/shard_map/ppermute | solution.py:310
  42.9 5.4 %collective-permute-done.4 = f32[4,1,256]{2,1,0:T(1,128)S(1)} collective-permute-done((f32[4,1,256]{2,1,0:T(1,128)S(1)}, f32[4,1,256]{2,1,0:T(1,128)S(1)}, u32[]{:S(2)}, u32[]{:S(2)}) %collective-permute-start.4) | collective-permute-done | bytes 4128 | tf_op jit(solution)/shard_map/ppermute | solution.py:285
  51.6 2.3 %collective-permute-start.15 = (bf16[256,512]{1,0:T(8,128)(2,1)S(1)}, bf16[256,512]{1,0:T(8,128)(2,1)S(1)}, u32[]{:S(2)}, u32[]{:S(2)}) collective-permute-start(bf16[256,512]{1,0:T(8,128)(2,1)S(1)} %slice.113), channel_id=1, source_target_pairs={{0,8},{8,0},{1,9},{9,1},{2,10},{10,2},{3,11},{11,3},{4,12},{12,4},... | collective-permute-start | bytes 786440 | tf_op jit(solution)/shard_map/ppermute | solution.py:252
  54.0 10.9 %shard_map.70 = (f32[512,8,256]{2,1,0:T(8,128)}, bf16[512,512]{1,0:T(8,128)(2,1)S(1)}, bf16[512,512]{1,0:T(8,128)(2,1)S(1)}) custom-call(s32[5]{0:T(128)S(1)} %stack.35.info.refs_0_, f32[512,8,256]{2,1,0:T(8,128)S(1)} %copy-done.1, bf16[2,512,256]{2,1,0:T(8,128)(2,1)S(1)} %collective-permute-done.up_ref, ...), custom_call_target="tpu_custom_call", output_to_operand_aliasing={{0}: (7, {})} | custom-call | flops 1000 | bytes 20971520 | tf_op jit(solution)/shard_map/pallas_call | solution.py:149
  69.4 5.3 %shard_map.71 = (f32[16,128,512]{2,1,0:T(8,128)S(1)}, f32[16,128,512]{2,1,0:T(8,128)S(1)}) custom-call(s32[5]{0:T(128)S(1)} %stack.35.info.refs_0_, bf16[512,512]{1,0:T(8,128)(2,1)S(1)} %get-tuple-element.25.refs_1_, bf16[512,512]{1,0:T(8,128)(2,1)S(1)} %collective-permute-done.11.refs_2_, bf16[512,512]{1,0:T(8,128)(2,1)S(1)} %collective-permute-done.12.refs_3_, ...), custom_call_target="tpu_custom_call" | custom-call | flops 1000 | bytes 8388608 | tf_op jit(solution)/shard_map/pallas_call | solution.py:220
  74.7 4.4 %collective-permute-done.6.refs_2_ = bf16[512,512]{1,0:T(8,128)(2,1)S(1)} collective-permute-done((bf16[512,512]{1,0:T(8,128)(2,1)S(1)}, bf16[512,512]{1,0:T(8,128)(2,1)S(1)}, u32[]{:S(2)}, u32[]{:S(2)}) %collective-permute-start.6) | collective-permute-done | bytes 524320 | tf_op jit(solution)/shard_map/ppermute | solution.py:320
  79.9 2.4 %collective-permute-done.9.refs_5_ = bf16[512,512]{1,0:T(8,128)(2,1)S(1)} collective-permute-done((bf16[512,512]{1,0:T(8,128)(2,1)S(1)}, bf16[512,512]{1,0:T(8,128)(2,1)S(1)}, u32[]{:S(2)}, u32[]{:S(2)}) %collective-permute-start.9) | collective-permute-done | bytes 524320 | tf_op jit(solution)/shard_map/ppermute | solution.py:244
  84.8 10.5 %collective-permute-done.23.refs_10_ = bf16[512,512]{1,0:T(8,128)(2,1)S(1)} collective-permute-done((bf16[512,512]{1,0:T(8,128)(2,1)S(1)}, bf16[512,512]{1,0:T(8,128)(2,1)S(1)}, u32[]{:S(2)}, u32[]{:S(2)}) %collective-permute-start.23) | collective-permute-done | bytes 524320 | tf_op jit(solution)/shard_map/ppermute | solution.py:245
  98.8 5.4 %shard_map.72 = (f32[16,128,512]{2,1,0:T(8,128)S(1)}, f32[16,128,512]{2,1,0:T(8,128)S(1)}) custom-call(s32[5]{0:T(128)S(1)} %stack.35.info.refs_0_, bf16[512,512]{1,0:T(8,128)(2,1)S(1)} %get-tuple-element.30.refs_1_, bf16[512,512]{1,0:T(8,128)(2,1)S(1)} %collective-permute-done.6.refs_2_, bf16[512,512]{1,0:T(8,128)(2,1)S(1)} %collective-permute-done.7.refs_3_, ...), custom_call_target="tpu_custom_call" | custom-call | flops 1000 | bytes 8388608 | tf_op jit(solution)/shard_map/pallas_call | solution.py:220
  106.2 2.0 %multiply_convert_fusion.1 = f16[16,128,512]{2,1,0:T(8,128)(2,1)} fusion(f32[16,128,512]{2,1,0:T(8,128)S(1)} %get-tuple-element.37), kind=kLoop, calls=%fused_computation.2 | loop fusion | flops 2097152 | bytes 6291456 | tf_op jit(solution)/shard_map/convert_element_type | solution.py:326
  108.2 5.0 %all-to-all-start = ((f16[4,4,128,512]{3,2,1,0:T(8,128)(2,1)}), f16[4,4,128,512]{3,2,1,0:T(8,128)(2,1)S(1)}, u32[]{:S(2)}, u32[]{:S(2)}) async-start(f16[4,4,128,512]{3,2,1,0:T(8,128)(2,1)} %bitcast.6), calls=%async_computation | async-start | bytes 4194304 | tf_op jit(solution)/shard_map/all_to_all | solution.py:328
  113.1 2.8 %multiply_convert_fusion = f16[16,128,512]{2,1,0:T(8,128)(2,1)S(1)} fusion(f32[16,128,512]{2,1,0:T(8,128)} %copy-done.2), kind=kLoop, calls=%fused_computation | loop fusion | flops 2097152 | bytes 6291456 | tf_op jit(solution)/shard_map/convert_element_type | solution.py:326
  119.6 2.2 %collective-permute-start.30 = (f16[4,128,512]{2,1,0:T(8,128)(2,1)S(1)}, f16[4,128,512]{2,1,0:T(8,128)(2,1)S(1)}, u32[]{:S(2)}, u32[]{:S(2)}) collective-permute-start(f16[4,128,512]{2,1,0:T(8,128)(2,1)S(1)} %get-tuple-element.42), channel_id=1, source_target_pairs={{0,16},{1,17},{16,0},{17,1},{2,18},{3,19},{18,2},{19,3},{4,20},{5,... | collective-permute-start | bytes 1572872 | tf_op jit(solution)/shard_map/ppermute | solution.py:234
  121.8 9.9 %collective-permute-done.29 = f16[4,128,512]{2,1,0:T(8,128)(2,1)S(1)} collective-permute-done((f16[4,128,512]{2,1,0:T(8,128)(2,1)S(1)}, f16[4,128,512]{2,1,0:T(8,128)(2,1)S(1)}, u32[]{:S(2)}, u32[]{:S(2)}) %collective-permute-start.29) | collective-permute-done | bytes 524320 | tf_op jit(solution)/shard_map/ppermute | solution.py:234
  132.7 10.1 %collective-permute-done.30 = f16[4,128,512]{2,1,0:T(8,128)(2,1)S(1)} collective-permute-done((f16[4,128,512]{2,1,0:T(8,128)(2,1)S(1)}, f16[4,128,512]{2,1,0:T(8,128)(2,1)S(1)}, u32[]{:S(2)}, u32[]{:S(2)}) %collective-permute-start.30) | collective-permute-done | bytes 524320 | tf_op jit(solution)/shard_map/ppermute | solution.py:234
  144.4 4.8 %all-to-all-start.1 = ((f16[4,128,512]{2,1,0:T(8,128)(2,1)}), f16[4,128,512]{2,1,0:T(8,128)(2,1)S(1)}, u32[]{:S(2)}, u32[]{:S(2)}) async-start(f16[4,128,512]{2,1,0:T(8,128)(2,1)} %multiply_convert_fusion.2), calls=%async_computation.1 | async-start | bytes 1048576 | tf_op jit(solution)/shard_map/all_to_all | solution.py:331
  153.3 3.2 %collective-permute-done.26 = f16[128,512]{1,0:T(8,128)(2,1)S(1)} collective-permute-done((f16[128,512]{1,0:T(8,128)(2,1)S(1)}, f16[128,512]{1,0:T(8,128)(2,1)S(1)}, u32[]{:S(2)}, u32[]{:S(2)}) %collective-permute-start.26) | collective-permute-done | bytes 131104 | tf_op jit(solution)/shard_map/ppermute | solution.py:234
  156.6 2.5 %collective-permute-done.27 = f16[128,512]{1,0:T(8,128)(2,1)S(1)} collective-permute-done((f16[128,512]{1,0:T(8,128)(2,1)S(1)}, f16[128,512]{1,0:T(8,128)(2,1)S(1)}, u32[]{:S(2)}, u32[]{:S(2)}) %collective-permute-start.27) | collective-permute-done | bytes 131104 | tf_op jit(solution)/shard_map/ppermute | solution.py:234
  161.2 8.4 %collective-permute-done.32 = f16[256,512]{1,0:T(8,128)(2,1)S(1)} collective-permute-done((f16[256,512]{1,0:T(8,128)(2,1)S(1)}, f16[256,512]{1,0:T(8,128)(2,1)S(1)}, u32[]{:S(2)}, u32[]{:S(2)}) %collective-permute-start.32) | collective-permute-done | bytes 262176 | tf_op jit(solution)/shard_map/ppermute | solution.py:335
  (95 shorter events, 42.8 us)
Async XLA Ops:
  5.1 20.1 %collective-permute-start = (bf16[2,512,256]{2,1,0:T(8,128)(2,1)S(1)}, bf16[2,512,256]{2,1,0:T(8,128)(2,1)S(1)}, u32[]{:S(2)}, u32[]{:S(2)}) collective-permute-start(bf16[2,512,256]{2,1,0:T(8,128)(2,1)S(1)} %get-tuple-element.22), channel_id=1, source_target_pairs={{0,8},{8,16},{16,24},{24,32},{32,40},{40,48},{48,56},{56,64},{64,7... | collective-permute-start | bytes 1572872 | tf_op jit(solution)/shard_map/ppermute | solution.py:282
  7.0 18.2 %collective-permute-start.1 = (bf16[2,512,256]{2,1,0:T(8,128)(2,1)S(1)}, bf16[2,512,256]{2,1,0:T(8,128)(2,1)S(1)}, u32[]{:S(2)}, u32[]{:S(2)}) collective-permute-start(bf16[2,512,256]{2,1,0:T(8,128)(2,1)S(1)} %get-tuple-element.21), channel_id=1, source_target_pairs={{8,0},{16,8},{24,16},{32,24},{40,32},{48,40},{56,48},{64,56},{72,6... | collective-permute-start | bytes 1572872 | tf_op jit(solution)/shard_map/ppermute | solution.py:283
  23.8 12.8 %collective-permute-start.11 = (bf16[512,512]{1,0:T(8,128)(2,1)S(1)}, bf16[512,512]{1,0:T(8,128)(2,1)S(1)}, u32[]{:S(2)}, u32[]{:S(2)}) collective-permute-start(bf16[512,512]{1,0:T(8,128)(2,1)S(1)} %get-tuple-element.32), channel_id=1, source_target_pairs={{0,1},{1,0},{2,3},{3,2},{4,5},{5,4},{6,7},{7,6},{8,9},{9,8},{10,11... | collective-permute-start | bytes 1572872 | tf_op jit(solution)/shard_map/ppermute | solution.py:310
  25.3 12.5 %collective-permute-start.3 = (bf16[512,512]{1,0:T(8,128)(2,1)S(1)}, bf16[512,512]{1,0:T(8,128)(2,1)S(1)}, u32[]{:S(2)}, u32[]{:S(2)}) collective-permute-start(bf16[512,512]{1,0:T(8,128)(2,1)S(1)} %get-tuple-element.25.refs_1_), channel_id=1, source_target_pairs={{0,2},{2,4},{4,6},{6,0},{1,3},{3,5},{5,7},{7,1},{8,10},{10,12},{12... | collective-permute-start | bytes 1572872 | tf_op jit(solution)/shard_map/ppermute | solution.py:245
  25.5 13.5 %collective-permute-start.2 = (bf16[512,512]{1,0:T(8,128)(2,1)S(1)}, bf16[512,512]{1,0:T(8,128)(2,1)S(1)}, u32[]{:S(2)}, u32[]{:S(2)}) collective-permute-start(bf16[512,512]{1,0:T(8,128)(2,1)S(1)} %get-tuple-element.25.refs_1_), channel_id=1, source_target_pairs={{2,0},{4,2},{6,4},{0,6},{3,1},{5,3},{7,5},{1,7},{10,8},{12,10},{14... | collective-permute-start | bytes 1572872 | tf_op jit(solution)/shard_map/ppermute | solution.py:244
  27.3 26.6 %collective-permute-start.12 = (bf16[512,512]{1,0:T(8,128)(2,1)S(1)}, bf16[512,512]{1,0:T(8,128)(2,1)S(1)}, u32[]{:S(2)}, u32[]{:S(2)}) collective-permute-start(bf16[512,512]{1,0:T(8,128)(2,1)S(1)} %get-tuple-element.25.refs_1_), channel_id=1, source_target_pairs={{0,8},{8,0},{1,9},{9,1},{2,10},{10,2},{3,11},{11,3},{4,12},{12,4},... | collective-permute-start | bytes 1572872 | tf_op jit(solution)/shard_map/ppermute | solution.py:251
  36.6 28.3 %collective-permute-start.13 = (bf16[512,512]{1,0:T(8,128)(2,1)S(1)}, bf16[512,512]{1,0:T(8,128)(2,1)S(1)}, u32[]{:S(2)}, u32[]{:S(2)}) collective-permute-start(bf16[512,512]{1,0:T(8,128)(2,1)S(1)} %collective-permute-done.11.refs_2_), channel_id=1, source_target_pairs={{0,8},{8,0},{1,9},{9,1},{2,10},{10,2},{3,11},{11,3},{4,12},{12,4},... | collective-permute-start | bytes 1572872 | tf_op jit(solution)/shard_map/ppermute | solution.py:251
  39.0 26.6 %collective-permute-start.17 = (bf16[512,512]{1,0:T(8,128)(2,1)S(1)}, bf16[512,512]{1,0:T(8,128)(2,1)S(1)}, u32[]{:S(2)}, u32[]{:S(2)}) collective-permute-start(bf16[512,512]{1,0:T(8,128)(2,1)S(1)} %collective-permute-done.11.refs_2_), channel_id=1, source_target_pairs={{0,2},{2,4},{4,6},{6,0},{1,3},{3,5},{5,7},{7,1},{8,10},{10,12},{12... | collective-permute-start | bytes 1572872 | tf_op jit(solution)/shard_map/ppermute | solution.py:245
  39.3 27.9 %collective-permute-start.14 = (bf16[512,512]{1,0:T(8,128)(2,1)S(1)}, bf16[512,512]{1,0:T(8,128)(2,1)S(1)}, u32[]{:S(2)}, u32[]{:S(2)}) collective-permute-start(bf16[512,512]{1,0:T(8,128)(2,1)S(1)} %collective-permute-done.11.refs_2_), channel_id=1, source_target_pairs={{2,0},{4,2},{6,4},{0,6},{3,1},{5,3},{7,5},{1,7},{10,8},{12,10},{14... | collective-permute-start | bytes 1572872 | tf_op jit(solution)/shard_map/ppermute | solution.py:244
  51.6 14.1 %collective-permute-start.15 = (bf16[256,512]{1,0:T(8,128)(2,1)S(1)}, bf16[256,512]{1,0:T(8,128)(2,1)S(1)}, u32[]{:S(2)}, u32[]{:S(2)}) collective-permute-start(bf16[256,512]{1,0:T(8,128)(2,1)S(1)} %slice.113), channel_id=1, source_target_pairs={{0,8},{8,0},{1,9},{9,1},{2,10},{10,2},{3,11},{11,3},{4,12},{12,4},... | collective-permute-start | bytes 786440 | tf_op jit(solution)/shard_map/ppermute | solution.py:252
  53.9 13.9 %collective-permute-start.18 = (bf16[512,512]{1,0:T(8,128)(2,1)S(1)}, bf16[512,512]{1,0:T(8,128)(2,1)S(1)}, u32[]{:S(2)}, u32[]{:S(2)}) collective-permute-start(bf16[512,512]{1,0:T(8,128)(2,1)S(1)} %collective-permute-done.3.refs_9_), channel_id=1, source_target_pairs={{0,8},{8,0},{1,9},{9,1},{2,10},{10,2},{3,11},{11,3},{4,12},{12,4},... | collective-permute-start | bytes 1572872 | tf_op jit(solution)/shard_map/ppermute | solution.py:253
  64.9 14.3 %collective-permute-start.6 = (bf16[512,512]{1,0:T(8,128)(2,1)S(1)}, bf16[512,512]{1,0:T(8,128)(2,1)S(1)}, u32[]{:S(2)}, u32[]{:S(2)}) collective-permute-start(bf16[512,512]{1,0:T(8,128)(2,1)S(1)} %get-tuple-element.31), channel_id=1, source_target_pairs={{0,1},{1,0},{2,3},{3,2},{4,5},{5,4},{6,7},{7,6},{8,9},{9,8},{10,11... | collective-permute-start | bytes 1572872 | tf_op jit(solution)/shard_map/ppermute | solution.py:320
  65.7 14.2 %collective-permute-start.10 = (bf16[512,512]{1,0:T(8,128)(2,1)S(1)}, bf16[512,512]{1,0:T(8,128)(2,1)S(1)}, u32[]{:S(2)}, u32[]{:S(2)}) collective-permute-start(bf16[512,512]{1,0:T(8,128)(2,1)S(1)} %get-tuple-element.30.refs_1_), channel_id=1, source_target_pairs={{0,2},{2,4},{4,6},{6,0},{1,3},{3,5},{5,7},{7,1},{8,10},{10,12},{12... | collective-permute-start | bytes 1572872 | tf_op jit(solution)/shard_map/ppermute | solution.py:245
  67.2 15.1 %collective-permute-start.9 = (bf16[512,512]{1,0:T(8,128)(2,1)S(1)}, bf16[512,512]{1,0:T(8,128)(2,1)S(1)}, u32[]{:S(2)}, u32[]{:S(2)}) collective-permute-start(bf16[512,512]{1,0:T(8,128)(2,1)S(1)} %get-tuple-element.30.refs_1_), channel_id=1, source_target_pairs={{2,0},{4,2},{6,4},{0,6},{3,1},{5,3},{7,5},{1,7},{10,8},{12,10},{14... | collective-permute-start | bytes 1572872 | tf_op jit(solution)/shard_map/ppermute | solution.py:244
  82.3 13.1 %collective-permute-start.23 = (bf16[512,512]{1,0:T(8,128)(2,1)S(1)}, bf16[512,512]{1,0:T(8,128)(2,1)S(1)}, u32[]{:S(2)}, u32[]{:S(2)}) collective-permute-start(bf16[512,512]{1,0:T(8,128)(2,1)S(1)} %collective-permute-done.6.refs_2_), channel_id=1, source_target_pairs={{0,2},{2,4},{4,6},{6,0},{1,3},{3,5},{5,7},{7,1},{8,10},{10,12},{12... | collective-permute-start | bytes 1572872 | tf_op jit(solution)/shard_map/ppermute | solution.py:245
  82.5 14.3 %collective-permute-start.20 = (bf16[512,512]{1,0:T(8,128)(2,1)S(1)}, bf16[512,512]{1,0:T(8,128)(2,1)S(1)}, u32[]{:S(2)}, u32[]{:S(2)}) collective-permute-start(bf16[512,512]{1,0:T(8,128)(2,1)S(1)} %collective-permute-done.6.refs_2_), channel_id=1, source_target_pairs={{2,0},{4,2},{6,4},{0,6},{3,1},{5,3},{7,5},{1,7},{10,8},{12,10},{14... | collective-permute-start | bytes 1572872 | tf_op jit(solution)/shard_map/ppermute | solution.py:244
  84.3 12.6 %collective-permute-start.7 = (bf16[512,512]{1,0:T(8,128)(2,1)S(1)}, bf16[512,512]{1,0:T(8,128)(2,1)S(1)}, u32[]{:S(2)}, u32[]{:S(2)}) collective-permute-start(bf16[512,512]{1,0:T(8,128)(2,1)S(1)} %get-tuple-element.30.refs_1_), channel_id=1, source_target_pairs={{0,8},{8,0},{1,9},{9,1},{2,10},{10,2},{3,11},{11,3},{4,12},{12,4},... | collective-permute-start | bytes 1572872 | tf_op jit(solution)/shard_map/ppermute | solution.py:251
  84.3 14.1 %collective-permute-start.8 = (bf16[512,512]{1,0:T(8,128)(2,1)S(1)}, bf16[512,512]{1,0:T(8,128)(2,1)S(1)}, u32[]{:S(2)}, u32[]{:S(2)}) collective-permute-start(bf16[512,512]{1,0:T(8,128)(2,1)S(1)} %collective-permute-done.6.refs_2_), channel_id=1, source_target_pairs={{0,8},{8,0},{1,9},{9,1},{2,10},{10,2},{3,11},{11,3},{4,12},{12,4},... | collective-permute-start | bytes 1572872 | tf_op jit(solution)/shard_map/ppermute | solution.py:251
  84.8 13.6 %collective-permute-start.24 = (bf16[512,512]{1,0:T(8,128)(2,1)S(1)}, bf16[512,512]{1,0:T(8,128)(2,1)S(1)}, u32[]{:S(2)}, u32[]{:S(2)}) collective-permute-start(bf16[512,512]{1,0:T(8,128)(2,1)S(1)} %collective-permute-done.10.refs_9_), channel_id=1, source_target_pairs={{0,8},{8,0},{1,9},{9,1},{2,10},{10,2},{3,11},{11,3},{4,12},{12,4},... | collective-permute-start | bytes 1572872 | tf_op jit(solution)/shard_map/ppermute | solution.py:253
  108.2 35.7 %all-to-all-start = ((f16[4,4,128,512]{3,2,1,0:T(8,128)(2,1)}), f16[4,4,128,512]{3,2,1,0:T(8,128)(2,1)S(1)}, u32[]{:S(2)}, u32[]{:S(2)}) async-start(f16[4,4,128,512]{3,2,1,0:T(8,128)(2,1)} %bitcast.6), calls=%async_computation | async-start | bytes 4194304 | tf_op jit(solution)/shard_map/all_to_all | solution.py:328
  116.3 15.4 %collective-permute-start.29 = (f16[4,128,512]{2,1,0:T(8,128)(2,1)S(1)}, f16[4,128,512]{2,1,0:T(8,128)(2,1)S(1)}, u32[]{:S(2)}, u32[]{:S(2)}) collective-permute-start(f16[4,128,512]{2,1,0:T(8,128)(2,1)S(1)} %get-tuple-element.40), channel_id=1, source_target_pairs={{0,1},{1,16},{16,17},{17,0},{2,3},{3,18},{18,19},{19,2},{4,5},{5,2... | collective-permute-start | bytes 1572872 | tf_op jit(solution)/shard_map/ppermute | solution.py:234
  117.8 14.9 %collective-permute-start.31 = (f16[4,128,512]{2,1,0:T(8,128)(2,1)S(1)}, f16[4,128,512]{2,1,0:T(8,128)(2,1)S(1)}, u32[]{:S(2)}, u32[]{:S(2)}) collective-permute-start(f16[4,128,512]{2,1,0:T(8,128)(2,1)S(1)} %get-tuple-element.41), channel_id=1, source_target_pairs={{0,17},{1,0},{16,1},{17,16},{2,19},{3,2},{18,3},{19,18},{4,21},{5,... | collective-permute-start | bytes 1572872 | tf_op jit(solution)/shard_map/ppermute | solution.py:234
  119.6 23.1 %collective-permute-start.30 = (f16[4,128,512]{2,1,0:T(8,128)(2,1)S(1)}, f16[4,128,512]{2,1,0:T(8,128)(2,1)S(1)}, u32[]{:S(2)}, u32[]{:S(2)}) collective-permute-start(f16[4,128,512]{2,1,0:T(8,128)(2,1)S(1)} %get-tuple-element.42), channel_id=1, source_target_pairs={{0,16},{1,17},{16,0},{17,1},{2,18},{3,19},{18,2},{19,3},{4,20},{5,... | collective-permute-start | bytes 1572872 | tf_op jit(solution)/shard_map/ppermute | solution.py:234
  144.4 14.7 %all-to-all-start.1 = ((f16[4,128,512]{2,1,0:T(8,128)(2,1)}), f16[4,128,512]{2,1,0:T(8,128)(2,1)S(1)}, u32[]{:S(2)}, u32[]{:S(2)}) async-start(f16[4,128,512]{2,1,0:T(8,128)(2,1)} %multiply_convert_fusion.2), calls=%async_computation.1 | async-start | bytes 1048576 | tf_op jit(solution)/shard_map/all_to_all | solution.py:331
  (19 other events, 111.8 us)

commit v4 on v3

--- a/solution.py
+++ b/solution.py
@@ -10,6 +10,7 @@
 HALF = jnp.float16
 BF = jnp.bfloat16
 VMEM_LIMIT = 16 * 1024 * 1024
+ALMOST_ALL = 60 * 1024 * 1024
 LIFT = 1.0 / 256
 SWAP = [(0, 1), (1, 0)]
 INNER = 100 << 20
@@ -24,27 +25,48 @@
     return pl.CostEstimate(flops=flops, bytes_accessed=moved, transcendentals=0)
 
 
-def edge_kernel(x_ref, top_ref, bot_ref):
-    top_ref[0] = x_ref[:, 0, :].astype(BF)
-    top_ref[1] = x_ref[:, 1, :].astype(BF)
-    bot_ref[0] = x_ref[:, 6, :].astype(BF)
-    bot_ref[1] = x_ref[:, 7, :].astype(BF)
-
-
-def edges(field):
+def edge_kernel(x_ref, c_ref, top_ref, bot_ref):
+    i = pl.program_id(0)
+    block, rows, _ = x_ref.shape
+    at = pl.ds(pl.multiple_of(i * block, block), block)
+    for out_ref, first, edge in ((top_ref, 0, 0), (bot_ref, rows - 2, rows - 1)):
+        out_ref[0, at, :] = x_ref[:, first, :].astype(BF)
+        out_ref[1, at, :] = x_ref[:, first + 1, :].astype(BF)
+
+        @pl.when(i == 0)
+        def _():
+            rest = c_ref[:, edge, :]
+            terms = []
+            for _ in range(3):
+                terms.append(rest.astype(BF).astype(jnp.float32))
+                rest = rest - terms[-1]
+            packed = jnp.concatenate(terms + [jnp.zeros_like(rest)], axis=0).astype(BF)
+            last = out_ref.shape[1] - packed.shape[0]
+            for k in range(2):
+                out_ref[k, last:, :] = packed
+
+
+def edges(field, courant):
     groups, rows, width = field.shape
     block = 64
-    shape = jax.ShapeDtypeStruct((2, groups, width), BF)
-    spec = pl.BlockSpec((2, block, width), lambda i: (0, i, 0))
+    shape = jax.ShapeDtypeStruct((2, groups + 16, width), BF)
+    spec = pl.BlockSpec(shape.shape, lambda i: (0, 0, 0))
     return pl.pallas_call(
         edge_kernel,
         grid=(groups // block,),
-        in_specs=[pl.BlockSpec((block, rows, width), lambda i: (i, 0, 0))],
+        in_specs=[
+            pl.BlockSpec((block, rows, width), lambda i: (i, 0, 0)),
+            pl.BlockSpec(courant.shape, lambda i: (0, 0, 0)),
+        ],
         out_specs=[spec, spec],
         out_shape=[shape, shape],
         cost_estimate=cost(1000, 6 << 20),
-        compiler_params=params(),
-    )(field)
+        compiler_params=pltpu.CompilerParams(vmem_limit_bytes=ALMOST_ALL),
+    )(field, courant)
+
+
+def edge_weights(halo, groups):
+    return jnp.sum(halo[0, groups:groups + 12].astype(jnp.float32).reshape(3, 4, 1, -1), axis=0)
 
 
 def stepper(coef_ref, offset, delta, width):
@@ -92,7 +114,7 @@
                     put(keep_ref, send_ref, at, q - 4, own_first, prints[q - 2], prints[q])
         return carry
 
-    lax.fori_loop(0, block // 16, group, 0, unroll=2)
+    lax.fori_loop(0, block // 16, group, 0, unroll=4)
 
 
 def outer_kernel(info, x_ref, up_ref, down_ref, coef_ref, emis_ref, det_ref, mid_ref, adv_ref, keep_ref, send_ref):
@@ -128,10 +150,10 @@
             put(keep_ref, send_ref, at, p, own_first, prints[p], prints[p + 6])
         return carry
 
-    lax.fori_loop(0, block // 16, group, 0, unroll=2)
-
-
-def stencil(kernel, info, field, halos, coef, emis, det, mid, work):
+    lax.fori_loop(0, block // 16, group, 0, unroll=4)
+
+
+def stencil(kernel, info, field, halos, coef, emis, det, mid, work, limit):
     groups, rows, width = field.shape
     block = 64
     count = groups // block
@@ -164,7 +186,7 @@
         out_shape=[jax.ShapeDtypeStruct(field.shape, jnp.float32), print_shape, print_shape],
         input_output_aliases={len(operands): 0} if mid else {},
         cost_estimate=cost(1000, work),
-        compiler_params=params(),
+        compiler_params=pltpu.CompilerParams(vmem_limit_bytes=limit),
     )(info, *operands)
 
 
@@ -176,56 +198,112 @@
 
 
 def gram_kernel(grows, info, *refs):
-    stack, outs = refs[-1], refs[-3:-1]
-    accs = refs[12:14] if grows else None
+    if grows:
+        accs, (*outs, done_ref, stack, acc_buf, sem) = refs[12:14], refs[15:]
+        copies = [
+            pltpu.make_async_copy(accs[upper], acc_buf.at[upper], sem.at[upper]) for upper in range(2)
+        ]
+    else:
+        *outs, done_ref, stack = refs[12:]
+    done_ref[...] = jnp.zeros_like(done_ref)
     own, own_s, nxt, nxt_s, last, last_s = (refs[2 * k:2 * k + 2] for k in range(6))
-    core, xl, y, xpos = info[0], info[1], info[3], info[4]
+    core, xl, y, xpos, z = info[0], info[1], info[3], info[4], info[5]
     rows = nxt_s[0].shape[0]
     half = own[0].shape[1]
     part = rows // 2
-    lefts = []
-    for e, tile, sibling, first in ((1, nxt, nxt_s, 0), (0, own, own_s, rows), (3, last, last_s, rows)):
-        for i in range(2):
-            at = pl.ds(len(lefts) * rows, rows)
+    m = pl.program_id(0)
+    places = [(e, i) for e in (1, 0, 3) for i in range(2)]
+
+    @pl.when(m == 0)
+    def _():
+        if grows:
+            for copy in copies:
+                copy.start()
+        for k, (e, i) in enumerate(places):
+            tile, sibling, first = ((own, own_s, rows), (nxt, nxt_s, 0), None, (last, last_s, rows))[e]
+            at = pl.ds(k * rows, rows)
             stack[at, :half] = tile[i][:rows, :]
             stack[at, half:] = sibling[i][first:first + rows, :]
-            lefts.append((e, i))
-
+
+    mine = pl.ds(pl.multiple_of(m * rows, rows), rows)
+    theirs = pl.ds(pl.multiple_of((1 - m) * rows, rows), rows)
+    cols = slice(None)
+    if grows:
+        cols = pl.ds(pl.multiple_of(lax.rem(core + m, 2) * rows, rows), rows)
     for j in range(2):
-        for m in range(2):
-            mine = slice(m * rows, (m + 1) * rows)
-            theirs = slice((1 - m) * rows, (2 - m) * rows)
-            here = dot(stack[:, :half], own[j][mine, :]) + dot(stack[:, half:], own_s[j][theirs, :])
-            far = dot(stack[:2 * rows, :half], last[j][mine, :]) + dot(
-                stack[:2 * rows, half:], last_s[j][theirs, :]
-            )
-            cols = pl.ds(pl.multiple_of(lax.rem(core + m, 2) * rows, rows), rows)
-            values = [(e, i, here[k * rows:(k + 1) * rows]) for k, (e, i) in enumerate(lefts)]
-            values += [(2, i, far[i * rows:(i + 1) * rows]) for i in range(2)]
-            for e, i, value in values:
-                at_z = lax.rem(y + e, 4)
-                at_x = lax.rem(lax.rem(i + xl, 2) * 2 + lax.rem(j + xl, 2) + 4 - xpos, 4)
-                for upper, slot in enumerate((at_z * 4 + at_x, at_x * 4 + at_z)):
-                    piece = value[upper * part:(upper + 1) * part]
-                    if accs is not None:
-                        piece = piece + accs[upper][slot, :, cols]
-                    outs[upper][slot, :, cols] = piece
+        here = dot(stack[:, :half], own[j][mine, :]) + dot(stack[:, half:], own_s[j][theirs, :])
+        far = dot(stack[:2 * rows, :half], last[j][mine, :]) + dot(
+            stack[:2 * rows, half:], last_s[j][theirs, :]
+        )
+        if grows and j == 0:
+            @pl.when(m == 0)
+            def _():
+                for copy in copies:
+                    copy.wait()
+        values = [(e, i, here[k * rows:(k + 1) * rows]) for k, (e, i) in enumerate(places)]
+        values += [(2, i, far[i * rows:(i + 1) * rows]) for i in range(2)]
+        for e, i, value in values:
+            at_z = lax.rem(y + e + 4 - z, 4)
+            at_x = lax.rem(lax.rem(i + xl, 2) * 2 + lax.rem(j + xl, 2) + 4 - xpos, 4)
+            for upper, slot in enumerate((at_z * 4 + at_x, at_x * 4 + at_z)):
+                piece = value[upper * part:(upper + 1) * part]
+                if grows:
+                    piece = piece + acc_buf[upper, slot, :, cols]
+                outs[upper][slot, :, cols] = piece
 
 
 def partial_gram(info, operands, acc):
     rows, half = operands[0].shape
     rows = rows // 2
     whole = pl.BlockSpec(memory_space=pltpu.VMEM)
-    shape = jax.ShapeDtypeStruct((16, rows // 2, 2 * rows), jnp.float32)
+    shape = (jax.ShapeDtypeStruct if acc else pltpu.HBM)((16, rows // 2, 2 * rows), jnp.float32)
+    block = pl.BlockSpec(
+        (16, rows // 2, rows), lambda m, info: (0, 0, lax.rem(info[0] + m, 2))
+    )
+    far = pl.BlockSpec(memory_space=pltpu.HBM)
+    grown = [
+        pltpu.VMEM((2, 16, rows // 2, 2 * rows), jnp.float32), pltpu.SemaphoreType.DMA((2,))
+    ]
+    token = pl.BlockSpec((8, 128), lambda m, info: (0, 0))
     return pl.pallas_call(
         lambda *refs: gram_kernel(bool(acc), *refs),
-        in_specs=[pl.BlockSpec(memory_space=pltpu.SMEM)] + [whole] * (len(operands) + len(acc)),
-        out_specs=[whole, whole],
-        out_shape=[shape, shape],
-        scratch_shapes=[pltpu.VMEM((6 * rows, 2 * half), BF)],
+        grid_spec=pltpu.PrefetchScalarGridSpec(
+            num_scalar_prefetch=1,
+            grid=(2,),
+            in_specs=[whole] * len(operands) + [far, far, token][:len(acc)],
+            out_specs=([whole, whole] if acc else [block, block])
+            + [token],
+            scratch_shapes=[pltpu.VMEM((6 * rows, 2 * half), BF)] + (grown if acc else []),
+        ),
+        out_shape=[shape, shape, jax.ShapeDtypeStruct((8, 128), jnp.float32)],
         cost_estimate=cost(1000, 8 << 20),
-        compiler_params=params(),
+        compiler_params=pltpu.CompilerParams(vmem_limit_bytes=(46 if acc else 24) << 20),
     )(info, *operands, *acc)
+
+
+def place(z, y, x):
+    return ((z % 4 * 2 + x % 4 // 2) * 4 + y % 4) * 2 + x % 2
+
+
+def to_place(pieces, dz, dx):
+    z, y = lax.axis_index("z"), lax.axis_index("y")
+    total = 0.0
+    for d in range(4):
+        pairs = []
+        for zi in range(4):
+            for yi in range(4):
+                for xi in range(4):
+                    zt, yt, xt = zi + d * dz, yi, xi + d * dx
+                    if (zt - yt) % 4 == 2:
+                        zt, yt = zt - 1, yt - 1
+                    elif d == 0:
+                        continue
+                    pairs.append((place(zi, yi, xi), place(zt, yt, xt)))
+        came = lax.ppermute(pieces[d], ("z", "xh", "y", "xl"), pairs)
+        if d == 0:
+            came = jnp.where(lax.rem(y + 2, 4) == z, came, pieces[0])
+        total = total + came.astype(jnp.float32)
+    return total * 0.25
 
 
 def to_four(pieces, axis):
@@ -258,10 +336,6 @@
     return [
         array for pair in zip(siblings(keep, *keep_y), siblings(other, *other_y)) for array in pair
     ]
-
-
-def mean_of_four(pieces):
-    return jnp.sum(pieces.astype(jnp.float32), axis=0) * 0.25
 
 
 def body(adjoint, courant, detector, sources, emission):
@@ -273,17 +347,14 @@
     tile = lax.axis_index(GRID)
     first_cell = tile * rows * width
     xpos = lax.axis_index(XS)
-    info = jnp.stack([core, xl, first_cell, y, xpos]).astype(jnp.int32)
+    info = jnp.stack([core, xl, first_cell, y, xpos, z]).astype(jnp.int32)
     count = lax.axis_size(GRID)
     forward = [(i, i + 1) for i in range(count - 1)]
     backward = [(i + 1, i) for i in range(count - 1)]
 
-    top, bottom = edges(adjoint)
+    top, bottom = edges(adjoint, courant)
     up = lax.ppermute(bottom, GRID, forward)
     down = lax.ppermute(top, GRID, backward)
-    near = after(courant, top)
-    coef_up = lax.ppermute(near[:, rows - 1:], GRID, forward)
-    coef_down = lax.ppermute(near[:, :1], GRID, backward)
     columns = jnp.arange(width)
 
     def weights(c):
@@ -305,35 +376,33 @@
 
     weights_in = weights(courant)
     mid, keep, send = stencil(
-        inner_kernel, after(info, top, bottom), adjoint, [], weights_in, emis, det, [], INNER
+        inner_kernel, after(info, top, bottom), adjoint, [], weights_in, emis, det, [], INNER,
+        VMEM_LIMIT,
     )
     other = lax.ppermute(send, "xl", SWAP)
     keep_y = along_y(after(keep, up, down))
     other_y = along_y(after(other, keep_y))
-    totals = partial_gram(info, gram_operands(keep, keep_y, other, other_y), [])
-
-    extended = jnp.concatenate([coef_up, courant, coef_down], axis=1)
+    *totals, done = partial_gram(info, gram_operands(keep, keep_y, other, other_y), [])
+
+    extended = jnp.concatenate(
+        [edge_weights(up, groups), courant, edge_weights(down, groups)], axis=1
+    )
     field, keep, send = stencil(
         outer_kernel, after(info, keep_y), adjoint, [up, down], weights(extended), emis, det,
-        [mid], OUTER
+        [mid], OUTER, VMEM_LIMIT
     )
     other = lax.ppermute(send, "xl", SWAP)
     keep_y = along_y(keep)
-    other_y = along_y(after(other, keep_y, totals))
-    totals = partial_gram(info, gram_operands(keep, keep_y, other, other_y), totals)
-
-    along_z, along_x = [
-        (total * LIFT).astype(HALF).reshape(4, 4, groups // 4, groups) for total in totals
-    ]
-    along_z = lax.all_to_all(along_z, "z", 0, 0, tiled=True)
-    along_x = after(to_four(along_x, XS).astype(HALF), along_z)
-    along_z = mean_of_four(along_z).astype(HALF)
-    along_x = mean_of_four(lax.all_to_all(along_x, "z", 0, 0, tiled=True))
-    along_z = to_four(along_z, XS)
-    summed = jnp.concatenate([along_z, along_x], axis=0)
-    moves = [((i + 2) % 4 * 4 + i, (i + 1) % 4 * 4 + (i + 3) % 4) for i in range(4)]
-    moved = lax.ppermute(summed.astype(HALF), ("z", "y"), moves).astype(jnp.float32)
-    summed = jnp.where(lax.rem(y + 2, 4) == z, moved, summed)
+    sent, done, _ = lax.optimization_barrier((other, done, keep_y))
+    other_y = along_y(sent)
+    *totals, _ = partial_gram(info, gram_operands(keep, keep_y, other, other_y), totals + [done])
+
+    def packed(total):
+        return (total * LIFT).astype(HALF).reshape(4, 4, groups // 4, groups)
+
+    along_z = to_four(packed(totals[0]), "z").astype(HALF)
+    along_x = to_four(packed(totals[1]), XS).astype(HALF)
+    summed = jnp.concatenate([to_place(along_z, 0, 1), to_place(along_x, 1, 0)], axis=0)
     total_sources = sources.shape[0] * count
     return field, summed * jnp.float32(16.0 / (LIFT * total_sources))
 

time: 171 us -> 173 us (1.012)
  the two profiles are of different devices: /device:TPU:56 before, /device:TPU:8 now
where the time goes in v4:
time: 173 us
  starting transfers between devices  53.3 us (31%)
  waiting for transfers between devices  51.6 us (30%)
  Pallas kernels  49.7 us (29%)
  local copies, waits for them, and re-layouts  10.8 us (6%)
  other arithmetic  5.38 us (3%)
    pallas_call x2, Pallas kernels, partial_gram(): pl.pallas_call(lambda *refs: gram_kernel(bool(acc), *refs), grid_spec=plt...  24.1 us
    ppermute x8, starting transfers between devices, to_place(): came = lax.ppermute(pieces[d], ('z', 'xh', 'y', 'xl'), pairs)  21.5 us
    pallas_call x2, Pallas kernels, stencil(): pl.pallas_call(kernel, grid_spec=pltpu.PrefetchScalarGridSpec(num_scalar_...  18.8 us
    ppermute x6, waiting for transfers between devices, to_four(): came = lax.ppermute(pieces[d], axis, [(i, (i + d) % 4) for i in range(4)])  18.1 us
    ppermute x6, starting transfers between devices, to_four(): came = lax.ppermute(pieces[d], axis, [(i, (i + d) % 4) for i in range(4)])  12.1 us
    ppermute x4, waiting for transfers between devices, along_y(): last = lax.ppermute(own, 'y', [(i, (i + 1) % 4) for i in range(4)])  11.6 us
    unnamed x26, local copies, waits for them, and re-layouts  8.1 us
    ppermute x2, waiting for transfers between devices, body(): other = lax.ppermute(send, 'xl', SWAP)  7.96 us
  transfers between devices with their start and end apart: 38, of which 14 were waited for; matrix products, arithmetic and copies ran while one was open for 3% of the time, Pallas kernels for 16%

profile of v4, /device:TPU:8, one launch (start us, length us, event | category | flops | bytes accessed | tf_op | source)
XLA Modules:
  0.0 172.7 jit_solution(169737435600326429)
XLA Ops:
  0.7 6.8 %shard_map.68 = (bf16[2,528,256]{2,1,0:T(8,128)(2,1)}, bf16[2,528,256]{2,1,0:T(8,128)(2,1)}) custom-call(f32[512,8,256]{2,1,0:T(8,128)} %x_ref.5, f32[4,8,256]{2,1,0:T(8,128)} %c_ref.1), custom_call_target="tpu_custom_call" | custom-call | flops 1000 | bytes 6291456 | tf_op jit(solution)/shard_map/pallas_call | solution.py:54
  8.8 3.1 %collective-permute-start = (bf16[2,528,256]{2,1,0:T(8,128)(2,1)}, bf16[2,528,256]{2,1,0:T(8,128)(2,1)S(1)}, u32[]{:S(2)}, u32[]{:S(2)}) collective-permute-start(bf16[2,528,256]{2,1,0:T(8,128)(2,1)} %get-tuple-element.22), channel_id=1, source_target_pairs={{0,8},{8,16},{16,24},{24,32},{32,40},{40,48},{48,56},{56,64},{64,7... | collective-permute-start | bytes 1622024 | tf_op jit(solution)/shard_map/ppermute | solution.py:356
  13.0 2.2 %copy-done = f32[512,8,256]{2,1,0:T(8,128)S(1)} copy-done((f32[512,8,256]{2,1,0:T(8,128)S(1)}, f32[512,8,256]{2,1,0:T(8,128)}, u32[]{:S(2)}) %copy-start) | copy-done | bytes 4194328
  15.2 7.7 %shard_map.69 = (f32[512,8,256]{2,1,0:T(8,128)}, bf16[512,512]{1,0:T(8,128)(2,1)S(1)}, bf16[512,512]{1,0:T(8,128)(2,1)S(1)}) custom-call(s32[6]{0:T(128)S(1)} %stack.39.info.refs_0_, f32[512,8,256]{2,1,0:T(8,128)S(1)} %copy-done, f32[5,8,256]{2,1,0:T(8,128)S(1)} %pad_maximum_fusion.2.coef_ref, f32[8,256]{1,0:T(8,128)S(1)} %fusion.emis_ref, ...), custom_call_target="tpu_custom_call" | custom-call | flops 1000 | bytes 104857600 | tf_op jit(solution)/shard_map/pallas_call | solution.py:171
  28.2 8.0 %collective-permute-done.8.refs_2_ = bf16[512,512]{1,0:T(8,128)(2,1)} collective-permute-done((bf16[512,512]{1,0:T(8,128)(2,1)S(1)}, bf16[512,512]{1,0:T(8,128)(2,1)}, u32[]{:S(2)}, u32[]{:S(2)}) %collective-permute-start.8) | collective-permute-done | bytes 524320 | tf_op jit(solution)/shard_map/ppermute | solution.py:382
  36.1 1.8 %collective-permute-start.10 = (bf16[512,512]{1,0:T(8,128)(2,1)}, bf16[512,512]{1,0:T(8,128)(2,1)}, u32[]{:S(2)}, u32[]{:S(2)}) collective-permute-start(bf16[512,512]{1,0:T(8,128)(2,1)} %collective-permute-done.8.refs_2_), channel_id=1, source_target_pairs={{0,8},{8,0},{1,9},{9,1},{2,10},{10,2},{3,11},{11,3},{4,12},{12,4},... | collective-permute-start | bytes 1572872 | tf_op jit(solution)/shard_map/ppermute | solution.py:329
  38.0 1.8 %collective-permute-done.2.refs_5_ = bf16[512,512]{1,0:T(8,128)(2,1)S(1)} collective-permute-done((bf16[512,512]{1,0:T(8,128)(2,1)S(1)}, bf16[512,512]{1,0:T(8,128)(2,1)S(1)}, u32[]{:S(2)}, u32[]{:S(2)}) %collective-permute-start.2) | collective-permute-done | bytes 524320 | tf_op jit(solution)/shard_map/ppermute | solution.py:322
  43.4 2.2 %copy-done.1 = f32[512,8,256]{2,1,0:T(8,128)S(1)} copy-done((f32[512,8,256]{2,1,0:T(8,128)S(1)}, f32[512,8,256]{2,1,0:T(8,128)}, u32[]{:S(2)}) %copy-start.1) | copy-done | bytes 4194328
  45.6 11.1 %shard_map.70 = (f32[512,8,256]{2,1,0:T(8,128)}, bf16[512,512]{1,0:T(8,128)(2,1)S(1)}, bf16[512,512]{1,0:T(8,128)(2,1)S(1)}) custom-call(s32[6]{0:T(128)S(1)} %stack.39.info.refs_0_, f32[512,8,256]{2,1,0:T(8,128)S(1)} %copy-done.1, bf16[2,528,256]{2,1,0:T(8,128)(2,1)S(1)} %collective-permute-done.up_ref, ...), custom_call_target="tpu_custom_call", output_to_operand_aliasing={{0}: (7, {})} | custom-call | flops 1000 | bytes 20971520 | tf_op jit(solution)/shard_map/pallas_call | solution.py:171
  62.0 9.4 %shard_map.71 = (f32[16,128,512]{2,1,0:T(8,128)}, f32[16,128,512]{2,1,0:T(8,128)}, f32[8,128]{1,0:T(8,128)S(1)}) custom-call(s32[6]{0:T(128)S(1)} %stack.39.info.refs_0_, bf16[512,512]{1,0:T(8,128)(2,1)S(1)} %copy-done.3, bf16[512,512]{1,0:T(8,128)(2,1)} %collective-permute-done.8.refs_2_, bf16[512,512]{1,0:T(8,128)(2,1)S(1)} %copy-done.5, ...), custom_call_target="tpu_custom_call" | custom-call | flops 1000 | bytes 8388608 | tf_op jit(solution)/shard_map/pallas_call | solution.py:268
  75.0 11.4 %collective-permute-done.21.refs_10_ = bf16[512,512]{1,0:T(8,128)(2,1)S(1)} collective-permute-done((bf16[512,512]{1,0:T(8,128)(2,1)S(1)}, bf16[512,512]{1,0:T(8,128)(2,1)S(1)}, u32[]{:S(2)}, u32[]{:S(2)}) %collective-permute-start.21) | collective-permute-done | bytes 524320 | tf_op jit(solution)/shard_map/ppermute | solution.py:323
  92.4 14.7 %shard_map.72 = (f32[16,128,512]{2,1,0:T(8,128)}, f32[16,128,512]{2,1,0:T(8,128)}, f32[8,128]{1,0:T(8,128)}) custom-call(s32[6]{0:T(128)S(1)} %stack.39.info.refs_0_, bf16[512,512]{1,0:T(8,128)(2,1)S(1)} %get-tuple-element.29.refs_1_, bf16[512,512]{1,0:T(8,128)(2,1)S(1)} %collective-permute-done.4.refs_2_, bf16[512,512]{1,0:T(8,128)(2,1)S(1)} %copy-done.7, ...), custom_call_target="tpu_custom_call" | custom-call | flops 1000 | bytes 8388608 | tf_op jit(solution)/shard_map/pallas_call | solution.py:268
  107.2 3.0 %multiply_convert_fusion.1 = f16[16,128,512]{2,1,0:T(8,128)(2,1)S(1)} fusion(f32[16,128,512]{2,1,0:T(8,128)} %get-tuple-element.38), kind=kLoop, calls=%fused_computation.1 | loop fusion | flops 2097152 | bytes 6291456 | tf_op jit(solution)/shard_map/convert_element_type | solution.py:401
  110.5 4.3 %collective-permute-start.24 = (f16[4,128,512]{2,1,0:T(8,128)(2,1)S(1)}, f16[4,128,512]{2,1,0:T(8,128)(2,1)S(1)}, u32[]{:S(2)}, u32[]{:S(2)}) collective-permute-start(f16[4,128,512]{2,1,0:T(8,128)(2,1)S(1)} %get-tuple-element.40), channel_id=1, source_target_pairs={{0,32},{32,64},{64,96},{96,0},{1,33},{33,65},{65,97},{97,1},{2,34}... | collective-permute-start | bytes 1572872 | tf_op jit(solution)/shard_map/ppermute | solution.py:312
  114.8 2.2 %collective-permute-start.26 = (f16[4,128,512]{2,1,0:T(8,128)(2,1)S(1)}, f16[4,128,512]{2,1,0:T(8,128)(2,1)S(1)}, u32[]{:S(2)}, u32[]{:S(2)}) collective-permute-start(f16[4,128,512]{2,1,0:T(8,128)(2,1)S(1)} %get-tuple-element.41), channel_id=1, source_target_pairs={{0,96},{32,0},{64,32},{96,64},{1,97},{33,1},{65,33},{97,65},{2,98}... | collective-permute-start | bytes 1572872 | tf_op jit(solution)/shard_map/ppermute | solution.py:312
  117.0 1.8 %collective-permute-start.25 = (f16[4,128,512]{2,1,0:T(8,128)(2,1)S(1)}, f16[4,128,512]{2,1,0:T(8,128)(2,1)S(1)}, u32[]{:S(2)}, u32[]{:S(2)}) collective-permute-start(f16[4,128,512]{2,1,0:T(8,128)(2,1)S(1)} %get-tuple-element.42), channel_id=1, source_target_pairs={{0,64},{32,96},{64,0},{96,32},{1,65},{33,97},{65,1},{97,33},{2,66}... | collective-permute-start | bytes 1572872 | tf_op jit(solution)/shard_map/ppermute | solution.py:312
  120.8 2.2 %collective-permute-start.33 = (f16[4,128,512]{2,1,0:T(8,128)(2,1)S(1)}, f16[4,128,512]{2,1,0:T(8,128)(2,1)S(1)}, u32[]{:S(2)}, u32[]{:S(2)}) collective-permute-start(f16[4,128,512]{2,1,0:T(8,128)(2,1)S(1)} %get-tuple-element.44), channel_id=1, source_target_pairs={{0,17},{1,0},{16,1},{17,16},{2,19},{3,2},{18,3},{19,18},{4,21},{5,... | collective-permute-start | bytes 1572872 | tf_op jit(solution)/shard_map/ppermute | solution.py:312
  123.0 6.3 %collective-permute-done.24 = f16[4,128,512]{2,1,0:T(8,128)(2,1)S(1)} collective-permute-done((f16[4,128,512]{2,1,0:T(8,128)(2,1)S(1)}, f16[4,128,512]{2,1,0:T(8,128)(2,1)S(1)}, u32[]{:S(2)}, u32[]{:S(2)}) %collective-permute-start.24) | collective-permute-done | bytes 524320 | tf_op jit(solution)/shard_map/ppermute | solution.py:312
  129.9 10.0 %collective-permute-done.26 = f16[4,128,512]{2,1,0:T(8,128)(2,1)S(1)} collective-permute-done((f16[4,128,512]{2,1,0:T(8,128)(2,1)S(1)}, f16[4,128,512]{2,1,0:T(8,128)(2,1)S(1)}, u32[]{:S(2)}, u32[]{:S(2)}) %collective-permute-start.26) | collective-permute-done | bytes 524320 | tf_op jit(solution)/shard_map/ppermute | solution.py:312
  139.9 1.8 %collective-permute-done.25 = f16[4,128,512]{2,1,0:T(8,128)(2,1)S(1)} collective-permute-done((f16[4,128,512]{2,1,0:T(8,128)(2,1)S(1)}, f16[4,128,512]{2,1,0:T(8,128)(2,1)S(1)}, u32[]{:S(2)}, u32[]{:S(2)}) %collective-permute-start.25) | collective-permute-done | bytes 524320 | tf_op jit(solution)/shard_map/ppermute | solution.py:312
  143.5 3.8 %collective-permute-start.29 = (f16[128,512]{1,0:T(8,128)(2,1)S(1)}, f16[128,512]{1,0:T(8,128)(2,1)S(1)}, u32[]{:S(2)}, u32[]{:S(2)}) collective-permute-start(f16[128,512]{1,0:T(8,128)(2,1)S(1)} %get-tuple-element.48), channel_id=1, source_target_pairs={{0,16},{1,17},{16,0},{17,1},{2,18},{3,19},{18,2},{19,3},{4,114},{5... | collective-permute-start | bytes 393224 | tf_op jit(solution)/shard_map/ppermute | solution.py:302
  148.4 15.6 %collective-permute-start.37 = (f16[128,512]{1,0:T(8,128)(2,1)S(1)}, f16[128,512]{1,0:T(8,128)(2,1)S(1)}, u32[]{:S(2)}, u32[]{:S(2)}) collective-permute-start(f16[128,512]{1,0:T(8,128)(2,1)S(1)} %get-tuple-element.51), channel_id=1, source_target_pairs={{0,96},{1,97},{16,112},{17,113},{2,64},{3,65},{18,80},{19,81},{4,1... | collective-permute-start | bytes 393224 | tf_op jit(solution)/shard_map/ppermute | solution.py:302
  164.3 2.3 %collective-permute-done.37 = f16[128,512]{1,0:T(8,128)(2,1)S(1)} collective-permute-done((f16[128,512]{1,0:T(8,128)(2,1)S(1)}, f16[128,512]{1,0:T(8,128)(2,1)S(1)}, u32[]{:S(2)}, u32[]{:S(2)}) %collective-permute-start.37) | collective-permute-done | bytes 131104 | tf_op jit(solution)/shard_map/ppermute | solution.py:302
  166.6 4.0 %collective-permute-done.36 = f16[128,512]{1,0:T(8,128)(2,1)S(1)} collective-permute-done((f16[128,512]{1,0:T(8,128)(2,1)S(1)}, f16[128,512]{1,0:T(8,128)(2,1)S(1)}, u32[]{:S(2)}, u32[]{:S(2)}) %collective-permute-start.36) | collective-permute-done | bytes 131104 | tf_op jit(solution)/shard_map/ppermute | solution.py:302
  (119 shorter events, 34.1 us)
Async XLA Ops:
  7.5 16.9 %collective-permute-start.1 = (bf16[2,528,256]{2,1,0:T(8,128)(2,1)}, bf16[2,528,256]{2,1,0:T(8,128)(2,1)S(1)}, u32[]{:S(2)}, u32[]{:S(2)}) collective-permute-start(bf16[2,528,256]{2,1,0:T(8,128)(2,1)} %get-tuple-element.21), channel_id=1, source_target_pairs={{8,0},{16,8},{24,16},{32,24},{40,32},{48,40},{56,48},{64,56},{72,6... | collective-permute-start | bytes 1622024 | tf_op jit(solution)/shard_map/ppermute | solution.py:357
  8.8 15.7 %collective-permute-start = (bf16[2,528,256]{2,1,0:T(8,128)(2,1)}, bf16[2,528,256]{2,1,0:T(8,128)(2,1)S(1)}, u32[]{:S(2)}, u32[]{:S(2)}) collective-permute-start(bf16[2,528,256]{2,1,0:T(8,128)(2,1)} %get-tuple-element.22), channel_id=1, source_target_pairs={{0,8},{8,16},{16,24},{24,32},{32,40},{40,48},{48,56},{56,64},{64,7... | collective-permute-start | bytes 1622024 | tf_op jit(solution)/shard_map/ppermute | solution.py:356
  26.4 15.9 %collective-permute-start.9 = (bf16[512,512]{1,0:T(8,128)(2,1)S(1)}, bf16[512,512]{1,0:T(8,128)(2,1)S(1)}, u32[]{:S(2)}, u32[]{:S(2)}) collective-permute-start(bf16[512,512]{1,0:T(8,128)(2,1)S(1)} %get-tuple-element.25.refs_1_), channel_id=1, source_target_pairs={{0,8},{8,0},{1,9},{9,1},{2,10},{10,2},{3,11},{11,3},{4,12},{12,4},... | collective-permute-start | bytes 1572872 | tf_op jit(solution)/shard_map/ppermute | solution.py:329
  36.1 20.6 %collective-permute-start.10 = (bf16[512,512]{1,0:T(8,128)(2,1)}, bf16[512,512]{1,0:T(8,128)(2,1)}, u32[]{:S(2)}, u32[]{:S(2)}) collective-permute-start(bf16[512,512]{1,0:T(8,128)(2,1)} %collective-permute-done.8.refs_2_), channel_id=1, source_target_pairs={{0,8},{8,0},{1,9},{9,1},{2,10},{10,2},{3,11},{11,3},{4,12},{12,4},... | collective-permute-start | bytes 1572872 | tf_op jit(solution)/shard_map/ppermute | solution.py:329
  39.8 17.4 %collective-permute-start.14 = (bf16[512,512]{1,0:T(8,128)(2,1)}, bf16[512,512]{1,0:T(8,128)(2,1)}, u32[]{:S(2)}, u32[]{:S(2)}) collective-permute-start(bf16[512,512]{1,0:T(8,128)(2,1)} %collective-permute-done.8.refs_2_), channel_id=1, source_target_pairs={{0,2},{2,4},{4,6},{6,0},{1,3},{3,5},{5,7},{7,1},{8,10},{10,12},{12... | collective-permute-start | bytes 1572872 | tf_op jit(solution)/shard_map/ppermute | solution.py:323
  41.1 17.5 %collective-permute-start.11 = (bf16[512,512]{1,0:T(8,128)(2,1)}, bf16[512,512]{1,0:T(8,128)(2,1)S(1)}, u32[]{:S(2)}, u32[]{:S(2)}) collective-permute-start(bf16[512,512]{1,0:T(8,128)(2,1)} %collective-permute-done.8.refs_2_), channel_id=1, source_target_pairs={{2,0},{4,2},{6,4},{0,6},{3,1},{5,3},{7,5},{1,7},{10,8},{12,10},{14... | collective-permute-start | bytes 1572872 | tf_op jit(solution)/shard_map/ppermute | solution.py:322
  42.0 15.3 %collective-permute-start.12 = (bf16[256,512]{1,0:T(8,128)(2,1)S(1)}, bf16[256,512]{1,0:T(8,128)(2,1)S(1)}, u32[]{:S(2)}, u32[]{:S(2)}) collective-permute-start(bf16[256,512]{1,0:T(8,128)(2,1)S(1)} %slice.153), channel_id=1, source_target_pairs={{0,8},{8,0},{1,9},{9,1},{2,10},{10,2},{3,11},{11,3},{4,12},{12,4},... | collective-permute-start | bytes 786440 | tf_op jit(solution)/shard_map/ppermute | solution.py:330
  43.1 16.2 %collective-permute-start.15 = (bf16[512,512]{1,0:T(8,128)(2,1)}, bf16[512,512]{1,0:T(8,128)(2,1)S(1)}, u32[]{:S(2)}, u32[]{:S(2)}) collective-permute-start(bf16[512,512]{1,0:T(8,128)(2,1)} %collective-permute-done.3.refs_9_), channel_id=1, source_target_pairs={{0,8},{8,0},{1,9},{9,1},{2,10},{10,2},{3,11},{11,3},{4,12},{12,4},... | collective-permute-start | bytes 1572872 | tf_op jit(solution)/shard_map/ppermute | solution.py:331
  56.7 14.7 %collective-permute-start.4 = (bf16[512,512]{1,0:T(8,128)(2,1)S(1)}, bf16[512,512]{1,0:T(8,128)(2,1)S(1)}, u32[]{:S(2)}, u32[]{:S(2)}) collective-permute-start(bf16[512,512]{1,0:T(8,128)(2,1)S(1)} %get-tuple-element.30), channel_id=1, source_target_pairs={{0,1},{1,0},{2,3},{3,2},{4,5},{5,4},{6,7},{7,6},{8,9},{9,8},{10,11... | collective-permute-start | bytes 1572872 | tf_op jit(solution)/shard_map/ppermute | solution.py:394
  57.2 14.3 %collective-permute-start.17 = (bf16[512,512]{1,0:T(8,128)(2,1)S(1)}, bf16[512,512]{1,0:T(8,128)(2,1)S(1)}, u32[]{:S(2)}, u32[]{:S(2)}) collective-permute-start(bf16[512,512]{1,0:T(8,128)(2,1)S(1)} %get-tuple-element.29.refs_1_), channel_id=1, source_target_pairs={{0,2},{2,4},{4,6},{6,0},{1,3},{3,5},{5,7},{7,1},{8,10},{10,12},{12... | collective-permute-start | bytes 1572872 | tf_op jit(solution)/shard_map/ppermute | solution.py:323
  73.8 14.1 %collective-permute-start.18 = (bf16[512,512]{1,0:T(8,128)(2,1)S(1)}, bf16[512,512]{1,0:T(8,128)(2,1)S(1)}, u32[]{:S(2)}, u32[]{:S(2)}) collective-permute-start(bf16[512,512]{1,0:T(8,128)(2,1)S(1)} %collective-permute-done.4.refs_2_), channel_id=1, source_target_pairs={{2,0},{4,2},{6,4},{0,6},{3,1},{5,3},{7,5},{1,7},{10,8},{12,10},{14... | collective-permute-start | bytes 1572872 | tf_op jit(solution)/shard_map/ppermute | solution.py:322
  74.5 15.4 %collective-permute-start.6 = (bf16[512,512]{1,0:T(8,128)(2,1)S(1)}, bf16[512,512]{1,0:T(8,128)(2,1)}, u32[]{:S(2)}, u32[]{:S(2)}) collective-permute-start(bf16[512,512]{1,0:T(8,128)(2,1)S(1)} %collective-permute-done.4.refs_2_), channel_id=1, source_target_pairs={{0,8},{8,0},{1,9},{9,1},{2,10},{10,2},{3,11},{11,3},{4,12},{12,4},... | collective-permute-start | bytes 1572872 | tf_op jit(solution)/shard_map/ppermute | solution.py:329
  75.0 14.9 %collective-permute-start.22 = (bf16[512,512]{1,0:T(8,128)(2,1)S(1)}, bf16[512,512]{1,0:T(8,128)(2,1)}, u32[]{:S(2)}, u32[]{:S(2)}) collective-permute-start(bf16[512,512]{1,0:T(8,128)(2,1)S(1)} %collective-permute-done.17.refs_9_), channel_id=1, source_target_pairs={{0,8},{8,0},{1,9},{9,1},{2,10},{10,2},{3,11},{11,3},{4,12},{12,4},... | collective-permute-start | bytes 1572872 | tf_op jit(solution)/shard_map/ppermute | solution.py:331
  110.5 18.8 %collective-permute-start.24 = (f16[4,128,512]{2,1,0:T(8,128)(2,1)S(1)}, f16[4,128,512]{2,1,0:T(8,128)(2,1)S(1)}, u32[]{:S(2)}, u32[]{:S(2)}) collective-permute-start(f16[4,128,512]{2,1,0:T(8,128)(2,1)S(1)} %get-tuple-element.40), channel_id=1, source_target_pairs={{0,32},{32,64},{64,96},{96,0},{1,33},{33,65},{65,97},{97,1},{2,34}... | collective-permute-start | bytes 1572872 | tf_op jit(solution)/shard_map/ppermute | solution.py:312
  114.8 25.2 %collective-permute-start.26 = (f16[4,128,512]{2,1,0:T(8,128)(2,1)S(1)}, f16[4,128,512]{2,1,0:T(8,128)(2,1)S(1)}, u32[]{:S(2)}, u32[]{:S(2)}) collective-permute-start(f16[4,128,512]{2,1,0:T(8,128)(2,1)S(1)} %get-tuple-element.41), channel_id=1, source_target_pairs={{0,96},{32,0},{64,32},{96,64},{1,97},{33,1},{65,33},{97,65},{2,98}... | collective-permute-start | bytes 1572872 | tf_op jit(solution)/shard_map/ppermute | solution.py:312
  117.0 24.8 %collective-permute-start.25 = (f16[4,128,512]{2,1,0:T(8,128)(2,1)S(1)}, f16[4,128,512]{2,1,0:T(8,128)(2,1)S(1)}, u32[]{:S(2)}, u32[]{:S(2)}) collective-permute-start(f16[4,128,512]{2,1,0:T(8,128)(2,1)S(1)} %get-tuple-element.42), channel_id=1, source_target_pairs={{0,64},{32,96},{64,0},{96,32},{1,65},{33,97},{65,1},{97,33},{2,66}... | collective-permute-start | bytes 1572872 | tf_op jit(solution)/shard_map/ppermute | solution.py:312
  119.7 23.7 %collective-permute-start.31 = (f16[4,128,512]{2,1,0:T(8,128)(2,1)S(1)}, f16[4,128,512]{2,1,0:T(8,128)(2,1)S(1)}, u32[]{:S(2)}, u32[]{:S(2)}) collective-permute-start(f16[4,128,512]{2,1,0:T(8,128)(2,1)S(1)} %get-tuple-element.43), channel_id=1, source_target_pairs={{0,1},{1,16},{16,17},{17,0},{2,3},{3,18},{18,19},{19,2},{4,5},{5,2... | collective-permute-start | bytes 1572872 | tf_op jit(solution)/shard_map/ppermute | solution.py:312
  120.8 26.5 %collective-permute-start.33 = (f16[4,128,512]{2,1,0:T(8,128)(2,1)S(1)}, f16[4,128,512]{2,1,0:T(8,128)(2,1)S(1)}, u32[]{:S(2)}, u32[]{:S(2)}) collective-permute-start(f16[4,128,512]{2,1,0:T(8,128)(2,1)S(1)} %get-tuple-element.44), channel_id=1, source_target_pairs={{0,17},{1,0},{16,1},{17,16},{2,19},{3,2},{18,3},{19,18},{4,21},{5,... | collective-permute-start | bytes 1572872 | tf_op jit(solution)/shard_map/ppermute | solution.py:312
  129.3 18.0 %collective-permute-start.32 = (f16[4,128,512]{2,1,0:T(8,128)(2,1)S(1)}, f16[4,128,512]{2,1,0:T(8,128)(2,1)S(1)}, u32[]{:S(2)}, u32[]{:S(2)}) collective-permute-start(f16[4,128,512]{2,1,0:T(8,128)(2,1)S(1)} %get-tuple-element.45), channel_id=1, source_target_pairs={{0,16},{1,17},{16,0},{17,1},{2,18},{3,19},{18,2},{19,3},{4,20},{5,... | collective-permute-start | bytes 1572872 | tf_op jit(solution)/shard_map/ppermute | solution.py:312
  142.9 21.2 %collective-permute-start.30 = (f16[128,512]{1,0:T(8,128)(2,1)S(1)}, f16[128,512]{1,0:T(8,128)(2,1)S(1)}, u32[]{:S(2)}, u32[]{:S(2)}) collective-permute-start(f16[128,512]{1,0:T(8,128)(2,1)S(1)} %get-tuple-element.47), channel_id=1, source_target_pairs={{0,17},{1,0},{16,1},{17,16},{2,19},{3,2},{18,3},{19,18},{4,115},{5... | collective-permute-start | bytes 393224 | tf_op jit(solution)/shard_map/ppermute | solution.py:302
  143.5 20.6 %collective-permute-start.29 = (f16[128,512]{1,0:T(8,128)(2,1)S(1)}, f16[128,512]{1,0:T(8,128)(2,1)S(1)}, u32[]{:S(2)}, u32[]{:S(2)}) collective-permute-start(f16[128,512]{1,0:T(8,128)(2,1)S(1)} %get-tuple-element.48), channel_id=1, source_target_pairs={{0,16},{1,17},{16,0},{17,1},{2,18},{3,19},{18,2},{19,3},{4,114},{5... | collective-permute-start | bytes 393224 | tf_op jit(solution)/shard_map/ppermute | solution.py:302
  147.3 16.9 %collective-permute-start.28 = (f16[128,512]{1,0:T(8,128)(2,1)S(1)}, f16[128,512]{1,0:T(8,128)(2,1)S(1)}, u32[]{:S(2)}, u32[]{:S(2)}) collective-permute-start(f16[128,512]{1,0:T(8,128)(2,1)S(1)} %get-tuple-element.49), channel_id=1, source_target_pairs={{0,1},{1,16},{16,17},{17,0},{2,3},{3,18},{18,19},{19,2},{4,99},{5,... | collective-permute-start | bytes 393224 | tf_op jit(solution)/shard_map/ppermute | solution.py:302
  147.8 16.5 %collective-permute-start.34 = (f16[128,512]{1,0:T(8,128)(2,1)S(1)}, f16[128,512]{1,0:T(8,128)(2,1)S(1)}, u32[]{:S(2)}, u32[]{:S(2)}) collective-permute-start(f16[128,512]{1,0:T(8,128)(2,1)S(1)} %get-tuple-element.50), channel_id=1, source_target_pairs={{4,98},{5,99},{20,114},{21,115},{38,4},{39,5},{54,20},{55,21},{64,... | collective-permute-start | bytes 393224 | tf_op jit(solution)/shard_map/ppermute | solution.py:302
  148.4 18.2 %collective-permute-start.37 = (f16[128,512]{1,0:T(8,128)(2,1)S(1)}, f16[128,512]{1,0:T(8,128)(2,1)S(1)}, u32[]{:S(2)}, u32[]{:S(2)}) collective-permute-start(f16[128,512]{1,0:T(8,128)(2,1)S(1)} %get-tuple-element.51), channel_id=1, source_target_pairs={{0,96},{1,97},{16,112},{17,113},{2,64},{3,65},{18,80},{19,81},{4,1... | collective-permute-start | bytes 393224 | tf_op jit(solution)/shard_map/ppermute | solution.py:302
  (28 other events, 243.3 us)

commit v5 on v3

v5 whole, which is shorter than its diff:
```python
import jax
import jax.numpy as jnp
from jax import lax
from jax.experimental import pallas as pl
from jax.experimental.pallas import tpu as pltpu
from jax.sharding import Mesh, PartitionSpec as P

GRID = ("z", "xh", "core")
XS = ("xh", "xl")
HALF = jnp.float16
BF = jnp.bfloat16
VMEM_LIMIT = 16 * 1024 * 1024
LIFT = 1.0 / 256
SWAP = [(0, 1), (1, 0)]
INNER = 100 << 20
OUTER = 20 << 20


def params():
    return pltpu.CompilerParams(vmem_limit_bytes=VMEM_LIMIT)


def cost(flops, moved):
    return pl.CostEstimate(flops=flops, bytes_accessed=moved, transcendentals=0)


def edge_kernel(x_ref, c_ref, top_ref, bot_ref):
    i = pl.program_id(0)
    block, rows, _ = x_ref.shape
    at = pl.ds(pl.multiple_of(i * block, block), block)
    for out_ref, first, edge in ((top_ref, 0, 0), (bot_ref, rows - 2, rows - 1)):
        out_ref[0, at, :] = x_ref[:, first, :].astype(BF)
        out_ref[1, at, :] = x_ref[:, first + 1, :].astype(BF)

        @pl.when(i == 0)
        def _():
            rest = c_ref[:, edge, :]
            terms = []
            for _ in range(3):
                terms.append(rest.astype(BF).astype(jnp.float32))
                rest = rest - terms[-1]
            packed = jnp.concatenate(terms + [jnp.zeros_like(rest)], axis=0).astype(BF)
            last = out_ref.shape[1] - packed.shape[0]
            for k in range(2):
                out_ref[k, last:, :] = packed


def edges(field, courant):
    groups, rows, width = field.shape
    block = 64
    shape = jax.ShapeDtypeStruct((2, groups + 16, width), BF)
    spec = pl.BlockSpec(shape.shape, lambda i: (0, 0, 0))
    return pl.pallas_call(
        edge_kernel,
        grid=(groups // block,),
        in_specs=[
            pl.BlockSpec((block, rows, width), lambda i: (i, 0, 0)),
            pl.BlockSpec(courant.shape, lambda i: (0, 0, 0)),
        ],
        out_specs=[spec, spec],
        out_shape=[shape, shape],
        cost_estimate=cost(1000, 6 << 20),
        compiler_params=params(),
    )(field, courant)


def edge_weights(halo, groups):
    return jnp.sum(halo[0, groups:groups + 12].astype(jnp.float32).reshape(3, 4, 1, -1), axis=0)


def stepper(coef_ref, offset, delta, width):
    def step(r, south, center, north):
        east = pltpu.roll(center, width - 1, 1)
        west = pltpu.roll(center, 1, 1)
        at = r + offset
        c = [coef_ref[k, at:at + 1, :] for k in range(5)]
        pulse = jnp.where(delta == r * width, 1.0, 0.0)
        return c[4] * center + c[0] * north + c[1] * south + c[2] * east + c[3] * west + pulse

    return step


def offsets(det_ref, at, first_cell, width):
    return det_ref[at, :] - first_cell - lax.broadcasted_iota(jnp.int32, (16, width), 1)


def put(keep_ref, send_ref, at, p, own_first, low, high):
    width = low.shape[1]
    cols = pl.ds(p * width, width)
    keep_ref[at, cols] = jnp.where(own_first, low, high).astype(BF)
    send_ref[at, cols] = jnp.where(own_first, high, low).astype(BF)


def inner_kernel(info, x_ref, coef_ref, emis_ref, det_ref, adv_ref, keep_ref, send_ref):
    block, rows, width = x_ref.shape
    own_first = info[1] == 0

    def group(g, carry):
        at = pl.ds(pl.multiple_of(g * 16, 16), 16)
        step = stepper(coef_ref, 0, offsets(det_ref, at, info[2], width), width)
        v = jnp.swapaxes(x_ref[at], 0, 1)
        first = {r: step(r, v[r - 1], v[r], v[r + 1]) for r in range(1, rows - 1)}
        out = {r: step(r, first[r - 1], first[r], first[r + 1]) for r in range(2, rows - 2)}
        tile = jnp.stack([out[min(max(r, 2), rows - 3)] for r in range(rows)])
        adv_ref[at] = jnp.swapaxes(tile, 0, 1)
        prints = {r: out[r] * emis_ref[r:r + 1, :] for r in out}
        for p in range(2):
            put(keep_ref, send_ref, at, p, own_first, prints[p + 2], prints[p + 4])
        return carry

    lax.fori_loop(0, block // 16, group, 0, unroll=2)


def outer_kernel(info, x_ref, up_ref, down_ref, coef_ref, emis_ref, det_ref, mid_ref, adv_ref, keep_ref, send_ref):
    block, rows, width = x_ref.shape
    own_first = info[1] == 0

    def group(g, carry):
        at = pl.ds(pl.multiple_of(g * 16, 16), 16)
        step = stepper(coef_ref, 1, offsets(det_ref, at, info[2], width), width)
        tile = jnp.swapaxes(x_ref[at], 0, 1)
        v = {r: tile[r] for r in range(rows)}
        for r in range(2):
            v[r - 2] = up_ref[r, at, :].astype(jnp.float32)
            v[r + rows] = down_ref[r, at, :].astype(jnp.float32)
        first = {r: step(r, v[r - 1], v[r], v[r + 1]) for r in (-1, 0, 1, 2, 5, 6, 7, 8)}
        out = {r: step(r, first[r - 1], first[r], first[r + 1]) for r in (0, 1, 6, 7)}
        tile = jnp.stack([out[r if r in out else (1 if r < 4 else 6)] for r in range(rows)])
        tile = jnp.swapaxes(tile, 0, 1)
        row = lax.broadcasted_iota(jnp.int32, tile.shape, 1)
        adv_ref[at] = jnp.where((row >= 2) & (row < 6), mid_ref[at], tile)
        prints = {r: out[r] * emis_ref[r:r + 1, :] for r in out}
        for p in range(2):
            put(keep_ref, send_ref, at, p, own_first, prints[p], prints[p + 6])
        return carry

    lax.fori_loop(0, block // 16, group, 0, unroll=2)


def stencil(kernel, info, field, halos, coef, emis, det, mid, work):
    groups, rows, width = field.shape
    block = 64
    count = groups // block
    half = count // 2
    cells = 2 * width

    def turned(i, info):
        return lax.rem(i + info[0] * half, count)

    fields = pl.BlockSpec((block, rows, width), lambda i, info: (turned(i, info), 0, 0))
    halo = pl.BlockSpec((2, block, width), lambda i, info: (0, turned(i, info), 0))
    prints = pl.BlockSpec((block, cells), lambda i, info: (i, 0))
    print_shape = jax.ShapeDtypeStruct((groups, cells), BF)
    operands = [field, *halos, coef, emis, det, *mid]
    return pl.pallas_call(
        kernel,
        grid_spec=pltpu.PrefetchScalarGridSpec(
            num_scalar_prefetch=1,
            grid=(count,),
            in_specs=[
                fields,
                *([halo] * len(halos)),
                pl.BlockSpec(coef.shape, lambda i, info: (0, 0, 0)),
                pl.BlockSpec((rows, width), lambda i, info: (0, 0)),
                pl.BlockSpec((block, 1), lambda i, info: (turned(i, info), 0)),
                *([fields] * len(mid)),
            ],
            out_specs=[fields, prints, prints],
        ),
        out_shape=[jax.ShapeDtypeStruct(field.shape, jnp.float32), print_shape, print_shape],
        input_output_aliases={len(operands): 0} if mid else {},
        cost_estimate=cost(1000, work),
        compiler_params=params(),
    )(info, *operands)


NT = (((1,), (1,)), ((), ()))


def dot(left, right):
    return lax.dot_general(left, right, NT, preferred_element_type=jnp.float32)


def gram_kernel(info, *refs):
    *refs, first_ref, second_ref, held, sem = refs
    outs = first_ref, second_ref
    own, own_s, nxt, nxt_s, last, last_s = (
        [(refs[2 * k + i], refs[2 * k + i + 12]) for i in range(2)] for k in range(6)
    )
    core, xl, y, xpos, z = info[0], info[1], info[3], info[4], info[5]
    rows = nxt_s[0][0].shape[0]
    half = own[0][0].shape[1]
    part = rows // 2
    sources = []
    for tile, sibling, start, start_s in (
        (nxt, nxt_s, 0, 0), (own, own_s, 0, rows), (last, last_s, 0, rows),
        (own, own_s, rows, 0), (last, last_s, rows, 0),
    ):
        sources += [(tile[i], sibling[i], start, start_s) for i in range(2)]
    copies = []
    for at, (tile, sibling, start, start_s) in enumerate(sources):
        for k in range(2):
            for side, (ref, first) in enumerate(((tile[k], start), (sibling[k], start_s))):
                copies.append(pltpu.make_async_copy(
                    ref.at[pl.ds(first, rows), :],
                    held.at[pl.ds(at * rows, rows), pl.ds((2 * k + side) * half, half)],
                    sem.at[len(copies)],
                ))
    for copy in copies:
        copy.start()
    for copy in copies:
        copy.wait()

    for j in range(2):
        for m in range(2):
            here, far = 2 + 4 * m + j, 4 + 4 * m + j
            here = dot(held[:6 * rows, :], held[here * rows:(here + 1) * rows, :])
            far = dot(held[:2 * rows, :], held[far * rows:(far + 1) * rows, :])
            cols = pl.ds(pl.multiple_of(lax.rem(core + m, 2) * rows, rows), rows)
            values = [(e, i, here[(2 * k + i) * rows:(2 * k + i + 1) * rows])
                      for k, e in enumerate((1, 0, 3)) for i in range(2)]
            values += [(2, i, far[i * rows:(i + 1) * rows]) for i in range(2)]
            for e, i, value in values:
                at_z = lax.rem(y + e + 4 - z, 4)
                at_x = lax.rem(lax.rem(i + xl, 2) * 2 + lax.rem(j + xl, 2) + 4 - xpos, 4)
                for upper, slot in enumerate((at_z * 4 + at_x, at_x * 4 + at_z)):
                    outs[upper][slot, :, cols] = value[upper * part:(upper + 1) * part]


def partial_gram(info, operands):
    rows, half = operands[0].shape
    rows = rows // 2
    whole = pl.BlockSpec(memory_space=pltpu.VMEM)
    shape = jax.ShapeDtypeStruct((16, rows // 2, 2 * rows), jnp.float32)
    return pl.pallas_call(
        gram_kernel,
        in_specs=[pl.BlockSpec(memory_space=pltpu.SMEM)]
        + [pl.BlockSpec(memory_space=pl.ANY)] * len(operands),
        out_specs=[whole, whole],
        out_shape=[shape, shape],
        scratch_shapes=[
            pltpu.VMEM((10 * rows, 4 * half), BF), pltpu.SemaphoreType.DMA((40,))
        ],
        cost_estimate=cost(1000, 8 << 20),
        compiler_params=pltpu.CompilerParams(vmem_limit_bytes=54 << 20),
    )(info, *operands)


def place(z, xh, y, xl):
    return ((z % 4 * 2 + xh) * 4 + y % 4) * 2 + xl


def home(z, y):
    return (z - 1, y - 1) if (z - y) % 4 == 2 else (z, y)


def to_homes(pieces, steps, axes=("z", "xh", "y", "xl")):
    total = 0.0
    stays = lax.rem(lax.axis_index("y") + 2, 4) != lax.axis_index("z")
    for d in range(steps):
        pairs = []
        for z in range(4):
            for y in range(4):
                target = home(z + d, y)
                if d or target != (z, y):
                    pairs += [
                        (place(z, xh, y, xl), place(target[0], xh, target[1], xl))
                        for xh in range(2) for xl in range(2)
                    ]
        came = lax.ppermute(pieces[d], axes, pairs)
        if d == 0:
            came = jnp.where(stays, pieces[0], came)
        total = total + came.astype(jnp.float32)
    return total


def to_four(pieces, axis):
    total = pieces[0].astype(jnp.float32)
    for d in (1, 2, 3):
        came = lax.ppermute(pieces[d], axis, [(i, (i + d) % 4) for i in range(4)])
        total = total + came.astype(jnp.float32)
    return total


def after(value, *others):
    return lax.optimization_barrier((value, others))[0]


def along_y(own):
    nxt = lax.ppermute(own, "y", [((i + 1) % 4, i) for i in range(4)])
    last = lax.ppermute(own, "y", [(i, (i + 1) % 4) for i in range(4)])
    return nxt, last


def siblings(own, nxt, last):
    part = own.shape[0] // 2
    own_s = lax.ppermute(own, "core", SWAP)
    nxt_s = lax.ppermute(nxt[part:], "core", SWAP)
    last_s = lax.ppermute(last, "core", SWAP)
    return own, own_s, nxt, nxt_s, last, last_s


def gram_operands(keep, keep_y, other, other_y):
    return [
        array for pair in zip(siblings(keep, *keep_y), siblings(other, *other_y)) for array in pair
    ]


def body(adjoint, courant, detector, sources, emission):
    groups, rows, width = adjoint.shape
    core = lax.axis_index("core")
    xl = lax.axis_index("xl")
    y = lax.axis_index("y")
    z = lax.axis_index("z")
    tile = lax.axis_index(GRID)
    first_cell = tile * rows * width
    xpos = lax.axis_index(XS)
    info = jnp.stack([core, xl, first_cell, y, xpos, z]).astype(jnp.int32)
    count = lax.axis_size(GRID)
    forward = [(i, i + 1) for i in range(count - 1)]
    backward = [(i + 1, i) for i in range(count - 1)]

    top, bottom = edges(adjoint, courant)
    up = lax.ppermute(bottom, GRID, forward)
    down = lax.ppermute(top, GRID, backward)
    columns = jnp.arange(width)

    def weights(c):
        return jnp.stack([
            c[0],
            c[1],
            jnp.where(columns == width - 1, 0.0, c[2]),
            jnp.where(columns == 0, 0.0, c[3]),
            1.0 - (c[0] + c[1] + c[2] + c[3]),
        ])

    local = sources - first_cell
    by_row = jnp.where(
        (local // width)[None, :] == jnp.arange(rows)[:, None], emission[None, :], 0.0
    )
    by_col = ((local % width)[:, None] == columns[None, :]).astype(jnp.float32)
    emis = jnp.dot(by_row, by_col, precision=lax.Precision.HIGHEST)
    det = detector[:, None]

    mid, keep, send = stencil(
        inner_kernel, after(info, top, bottom), adjoint, [], weights(courant), emis, det, [], INNER
    )
    other = lax.ppermute(send, "xl", SWAP)
    keep_y = along_y(after(keep, up, down))
    other_y = along_y(after(other, keep_y))
    operands = gram_operands(keep, keep_y, other, other_y)

    extended = jnp.concatenate(
        [edge_weights(up, groups), courant, edge_weights(down, groups)], axis=1
    )
    field, keep, send = stencil(
        outer_kernel, after(info, keep_y), adjoint, [up, down], weights(extended), emis, det,
        [mid], OUTER
    )
    other = lax.ppermute(send, "xl", SWAP)
    keep_y = along_y(after(keep, other_y))
    other_y = along_y(after(other, keep_y))
    operands += gram_operands(keep, keep_y, other, other_y)
    totals = partial_gram(info, operands)

    def packed(total):
        return (total * LIFT).astype(HALF).reshape(4, 4, groups // 4, groups)

    along_x, along_z = packed(totals[1]), packed(totals[0])
    along_x = (to_four(along_x, XS) * 0.25).astype(HALF)
    along_z = (to_homes(along_z, 4) * 0.25).astype(HALF)
    along_z = to_four(along_z, XS) * 0.25
    along_x = (to_four(along_x, "z") * 0.25).astype(HALF)
    summed = jnp.concatenate([along_z, to_homes(along_x[None], 1)], axis=0)
    total_sources = sources.shape[0] * count
    return field, summed * jnp.float32(16.0 / (LIFT * total_sources))


def solution(mesh):
    fine = Mesh(mesh.devices.reshape(4, 2, 2, 4, 2), ("z", "xh", "core", "y", "xl"))
    rec = ("y", "xl")
    in_specs = (P(rec, GRID, None), P(None, GRID, None), P(rec), P(GRID), P(GRID))
    out_specs = (P(rec, GRID, None), P(GRID, rec))
    return jax.shard_map(body, mesh=fine, in_specs=in_specs, out_specs=out_specs, check_vma=False)
```

time: 171 us -> 182 us (1.064)
  Pallas kernels: 31.2 us -> 37.1 us
  waiting for transfers between devices: 75.9 us -> 80.9 us
  local copies, waits for them, and re-layouts: 7.1 us -> 11 us
  starting transfers between devices: 47 us -> 44.8 us
  other arithmetic: 7.56 us -> 5.5 us
    ppermute x6 -> x9, waiting for transfers between devices: 26.7 us -> 11.1 us  [to_four(): came = lax.ppermute(pieces[d], axis, [(i, (i + d) % 4) for i in range(4)])]
    ppermute x3 -> x5, starting transfers between devices: 5.74 us -> 18.2 us  [to_homes(): came = lax.ppermute(pieces[d], axes, pairs)]
    ppermute x3 -> x5, waiting for transfers between devices: 15.1 us -> 26.7 us  [to_homes(): came = lax.ppermute(pieces[d], axes, pairs)]
    all_to_all x2 -> x0, starting transfers between devices: 9.77 us -> none  [the longest x1 4.96 us: body(): along_z = lax.all_to_all(along_z, 'z', 0, 0, tiled=True)]
    ppermute x2, waiting for transfers between devices: 13.7 us -> 21.4 us  [body(): other = lax.ppermute(send, 'xl', SWAP)]
    pallas_call x2 -> x1, Pallas kernels: 10.7 us -> 17.3 us  [partial_gram(): pl.pallas_call(gram_kernel, in_specs=[pl.BlockSpec(memory_space=pltpu.SME...]
    ppermute x1, starting transfers between devices: 6.05 us -> 3.92 us  [body(): down = lax.ppermute(top, GRID, backward)]
    unnamed x14 -> x52, local copies, waits for them, and re-layouts: 6.35 us -> 8.2 us
  transfers between devices with their start and end apart: 35 -> 38, of which waited for: 19 -> 20; matrix products, arithmetic and copies ran while one was open for 3% -> 3% of each run, Pallas kernels for 14% -> 10%
where the time goes in v5:
time: 182 us; the launch traced here: 181 us
  waiting for transfers between devices  80.9 us (44%)
  starting transfers between devices  44.8 us (25%)
  Pallas kernels  37.1 us (20%)
  local copies, waits for them, and re-layouts  11 us (6%)
  other arithmetic  5.5 us (3%)
    ppermute x5, waiting for transfers between devices, to_homes(): came = lax.ppermute(pieces[d], axes, pairs)  26.7 us
    ppermute x2, waiting for transfers between devices, body(): other = lax.ppermute(send, 'xl', SWAP)  21.4 us
    ppermute x5, starting transfers between devices, to_homes(): came = lax.ppermute(pieces[d], axes, pairs)  18.2 us
    pallas_call x2, Pallas kernels, stencil(): pl.pallas_call(kernel, grid_spec=pltpu.PrefetchScalarGridSpec(num_scalar_...  17.5 us
    pallas_call x1, Pallas kernels, partial_gram(): pl.pallas_call(gram_kernel, in_specs=[pl.BlockSpec(memory_space=pltpu.SME...  17.3 us
    ppermute x4, waiting for transfers between devices, along_y(): last = lax.ppermute(own, 'y', [(i, (i + 1) % 4) for i in range(4)])  12.9 us
    ppermute x9, waiting for transfers between devices, to_four(): came = lax.ppermute(pieces[d], axis, [(i, (i + d) % 4) for i in range(4)])  11.1 us
    ppermute x9, starting transfers between devices, to_four(): came = lax.ppermute(pieces[d], axis, [(i, (i + d) % 4) for i in range(4)])  9.38 us
  transfers between devices with their start and end apart: 38, of which 20 were waited for; matrix products, arithmetic and copies ran while one was open for 3% of the time, Pallas kernels for 10%

profile of v5, /device:TPU:56, one launch (start us, length us, event | category | flops | bytes accessed | tf_op | source)
XLA Modules:
  0.0 181.2 jit_solution(17467184508840446682)
XLA Ops:
  0.6 2.2 %copy-done = f32[512,8,256]{2,1,0:T(8,128)S(1)} copy-done((f32[512,8,256]{2,1,0:T(8,128)S(1)}, f32[512,8,256]{2,1,0:T(8,128)}, u32[]{:S(2)}) %copy-start) | copy-done | bytes 4194328
  3.6 2.3 %shard_map.68 = (bf16[2,528,256]{2,1,0:T(8,128)(2,1)S(1)}, bf16[2,528,256]{2,1,0:T(8,128)(2,1)S(1)}) custom-call(f32[512,8,256]{2,1,0:T(8,128)S(1)} %copy-done, f32[4,8,256]{2,1,0:T(8,128)S(1)} %copy-done.5), custom_call_target="tpu_custom_call" | custom-call | flops 1000 | bytes 6291456 | tf_op jit(solution)/shard_map/pallas_call | solution.py:53
  5.9 3.9 %collective-permute-start.1 = (bf16[2,528,256]{2,1,0:T(8,128)(2,1)S(1)}, bf16[2,528,256]{2,1,0:T(8,128)(2,1)S(1)}, u32[]{:S(2)}, u32[]{:S(2)}) collective-permute-start(bf16[2,528,256]{2,1,0:T(8,128)(2,1)S(1)} %get-tuple-element.18), channel_id=1, source_target_pairs={{8,0},{16,8},{24,16},{32,24},{40,32},{48,40},{56,48},{64,56},{72,6... | collective-permute-start | bytes 1622024 | tf_op jit(solution)/shard_map/ppermute | solution.py:325
  12.9 2.2 %copy-done.1 = f32[512,8,256]{2,1,0:T(8,128)S(1)} copy-done((f32[512,8,256]{2,1,0:T(8,128)S(1)}, f32[512,8,256]{2,1,0:T(8,128)}, u32[]{:S(2)}) %copy-start.1) | copy-done | bytes 4194328
  15.1 7.3 %shard_map.69 = (f32[512,8,256]{2,1,0:T(8,128)}, bf16[512,512]{1,0:T(8,128)(2,1)S(1)}, bf16[512,512]{1,0:T(8,128)(2,1)S(1)}) custom-call(s32[6]{0:T(128)S(1)} %stack.39.info, f32[512,8,256]{2,1,0:T(8,128)S(1)} %copy-done.1, f32[5,8,256]{2,1,0:T(8,128)S(1)} %pad_maximum_fusion.2.coef_ref, f32[8,256]{1,0:T(8,128)S(1)} %fusion.emis_ref, s32[512,1]{1,0:T(8,128)S(1)} %copy.8.det_ref), custom_call_target="tpu_custom_call" | custom-call | flops 1000 | bytes 104857600 | tf_op jit(solution)/shard_map/pallas_call | solution.py:155
  25.5 11.7 %collective-permute-done.4.refs_1_ = bf16[512,512]{1,0:T(8,128)(2,1)} collective-permute-done((bf16[512,512]{1,0:T(8,128)(2,1)S(1)}, bf16[512,512]{1,0:T(8,128)(2,1)}, u32[]{:S(2)}, u32[]{:S(2)}) %collective-permute-start.4) | collective-permute-done | bytes 524320 | tf_op jit(solution)/shard_map/ppermute | solution.py:348
  41.8 2.2 %copy-done.2 = f32[512,8,256]{2,1,0:T(8,128)S(1)} copy-done((f32[512,8,256]{2,1,0:T(8,128)S(1)}, f32[512,8,256]{2,1,0:T(8,128)}, u32[]{:S(2)}) %copy-start.2) | copy-done | bytes 4194328
  44.0 10.2 %shard_map.70 = (f32[512,8,256]{2,1,0:T(8,128)}, bf16[512,512]{1,0:T(8,128)(2,1)S(1)}, bf16[512,512]{1,0:T(8,128)(2,1)S(1)}) custom-call(s32[6]{0:T(128)S(1)} %stack.39.info, f32[512,8,256]{2,1,0:T(8,128)S(1)} %copy-done.2, bf16[2,528,256]{2,1,0:T(8,128)(2,1)S(1)} %collective-permute-done.up_ref, ...), custom_call_target="tpu_custom_call", output_to_operand_aliasing={{0}: (7, {})} | custom-call | flops 1000 | bytes 20971520 | tf_op jit(solution)/shard_map/pallas_call | solution.py:155
  57.9 9.7 %collective-permute-done.13.refs_13_ = bf16[512,512]{1,0:T(8,128)(2,1)S(1)} collective-permute-done((bf16[512,512]{1,0:T(8,128)(2,1)S(1)}, bf16[512,512]{1,0:T(8,128)(2,1)S(1)}, u32[]{:S(2)}, u32[]{:S(2)}) %collective-permute-start.13) | collective-permute-done | bytes 524320 | tf_op jit(solution)/shard_map/ppermute | solution.py:360
  68.3 2.7 %collective-permute-done.16.refs_16_ = bf16[512,512]{1,0:T(8,128)(2,1)S(1)} collective-permute-done((bf16[512,512]{1,0:T(8,128)(2,1)S(1)}, bf16[512,512]{1,0:T(8,128)(2,1)S(1)}, u32[]{:S(2)}, u32[]{:S(2)}) %collective-permute-start.16) | collective-permute-done | bytes 524320 | tf_op jit(solution)/shard_map/ppermute | solution.py:290
  73.9 11.4 %collective-permute-done.21.refs_21_ = bf16[512,512]{1,0:T(8,128)(2,1)S(1)} collective-permute-done((bf16[512,512]{1,0:T(8,128)(2,1)S(1)}, bf16[512,512]{1,0:T(8,128)(2,1)S(1)}, u32[]{:S(2)}, u32[]{:S(2)}) %collective-permute-start.21) | collective-permute-done | bytes 524320 | tf_op jit(solution)/shard_map/ppermute | solution.py:291
  92.1 17.3 %shard_map.71 = (f32[16,128,512]{2,1,0:T(8,128)}, f32[16,128,512]{2,1,0:T(8,128)}) custom-call(s32[6]{0:T(128)} %copy-done.7, bf16[512,512]{1,0:T(8,128)(2,1)} %copy-done.3, bf16[512,512]{1,0:T(8,128)(2,1)} %collective-permute-done.4.refs_1_, bf16[512,512]{1,0:T(8,128)(2,1)} %copy-done.16, bf16[512,512]{1,0:T(8,128)(2,1)} %copy-done.17, ...), custom_call_target="tpu_custom_call" | custom-call | flops 1000 | bytes 8388608 | tf_op jit(solution)/shard_map/pallas_call | solution.py:235
  109.3 3.0 %multiply_convert_fusion = f16[16,128,512]{2,1,0:T(8,128)(2,1)S(1)} fusion(f32[16,128,512]{2,1,0:T(8,128)} %get-tuple-element.33), kind=kLoop, calls=%fused_computation | loop fusion | flops 2097152 | bytes 6291456 | tf_op jit(solution)/shard_map/convert_element_type | solution.py:367
  116.0 2.1 %collective-permute-start.32 = (f16[4,128,512]{2,1,0:T(8,128)(2,1)S(1)}, f16[4,128,512]{2,1,0:T(8,128)(2,1)S(1)}, u32[]{:S(2)}, u32[]{:S(2)}) collective-permute-start(f16[4,128,512]{2,1,0:T(8,128)(2,1)S(1)} %get-tuple-element.40), channel_id=1, source_target_pairs={{0,16},{1,17},{16,0},{17,1},{2,18},{3,19},{18,2},{19,3},{4,20},{5,... | collective-permute-start | bytes 1572872 | tf_op jit(solution)/shard_map/ppermute | solution.py:280
  121.3 6.6 %collective-permute-done.31 = f16[4,128,512]{2,1,0:T(8,128)(2,1)S(1)} collective-permute-done((f16[4,128,512]{2,1,0:T(8,128)(2,1)S(1)}, f16[4,128,512]{2,1,0:T(8,128)(2,1)S(1)}, u32[]{:S(2)}, u32[]{:S(2)}) %collective-permute-start.31) | collective-permute-done | bytes 524320 | tf_op jit(solution)/shard_map/ppermute | solution.py:280
  127.9 14.2 %collective-permute-start.26 = (f16[4,128,512]{2,1,0:T(8,128)(2,1)S(1)}, f16[4,128,512]{2,1,0:T(8,128)(2,1)S(1)}, u32[]{:S(2)}, u32[]{:S(2)}) collective-permute-start(f16[4,128,512]{2,1,0:T(8,128)(2,1)S(1)} %get-tuple-element.36), channel_id=1, source_target_pairs={{0,38},{1,39},{16,54},{17,55},{2,66},{3,67},{18,82},{19,83},{4,68}... | collective-permute-start | bytes 1572872 | tf_op jit(solution)/shard_map/ppermute | solution.py:270
  143.2 2.4 %collective-permute-done.24 = f16[4,128,512]{2,1,0:T(8,128)(2,1)S(1)} collective-permute-done((f16[4,128,512]{2,1,0:T(8,128)(2,1)S(1)}, f16[4,128,512]{2,1,0:T(8,128)(2,1)S(1)}, u32[]{:S(2)}, u32[]{:S(2)}) %collective-permute-start.24) | collective-permute-done | bytes 524320 | tf_op jit(solution)/shard_map/ppermute | solution.py:270
  145.7 2.1 %collective-permute-done.27 = f16[4,128,512]{2,1,0:T(8,128)(2,1)S(1)} collective-permute-done((f16[4,128,512]{2,1,0:T(8,128)(2,1)S(1)}, f16[4,128,512]{2,1,0:T(8,128)(2,1)S(1)}, u32[]{:S(2)}, u32[]{:S(2)}) %collective-permute-start.27) | collective-permute-done | bytes 524320 | tf_op jit(solution)/shard_map/ppermute | solution.py:270
  147.7 6.9 %collective-permute-done.26 = f16[4,128,512]{2,1,0:T(8,128)(2,1)S(1)} collective-permute-done((f16[4,128,512]{2,1,0:T(8,128)(2,1)S(1)}, f16[4,128,512]{2,1,0:T(8,128)(2,1)S(1)}, u32[]{:S(2)}, u32[]{:S(2)}) %collective-permute-start.26) | collective-permute-done | bytes 524320 | tf_op jit(solution)/shard_map/ppermute | solution.py:270
  154.6 12.8 %collective-permute-done.25 = f16[4,128,512]{2,1,0:T(8,128)(2,1)S(1)} collective-permute-done((f16[4,128,512]{2,1,0:T(8,128)(2,1)S(1)}, f16[4,128,512]{2,1,0:T(8,128)(2,1)S(1)}, u32[]{:S(2)}, u32[]{:S(2)}) %collective-permute-start.25) | collective-permute-done | bytes 524320 | tf_op jit(solution)/shard_map/ppermute | solution.py:270
  168.0 3.2 %collective-permute-start.30 = (f16[128,512]{1,0:T(8,128)(2,1)S(1)}, f16[128,512]{1,0:T(8,128)(2,1)S(1)}, u32[]{:S(2)}, u32[]{:S(2)}) collective-permute-start(f16[128,512]{1,0:T(8,128)(2,1)S(1)} %get-tuple-element.42), channel_id=1, source_target_pairs={{0,17},{1,0},{16,1},{17,16},{2,19},{3,2},{18,3},{19,18},{4,21},{5,... | collective-permute-start | bytes 393224 | tf_op jit(solution)/shard_map/ppermute | solution.py:280
  173.3 2.3 %collective-permute-done.28 = f16[128,512]{1,0:T(8,128)(2,1)S(1)} collective-permute-done((f16[128,512]{1,0:T(8,128)(2,1)S(1)}, f16[128,512]{1,0:T(8,128)(2,1)S(1)}, u32[]{:S(2)}, u32[]{:S(2)}) %collective-permute-start.28) | collective-permute-done | bytes 131104 | tf_op jit(solution)/shard_map/ppermute | solution.py:280
  175.6 2.1 %collective-permute-done.29 = f16[128,512]{1,0:T(8,128)(2,1)S(1)} collective-permute-done((f16[128,512]{1,0:T(8,128)(2,1)S(1)}, f16[128,512]{1,0:T(8,128)(2,1)S(1)}, u32[]{:S(2)}, u32[]{:S(2)}) %collective-permute-start.29) | collective-permute-done | bytes 131104 | tf_op jit(solution)/shard_map/ppermute | solution.py:280
  177.8 2.5 %collective-permute-done.37 = f16[128,512]{1,0:T(8,128)(2,1)S(1)} collective-permute-done((f16[128,512]{1,0:T(8,128)(2,1)S(1)}, f16[128,512]{1,0:T(8,128)(2,1)S(1)}, u32[]{:S(2)}, u32[]{:S(2)}) %collective-permute-start.37) | collective-permute-done | bytes 131104 | tf_op jit(solution)/shard_map/ppermute | solution.py:270
  (145 shorter events, 36.7 us)
Async XLA Ops:
  5.9 17.2 %collective-permute-start.1 = (bf16[2,528,256]{2,1,0:T(8,128)(2,1)S(1)}, bf16[2,528,256]{2,1,0:T(8,128)(2,1)S(1)}, u32[]{:S(2)}, u32[]{:S(2)}) collective-permute-start(bf16[2,528,256]{2,1,0:T(8,128)(2,1)S(1)} %get-tuple-element.18), channel_id=1, source_target_pairs={{8,0},{16,8},{24,16},{32,24},{40,32},{48,40},{56,48},{64,56},{72,6... | collective-permute-start | bytes 1622024 | tf_op jit(solution)/shard_map/ppermute | solution.py:325
  9.8 13.7 %collective-permute-start = (bf16[2,528,256]{2,1,0:T(8,128)(2,1)S(1)}, bf16[2,528,256]{2,1,0:T(8,128)(2,1)S(1)}, u32[]{:S(2)}, u32[]{:S(2)}) collective-permute-start(bf16[2,528,256]{2,1,0:T(8,128)(2,1)S(1)} %get-tuple-element.19), channel_id=1, source_target_pairs={{0,8},{8,16},{16,24},{24,32},{32,40},{40,48},{48,56},{56,64},{64,7... | collective-permute-start | bytes 1622024 | tf_op jit(solution)/shard_map/ppermute | solution.py:324
  22.4 14.7 %collective-permute-start.4 = (bf16[512,512]{1,0:T(8,128)(2,1)S(1)}, bf16[512,512]{1,0:T(8,128)(2,1)}, u32[]{:S(2)}, u32[]{:S(2)}) collective-permute-start(bf16[512,512]{1,0:T(8,128)(2,1)S(1)} %get-tuple-element.26), channel_id=1, source_target_pairs={{0,1},{1,0},{2,3},{3,2},{4,5},{5,4},{6,7},{7,6},{8,9},{9,8},{10,11... | collective-permute-start | bytes 1572872 | tf_op jit(solution)/shard_map/ppermute | solution.py:348
  23.5 14.5 %collective-permute-start.3 = (bf16[512,512]{1,0:T(8,128)(2,1)S(1)}, bf16[512,512]{1,0:T(8,128)(2,1)S(1)}, u32[]{:S(2)}, u32[]{:S(2)}) collective-permute-start(bf16[512,512]{1,0:T(8,128)(2,1)S(1)} %get-tuple-element.22.refs_0_), channel_id=1, source_target_pairs={{0,2},{2,4},{4,6},{6,0},{1,3},{3,5},{5,7},{7,1},{8,10},{10,12},{12... | collective-permute-start | bytes 1572872 | tf_op jit(solution)/shard_map/ppermute | solution.py:291
  23.7 15.9 %collective-permute-start.2 = (bf16[512,512]{1,0:T(8,128)(2,1)S(1)}, bf16[512,512]{1,0:T(8,128)(2,1)S(1)}, u32[]{:S(2)}, u32[]{:S(2)}) collective-permute-start(bf16[512,512]{1,0:T(8,128)(2,1)S(1)} %get-tuple-element.22.refs_0_), channel_id=1, source_target_pairs={{2,0},{4,2},{6,4},{0,6},{3,1},{5,3},{7,5},{1,7},{10,8},{12,10},{14... | collective-permute-start | bytes 1572872 | tf_op jit(solution)/shard_map/ppermute | solution.py:290
  39.6 15.5 %collective-permute-start.10 = (bf16[512,512]{1,0:T(8,128)(2,1)}, bf16[512,512]{1,0:T(8,128)(2,1)}, u32[]{:S(2)}, u32[]{:S(2)}) collective-permute-start(bf16[512,512]{1,0:T(8,128)(2,1)} %collective-permute-done.4.refs_1_), channel_id=1, source_target_pairs={{0,2},{2,4},{4,6},{6,0},{1,3},{3,5},{5,7},{7,1},{8,10},{10,12},{12... | collective-permute-start | bytes 1572872 | tf_op jit(solution)/shard_map/ppermute | solution.py:291
  40.2 15.1 %collective-permute-start.7 = (bf16[512,512]{1,0:T(8,128)(2,1)}, bf16[512,512]{1,0:T(8,128)(2,1)S(1)}, u32[]{:S(2)}, u32[]{:S(2)}) collective-permute-start(bf16[512,512]{1,0:T(8,128)(2,1)} %collective-permute-done.4.refs_1_), channel_id=1, source_target_pairs={{2,0},{4,2},{6,4},{0,6},{3,1},{5,3},{7,5},{1,7},{10,8},{12,10},{14... | collective-permute-start | bytes 1572872 | tf_op jit(solution)/shard_map/ppermute | solution.py:290
  57.3 13.6 %collective-permute-start.5 = (bf16[512,512]{1,0:T(8,128)(2,1)S(1)}, bf16[512,512]{1,0:T(8,128)(2,1)S(1)}, u32[]{:S(2)}, u32[]{:S(2)}) collective-permute-start(bf16[512,512]{1,0:T(8,128)(2,1)S(1)} %get-tuple-element.22.refs_0_), channel_id=1, source_target_pairs={{0,8},{8,0},{1,9},{9,1},{2,10},{10,2},{3,11},{11,3},{4,12},{12,4},... | collective-permute-start | bytes 1572872 | tf_op jit(solution)/shard_map/ppermute | solution.py:297
  57.4 14.6 %collective-permute-start.6 = (bf16[512,512]{1,0:T(8,128)(2,1)}, bf16[512,512]{1,0:T(8,128)(2,1)S(1)}, u32[]{:S(2)}, u32[]{:S(2)}) collective-permute-start(bf16[512,512]{1,0:T(8,128)(2,1)} %collective-permute-done.4.refs_1_), channel_id=1, source_target_pairs={{0,8},{8,0},{1,9},{9,1},{2,10},{10,2},{3,11},{11,3},{4,12},{12,4},... | collective-permute-start | bytes 1572872 | tf_op jit(solution)/shard_map/ppermute | solution.py:297
  71.0 14.3 %collective-permute-start.21 = (bf16[512,512]{1,0:T(8,128)(2,1)S(1)}, bf16[512,512]{1,0:T(8,128)(2,1)S(1)}, u32[]{:S(2)}, u32[]{:S(2)}) collective-permute-start(bf16[512,512]{1,0:T(8,128)(2,1)S(1)} %collective-permute-done.13.refs_13_), channel_id=1, source_target_pairs={{0,2},{2,4},{4,6},{6,0},{1,3},{3,5},{5,7},{7,1},{8,10},{10,12},{12... | collective-permute-start | bytes 1572872 | tf_op jit(solution)/shard_map/ppermute | solution.py:291
  72.0 15.4 %collective-permute-start.18 = (bf16[512,512]{1,0:T(8,128)(2,1)S(1)}, bf16[512,512]{1,0:T(8,128)(2,1)S(1)}, u32[]{:S(2)}, u32[]{:S(2)}) collective-permute-start(bf16[512,512]{1,0:T(8,128)(2,1)S(1)} %collective-permute-done.13.refs_13_), channel_id=1, source_target_pairs={{2,0},{4,2},{6,4},{0,6},{3,1},{5,3},{7,5},{1,7},{10,8},{12,10},{14... | collective-permute-start | bytes 1572872 | tf_op jit(solution)/shard_map/ppermute | solution.py:290
  73.2 16.1 %collective-permute-start.15 = (bf16[512,512]{1,0:T(8,128)(2,1)S(1)}, bf16[512,512]{1,0:T(8,128)(2,1)S(1)}, u32[]{:S(2)}, u32[]{:S(2)}) collective-permute-start(bf16[512,512]{1,0:T(8,128)(2,1)S(1)} %collective-permute-done.13.refs_13_), channel_id=1, source_target_pairs={{0,8},{8,0},{1,9},{9,1},{2,10},{10,2},{3,11},{11,3},{4,12},{12,4},... | collective-permute-start | bytes 1572872 | tf_op jit(solution)/shard_map/ppermute | solution.py:297
  73.2 15.6 %collective-permute-start.9 = (bf16[256,512]{1,0:T(8,128)(2,1)S(1)}, bf16[256,512]{1,0:T(8,128)(2,1)S(1)}, u32[]{:S(2)}, u32[]{:S(2)}) collective-permute-start(bf16[256,512]{1,0:T(8,128)(2,1)S(1)} %slice.153), channel_id=1, source_target_pairs={{0,8},{8,0},{1,9},{9,1},{2,10},{10,2},{3,11},{11,3},{4,12},{12,4},... | collective-permute-start | bytes 786440 | tf_op jit(solution)/shard_map/ppermute | solution.py:298
  73.8 16.4 %collective-permute-start.12 = (bf16[512,512]{1,0:T(8,128)(2,1)}, bf16[512,512]{1,0:T(8,128)(2,1)}, u32[]{:S(2)}, u32[]{:S(2)}) collective-permute-start(bf16[512,512]{1,0:T(8,128)(2,1)} %collective-permute-done.10.refs_9_), channel_id=1, source_target_pairs={{0,8},{8,0},{1,9},{9,1},{2,10},{10,2},{3,11},{11,3},{4,12},{12,4},... | collective-permute-start | bytes 1572872 | tf_op jit(solution)/shard_map/ppermute | solution.py:299
  112.7 15.2 %collective-permute-start.31 = (f16[4,128,512]{2,1,0:T(8,128)(2,1)S(1)}, f16[4,128,512]{2,1,0:T(8,128)(2,1)S(1)}, u32[]{:S(2)}, u32[]{:S(2)}) collective-permute-start(f16[4,128,512]{2,1,0:T(8,128)(2,1)S(1)} %get-tuple-element.38), channel_id=1, source_target_pairs={{0,1},{1,16},{16,17},{17,0},{2,3},{3,18},{18,19},{19,2},{4,5},{5,2... | collective-permute-start | bytes 1572872 | tf_op jit(solution)/shard_map/ppermute | solution.py:280
  114.0 28.2 %collective-permute-start.33 = (f16[4,128,512]{2,1,0:T(8,128)(2,1)S(1)}, f16[4,128,512]{2,1,0:T(8,128)(2,1)S(1)}, u32[]{:S(2)}, u32[]{:S(2)}) collective-permute-start(f16[4,128,512]{2,1,0:T(8,128)(2,1)S(1)} %get-tuple-element.39), channel_id=1, source_target_pairs={{0,17},{1,0},{16,1},{17,16},{2,19},{3,2},{18,3},{19,18},{4,21},{5,... | collective-permute-start | bytes 1572872 | tf_op jit(solution)/shard_map/ppermute | solution.py:280
  116.0 26.2 %collective-permute-start.32 = (f16[4,128,512]{2,1,0:T(8,128)(2,1)S(1)}, f16[4,128,512]{2,1,0:T(8,128)(2,1)S(1)}, u32[]{:S(2)}, u32[]{:S(2)}) collective-permute-start(f16[4,128,512]{2,1,0:T(8,128)(2,1)S(1)} %get-tuple-element.40), channel_id=1, source_target_pairs={{0,16},{1,17},{16,0},{17,1},{2,18},{3,19},{18,2},{19,3},{4,20},{5,... | collective-permute-start | bytes 1572872 | tf_op jit(solution)/shard_map/ppermute | solution.py:280
  119.3 26.4 %collective-permute-start.24 = (f16[4,128,512]{2,1,0:T(8,128)(2,1)S(1)}, f16[4,128,512]{2,1,0:T(8,128)(2,1)S(1)}, u32[]{:S(2)}, u32[]{:S(2)}) collective-permute-start(f16[4,128,512]{2,1,0:T(8,128)(2,1)S(1)} %get-tuple-element.34), channel_id=1, source_target_pairs={{4,98},{5,99},{20,114},{21,115},{38,4},{39,5},{54,20},{55,21},{64,... | collective-permute-start | bytes 1572872 | tf_op jit(solution)/shard_map/ppermute | solution.py:270
  121.2 26.5 %collective-permute-start.27 = (f16[4,128,512]{2,1,0:T(8,128)(2,1)S(1)}, f16[4,128,512]{2,1,0:T(8,128)(2,1)S(1)}, u32[]{:S(2)}, u32[]{:S(2)}) collective-permute-start(f16[4,128,512]{2,1,0:T(8,128)(2,1)S(1)} %get-tuple-element.35), channel_id=1, source_target_pairs={{0,96},{1,97},{16,112},{17,113},{2,64},{3,65},{18,80},{19,81},{4,1... | collective-permute-start | bytes 1572872 | tf_op jit(solution)/shard_map/ppermute | solution.py:270
  127.9 26.7 %collective-permute-start.26 = (f16[4,128,512]{2,1,0:T(8,128)(2,1)S(1)}, f16[4,128,512]{2,1,0:T(8,128)(2,1)S(1)}, u32[]{:S(2)}, u32[]{:S(2)}) collective-permute-start(f16[4,128,512]{2,1,0:T(8,128)(2,1)S(1)} %get-tuple-element.36), channel_id=1, source_target_pairs={{0,38},{1,39},{16,54},{17,55},{2,66},{3,67},{18,82},{19,83},{4,68}... | collective-permute-start | bytes 1572872 | tf_op jit(solution)/shard_map/ppermute | solution.py:270
  142.2 25.3 %collective-permute-start.25 = (f16[4,128,512]{2,1,0:T(8,128)(2,1)S(1)}, f16[4,128,512]{2,1,0:T(8,128)(2,1)S(1)}, u32[]{:S(2)}, u32[]{:S(2)}) collective-permute-start(f16[4,128,512]{2,1,0:T(8,128)(2,1)S(1)} %get-tuple-element.37), channel_id=1, source_target_pairs={{0,32},{1,33},{16,48},{17,49},{2,34},{3,35},{18,50},{19,51},{4,36}... | collective-permute-start | bytes 1572872 | tf_op jit(solution)/shard_map/ppermute | solution.py:270
  142.6 28.6 %collective-permute-start.34 = (f16[128,512]{1,0:T(8,128)(2,1)S(1)}, f16[128,512]{1,0:T(8,128)(2,1)S(1)}, u32[]{:S(2)}, u32[]{:S(2)}) collective-permute-start(f16[128,512]{1,0:T(8,128)(2,1)S(1)} %get-tuple-element.44), channel_id=1, source_target_pairs={{0,32},{32,64},{64,96},{96,0},{1,33},{33,65},{65,97},{97,1},{2,34}... | collective-permute-start | bytes 393224 | tf_op jit(solution)/shard_map/ppermute | solution.py:280
  145.7 25.6 %collective-permute-start.36 = (f16[128,512]{1,0:T(8,128)(2,1)S(1)}, f16[128,512]{1,0:T(8,128)(2,1)S(1)}, u32[]{:S(2)}, u32[]{:S(2)}) collective-permute-start(f16[128,512]{1,0:T(8,128)(2,1)S(1)} %get-tuple-element.45), channel_id=1, source_target_pairs={{0,96},{32,0},{64,32},{96,64},{1,97},{33,1},{65,33},{97,65},{2,98}... | collective-permute-start | bytes 393224 | tf_op jit(solution)/shard_map/ppermute | solution.py:280
  147.7 23.5 %collective-permute-start.35 = (f16[128,512]{1,0:T(8,128)(2,1)S(1)}, f16[128,512]{1,0:T(8,128)(2,1)S(1)}, u32[]{:S(2)}, u32[]{:S(2)}) collective-permute-start(f16[128,512]{1,0:T(8,128)(2,1)S(1)} %get-tuple-element.46), channel_id=1, source_target_pairs={{0,64},{32,96},{64,0},{96,32},{1,65},{33,97},{65,1},{97,33},{2,66}... | collective-permute-start | bytes 393224 | tf_op jit(solution)/shard_map/ppermute | solution.py:280
  (41 other events, 463.5 us)

commit v6 on v3

--- a/solution.py
+++ b/solution.py
@@ -24,27 +24,48 @@
     return pl.CostEstimate(flops=flops, bytes_accessed=moved, transcendentals=0)
 
 
-def edge_kernel(x_ref, top_ref, bot_ref):
-    top_ref[0] = x_ref[:, 0, :].astype(BF)
-    top_ref[1] = x_ref[:, 1, :].astype(BF)
-    bot_ref[0] = x_ref[:, 6, :].astype(BF)
-    bot_ref[1] = x_ref[:, 7, :].astype(BF)
-
-
-def edges(field):
+def edge_kernel(x_ref, c_ref, top_ref, bot_ref):
+    i = pl.program_id(0)
+    block, rows, _ = x_ref.shape
+    at = pl.ds(pl.multiple_of(i * block, block), block)
+    for out_ref, first, edge in ((top_ref, 0, 0), (bot_ref, rows - 2, rows - 1)):
+        out_ref[0, at, :] = x_ref[:, first, :].astype(BF)
+        out_ref[1, at, :] = x_ref[:, first + 1, :].astype(BF)
+
+        @pl.when(i == 0)
+        def _():
+            rest = c_ref[:, edge, :]
+            terms = []
+            for _ in range(3):
+                terms.append(rest.astype(BF).astype(jnp.float32))
+                rest = rest - terms[-1]
+            packed = jnp.concatenate(terms + [jnp.zeros_like(rest)], axis=0).astype(BF)
+            last = out_ref.shape[1] - packed.shape[0]
+            for k in range(2):
+                out_ref[k, last:, :] = packed
+
+
+def edges(field, courant):
     groups, rows, width = field.shape
     block = 64
-    shape = jax.ShapeDtypeStruct((2, groups, width), BF)
-    spec = pl.BlockSpec((2, block, width), lambda i: (0, i, 0))
+    shape = jax.ShapeDtypeStruct((2, groups + 16, width), BF)
+    spec = pl.BlockSpec(shape.shape, lambda i: (0, 0, 0))
     return pl.pallas_call(
         edge_kernel,
         grid=(groups // block,),
-        in_specs=[pl.BlockSpec((block, rows, width), lambda i: (i, 0, 0))],
+        in_specs=[
+            pl.BlockSpec((block, rows, width), lambda i: (i, 0, 0)),
+            pl.BlockSpec(courant.shape, lambda i: (0, 0, 0)),
+        ],
         out_specs=[spec, spec],
         out_shape=[shape, shape],
         cost_estimate=cost(1000, 6 << 20),
         compiler_params=params(),
-    )(field)
+    )(field, courant)
+
+
+def edge_weights(halo, groups):
+    return jnp.sum(halo[0, groups:groups + 12].astype(jnp.float32).reshape(3, 4, 1, -1), axis=0)
 
 
 def stepper(coef_ref, offset, delta, width):
@@ -71,59 +92,44 @@
 
 
 def inner_kernel(info, x_ref, coef_ref, emis_ref, det_ref, adv_ref, keep_ref, send_ref):
-    block, _, width = x_ref.shape
+    block, rows, width = x_ref.shape
     own_first = info[1] == 0
 
     def group(g, carry):
         at = pl.ds(pl.multiple_of(g * 16, 16), 16)
         step = stepper(coef_ref, 0, offsets(det_ref, at, info[2], width), width)
-        v = {r: x_ref[at, r, :] for r in (0, 1)}
-        first = {}
-        prints = {}
-        for r in range(1, 7):
-            v[r + 1] = x_ref[at, r + 1, :]
-            first[r] = step(r, v[r - 1], v[r], v[r + 1])
-            if r >= 3:
-                q = r - 1
-                out = step(q, first[q - 1], first[q], first[q + 1])
-                adv_ref[at, q, :] = out
-                prints[q] = out * emis_ref[q:q + 1, :]
-                if q >= 4:
-                    put(keep_ref, send_ref, at, q - 4, own_first, prints[q - 2], prints[q])
+        v = jnp.swapaxes(x_ref[at], 0, 1)
+        first = {r: step(r, v[r - 1], v[r], v[r + 1]) for r in range(1, rows - 1)}
+        out = {r: step(r, first[r - 1], first[r], first[r + 1]) for r in range(2, rows - 2)}
+        tile = jnp.stack([out[min(max(r, 2), rows - 3)] for r in range(rows)])
+        adv_ref[at] = jnp.swapaxes(tile, 0, 1)
+        prints = {r: out[r] * emis_ref[r:r + 1, :] for r in out}
+        for p in range(2):
+            put(keep_ref, send_ref, at, p, own_first, prints[p + 2], prints[p + 4])
         return carry
 
     lax.fori_loop(0, block // 16, group, 0, unroll=2)
 
 
 def outer_kernel(info, x_ref, up_ref, down_ref, coef_ref, emis_ref, det_ref, mid_ref, adv_ref, keep_ref, send_ref):
-    block, _, width = x_ref.shape
+    block, rows, width = x_ref.shape
     own_first = info[1] == 0
 
     def group(g, carry):
         at = pl.ds(pl.multiple_of(g * 16, 16), 16)
         step = stepper(coef_ref, 1, offsets(det_ref, at, info[2], width), width)
-
-        def value(r):
-            if r < 0:
-                return up_ref[r + 2, at, :].astype(jnp.float32)
-            if r > 7:
-                return down_ref[r - 8, at, :].astype(jnp.float32)
-            return x_ref[at, r, :]
-
-        prints = {}
-        for base in (-1, 5):
-            v = {r: value(r) for r in (base - 1, base)}
-            first = {}
-            for r in range(base, base + 4):
-                v[r + 1] = value(r + 1)
-                first[r] = step(r, v[r - 1], v[r], v[r + 1])
-                if r >= base + 2:
-                    q = r - 1
-                    out = step(q, first[q - 1], first[q], first[q + 1])
-                    adv_ref[at, q, :] = out
-                    prints[q] = out * emis_ref[q:q + 1, :]
-        for r in range(2, 6):
-            adv_ref[at, r, :] = mid_ref[at, r, :]
+        tile = jnp.swapaxes(x_ref[at], 0, 1)
+        v = {r: tile[r] for r in range(rows)}
+        for r in range(2):
+            v[r - 2] = up_ref[r, at, :].astype(jnp.float32)
+            v[r + rows] = down_ref[r, at, :].astype(jnp.float32)
+        first = {r: step(r, v[r - 1], v[r], v[r + 1]) for r in (-1, 0, 1, 2, 5, 6, 7, 8)}
+        out = {r: step(r, first[r - 1], first[r], first[r + 1]) for r in (0, 1, 6, 7)}
+        tile = jnp.stack([out[r if r in out else (1 if r < 4 else 6)] for r in range(rows)])
+        tile = jnp.swapaxes(tile, 0, 1)
+        row = lax.broadcasted_iota(jnp.int32, tile.shape, 1)
+        adv_ref[at] = jnp.where((row >= 2) & (row < 6), mid_ref[at], tile)
+        prints = {r: out[r] * emis_ref[r:r + 1, :] for r in out}
         for p in range(2):
             put(keep_ref, send_ref, at, p, own_first, prints[p], prints[p + 6])
         return carry
@@ -179,7 +185,7 @@
     stack, outs = refs[-1], refs[-3:-1]
     accs = refs[12:14] if grows else None
     own, own_s, nxt, nxt_s, last, last_s = (refs[2 * k:2 * k + 2] for k in range(6))
-    core, xl, y, xpos = info[0], info[1], info[3], info[4]
+    core, xl, y, xpos, z = info[0], info[1], info[3], info[4], info[5]
     rows = nxt_s[0].shape[0]
     half = own[0].shape[1]
     part = rows // 2
@@ -205,7 +211,8 @@
             for e, i, value in values:
                 at_z = lax.rem(y + e, 4)
                 at_x = lax.rem(lax.rem(i + xl, 2) * 2 + lax.rem(j + xl, 2) + 4 - xpos, 4)
-                for upper, slot in enumerate((at_z * 4 + at_x, at_x * 4 + at_z)):
+                from_z = lax.rem(at_z + 4 - z, 4)
+                for upper, slot in enumerate((from_z * 4 + at_x, at_x * 4 + at_z)):
                     piece = value[upper * part:(upper + 1) * part]
                     if accs is not None:
                         piece = piece + accs[upper][slot, :, cols]
@@ -273,17 +280,14 @@
     tile = lax.axis_index(GRID)
     first_cell = tile * rows * width
     xpos = lax.axis_index(XS)
-    info = jnp.stack([core, xl, first_cell, y, xpos]).astype(jnp.int32)
+    info = jnp.stack([core, xl, first_cell, y, xpos, z]).astype(jnp.int32)
     count = lax.axis_size(GRID)
     forward = [(i, i + 1) for i in range(count - 1)]
     backward = [(i + 1, i) for i in range(count - 1)]
 
-    top, bottom = edges(adjoint)
+    top, bottom = edges(adjoint, courant)
     up = lax.ppermute(bottom, GRID, forward)
     down = lax.ppermute(top, GRID, backward)
-    near = after(courant, top)
-    coef_up = lax.ppermute(near[:, rows - 1:], GRID, forward)
-    coef_down = lax.ppermute(near[:, :1], GRID, backward)
     columns = jnp.arange(width)
 
     def weights(c):
@@ -312,7 +316,9 @@
     other_y = along_y(after(other, keep_y))
     totals = partial_gram(info, gram_operands(keep, keep_y, other, other_y), [])
 
-    extended = jnp.concatenate([coef_up, courant, coef_down], axis=1)
+    extended = jnp.concatenate(
+        [edge_weights(up, groups), courant, edge_weights(down, groups)], axis=1
+    )
     field, keep, send = stencil(
         outer_kernel, after(info, keep_y), adjoint, [up, down], weights(extended), emis, det,
         [mid], OUTER
@@ -325,9 +331,8 @@
     along_z, along_x = [
         (total * LIFT).astype(HALF).reshape(4, 4, groups // 4, groups) for total in totals
     ]
-    along_z = lax.all_to_all(along_z, "z", 0, 0, tiled=True)
-    along_x = after(to_four(along_x, XS).astype(HALF), along_z)
-    along_z = mean_of_four(along_z).astype(HALF)
+    along_x = to_four(along_x, XS).astype(HALF)
+    along_z = to_four(along_z, "z").astype(HALF)
     along_x = mean_of_four(lax.all_to_all(along_x, "z", 0, 0, tiled=True))
     along_z = to_four(along_z, XS)
     summed = jnp.concatenate([along_z, along_x], axis=0)

time: 171 us -> 163 us (0.953)
  waiting for transfers between devices: 75.9 us -> 66.4 us
  other arithmetic: 7.56 us -> 5.07 us
  local copies, waits for them, and re-layouts: 7.1 us -> 9.41 us
    ppermute x6 -> x9, starting transfers between devices: 9.54 us -> 24.3 us  [to_four(): came = lax.ppermute(pieces[d], axis, [(i, (i + d) % 4) for i in range(4)])]
    ppermute x2 -> x0, waiting for transfers between devices: 6.71 us -> none  [the longest x1 5.4 us: body(): coef_up = lax.ppermute(near[:, rows - 1:], GRID, forward)]
    ppermute x6 -> x9, waiting for transfers between devices: 26.7 us -> 21.6 us  [to_four(): came = lax.ppermute(pieces[d], axis, [(i, (i + d) % 4) for i in range(4)])]
    all_to_all x1 -> x0, starting transfers between devices: 4.96 us -> none  [body(): along_z = lax.all_to_all(along_z, 'z', 0, 0, tiled=True)]
    ppermute x2 -> x0, starting transfers between devices: 3.82 us -> none  [the longest x1 1.91 us: body(): coef_down = lax.ppermute(near[:, :1], GRID, backward)]
    convert_element_type x2, other arithmetic: 4.8 us -> 1.22 us  [body(): (total * LIFT).astype(HALF).reshape(4, 4, groups // 4, groups)]
    ppermute x1, starting transfers between devices: 6.05 us -> 3.9 us  [body(): down = lax.ppermute(top, GRID, backward)]
    ppermute x4, starting transfers between devices: 2.95 us -> 0.91 us  [siblings(): nxt_s = lax.ppermute(nxt[part:], 'core', SWAP)]
  transfers between devices with their start and end apart: 35 -> 35, of which waited for: 19 -> 18; matrix products, arithmetic and copies ran while one was open for 3% -> 4% of each run, Pallas kernels for 14% -> 15%
where the time goes in v6:
time: 163 us
  waiting for transfers between devices  66.4 us (41%)
  starting transfers between devices  47.7 us (29%)
  Pallas kernels  32.2 us (20%)
  local copies, waits for them, and re-layouts  9.41 us (6%)
  other arithmetic  5.07 us (3%)
    ppermute x9, starting transfers between devices, to_four(): came = lax.ppermute(pieces[d], axis, [(i, (i + d) % 4) for i in range(4)])  24.3 us
    ppermute x9, waiting for transfers between devices, to_four(): came = lax.ppermute(pieces[d], axis, [(i, (i + d) % 4) for i in range(4)])  21.6 us
    pallas_call x2, Pallas kernels, stencil(): pl.pallas_call(kernel, grid_spec=pltpu.PrefetchScalarGridSpec(num_scalar_...  17.5 us
    ppermute x2, waiting for transfers between devices, body(): other = lax.ppermute(send, 'xl', SWAP)  14.2 us
    ppermute x4, waiting for transfers between devices, along_y(): last = lax.ppermute(own, 'y', [(i, (i + 1) % 4) for i in range(4)])  12.7 us
    pallas_call x2, Pallas kernels, partial_gram(): pl.pallas_call(lambda *refs: gram_kernel(bool(acc), *refs), in_specs=[pl....  11.5 us
    ppermute x1, waiting for transfers between devices, body(): lax.ppermute(summed.astype(HALF), ('z', 'y'), moves).astype(jnp.float32)  8.44 us
    unnamed x20, local copies, waits for them, and re-layouts  7.34 us
  transfers between devices with their start and end apart: 35, of which 18 were waited for; matrix products, arithmetic and copies ran while one was open for 4% of the time, Pallas kernels for 15%

profile of v6, /device:TPU:56, one launch (start us, length us, event | category | flops | bytes accessed | tf_op | source)
XLA Modules:
  0.0 162.6 jit_solution(8822099128903216712)
XLA Ops:
  0.6 2.2 %copy-done = f32[512,8,256]{2,1,0:T(8,128)S(1)} copy-done((f32[512,8,256]{2,1,0:T(8,128)S(1)}, f32[512,8,256]{2,1,0:T(8,128)}, u32[]{:S(2)}) %copy-start) | copy-done | bytes 4194328
  3.6 3.1 %shard_map.68 = (bf16[2,528,256]{2,1,0:T(8,128)(2,1)}, bf16[2,528,256]{2,1,0:T(8,128)(2,1)S(1)}) custom-call(f32[512,8,256]{2,1,0:T(8,128)S(1)} %copy-done, f32[4,8,256]{2,1,0:T(8,128)S(1)} %copy-done.5), custom_call_target="tpu_custom_call" | custom-call | flops 1000 | bytes 6291456 | tf_op jit(solution)/shard_map/pallas_call | solution.py:53
  6.7 3.9 %collective-permute-start.1 = (bf16[2,528,256]{2,1,0:T(8,128)(2,1)}, bf16[2,528,256]{2,1,0:T(8,128)(2,1)S(1)}, u32[]{:S(2)}, u32[]{:S(2)}) collective-permute-start(bf16[2,528,256]{2,1,0:T(8,128)(2,1)} %get-tuple-element.19), channel_id=1, source_target_pairs={{8,0},{16,8},{24,16},{32,24},{40,32},{48,40},{56,48},{64,56},{72,6... | collective-permute-start | bytes 1622024 | tf_op jit(solution)/shard_map/ppermute | solution.py:290
  10.6 1.9 %collective-permute-start = (bf16[2,528,256]{2,1,0:T(8,128)(2,1)S(1)}, bf16[2,528,256]{2,1,0:T(8,128)(2,1)S(1)}, u32[]{:S(2)}, u32[]{:S(2)}) collective-permute-start(bf16[2,528,256]{2,1,0:T(8,128)(2,1)S(1)} %get-tuple-element.20), channel_id=1, source_target_pairs={{0,8},{8,16},{16,24},{24,32},{32,40},{40,48},{48,56},{56,64},{64,7... | collective-permute-start | bytes 1622024 | tf_op jit(solution)/shard_map/ppermute | solution.py:289
  13.7 2.2 %copy-done.1 = f32[512,8,256]{2,1,0:T(8,128)S(1)} copy-done((f32[512,8,256]{2,1,0:T(8,128)S(1)}, f32[512,8,256]{2,1,0:T(8,128)}, u32[]{:S(2)}) %copy-start.1) | copy-done | bytes 4194328
  15.9 7.3 %shard_map.69 = (f32[512,8,256]{2,1,0:T(8,128)}, bf16[512,512]{1,0:T(8,128)(2,1)S(1)}, bf16[512,512]{1,0:T(8,128)(2,1)S(1)}) custom-call(s32[6]{0:T(128)S(1)} %stack.39.info.refs_0_, f32[512,8,256]{2,1,0:T(8,128)S(1)} %copy-done.1, f32[5,8,256]{2,1,0:T(8,128)S(1)} %pad_maximum_fusion.3.coef_ref, f32[8,256]{1,0:T(8,128)S(1)} %fusion.emis_ref, ...), custom_call_target="tpu_custom_call" | custom-call | flops 1000 | bytes 104857600 | tf_op jit(solution)/shard_map/pallas_call | solution.py:155
  27.0 10.9 %collective-permute-done.9.refs_2_ = bf16[512,512]{1,0:T(8,128)(2,1)S(1)} collective-permute-done((bf16[512,512]{1,0:T(8,128)(2,1)S(1)}, bf16[512,512]{1,0:T(8,128)(2,1)S(1)}, u32[]{:S(2)}, u32[]{:S(2)}) %collective-permute-start.9) | collective-permute-done | bytes 524320 | tf_op jit(solution)/shard_map/ppermute | solution.py:314
  43.4 2.2 %copy-done.2 = f32[512,8,256]{2,1,0:T(8,128)S(1)} copy-done((f32[512,8,256]{2,1,0:T(8,128)S(1)}, f32[512,8,256]{2,1,0:T(8,128)}, u32[]{:S(2)}) %copy-start.2) | copy-done | bytes 4194328
  45.6 10.2 %shard_map.70 = (f32[512,8,256]{2,1,0:T(8,128)}, bf16[512,512]{1,0:T(8,128)(2,1)S(1)}, bf16[512,512]{1,0:T(8,128)(2,1)S(1)}) custom-call(s32[6]{0:T(128)S(1)} %stack.39.info.refs_0_, f32[512,8,256]{2,1,0:T(8,128)S(1)} %copy-done.2, bf16[2,528,256]{2,1,0:T(8,128)(2,1)S(1)} %collective-permute-done.up_ref, ...), custom_call_target="tpu_custom_call", output_to_operand_aliasing={{0}: (7, {})} | custom-call | flops 1000 | bytes 20971520 | tf_op jit(solution)/shard_map/pallas_call | solution.py:155
  56.4 2.3 %collective-permute-start.8 = (bf16[512,512]{1,0:T(8,128)(2,1)S(1)}, bf16[512,512]{1,0:T(8,128)(2,1)S(1)}, u32[]{:S(2)}, u32[]{:S(2)}) collective-permute-start(bf16[512,512]{1,0:T(8,128)(2,1)S(1)} %get-tuple-element.27.refs_1_), channel_id=1, source_target_pairs={{0,2},{2,4},{4,6},{6,0},{1,3},{3,5},{5,7},{7,1},{8,10},{10,12},{12... | collective-permute-start | bytes 1572872 | tf_op jit(solution)/shard_map/ppermute | solution.py:252
  60.4 6.1 %shard_map.71 = (f32[16,128,512]{2,1,0:T(8,128)S(1)}, f32[16,128,512]{2,1,0:T(8,128)S(1)}) custom-call(s32[6]{0:T(128)S(1)} %stack.39.info.refs_0_, bf16[512,512]{1,0:T(8,128)(2,1)S(1)} %get-tuple-element.23.refs_1_, bf16[512,512]{1,0:T(8,128)(2,1)S(1)} %collective-permute-done.9.refs_2_, bf16[512,512]{1,0:T(8,128)(2,1)} %collective-permute-done.10.refs_3_, ...), custom_call_target="tpu_custom_call" | custom-call | flops 1000 | bytes 8388608 | tf_op jit(solution)/shard_map/pallas_call | solution.py:227
  66.4 3.3 %collective-permute-done.4.refs_2_ = bf16[512,512]{1,0:T(8,128)(2,1)S(1)} collective-permute-done((bf16[512,512]{1,0:T(8,128)(2,1)S(1)}, bf16[512,512]{1,0:T(8,128)(2,1)S(1)}, u32[]{:S(2)}, u32[]{:S(2)}) %collective-permute-start.4) | collective-permute-done | bytes 524320 | tf_op jit(solution)/shard_map/ppermute | solution.py:326
  70.8 3.1 %collective-permute-done.7.refs_5_ = bf16[512,512]{1,0:T(8,128)(2,1)S(1)} collective-permute-done((bf16[512,512]{1,0:T(8,128)(2,1)S(1)}, bf16[512,512]{1,0:T(8,128)(2,1)S(1)}, u32[]{:S(2)}, u32[]{:S(2)}) %collective-permute-start.7) | collective-permute-done | bytes 524320 | tf_op jit(solution)/shard_map/ppermute | solution.py:251
  76.5 10.6 %collective-permute-done.21.refs_10_ = bf16[512,512]{1,0:T(8,128)(2,1)S(1)} collective-permute-done((bf16[512,512]{1,0:T(8,128)(2,1)S(1)}, bf16[512,512]{1,0:T(8,128)(2,1)S(1)}, u32[]{:S(2)}, u32[]{:S(2)}) %collective-permute-start.21) | collective-permute-done | bytes 524320 | tf_op jit(solution)/shard_map/ppermute | solution.py:252
  90.5 5.5 %shard_map.72 = (f32[16,128,512]{2,1,0:T(8,128)S(1)}, f32[16,128,512]{2,1,0:T(8,128)S(1)}) custom-call(s32[6]{0:T(128)S(1)} %stack.39.info.refs_0_, bf16[512,512]{1,0:T(8,128)(2,1)S(1)} %get-tuple-element.27.refs_1_, bf16[512,512]{1,0:T(8,128)(2,1)S(1)} %collective-permute-done.4.refs_2_, bf16[512,512]{1,0:T(8,128)(2,1)S(1)} %collective-permute-done.5.refs_3_, ...), custom_call_target="tpu_custom_call" | custom-call | flops 1000 | bytes 8388608 | tf_op jit(solution)/shard_map/pallas_call | solution.py:227
  98.2 2.0 %collective-permute-start.32 = (f16[4,128,512]{2,1,0:T(8,128)(2,1)S(1)}, f16[4,128,512]{2,1,0:T(8,128)(2,1)S(1)}, u32[]{:S(2)}, u32[]{:S(2)}) collective-permute-start(f16[4,128,512]{2,1,0:T(8,128)(2,1)S(1)} %get-tuple-element.40), channel_id=1, source_target_pairs={{0,17},{1,0},{16,1},{17,16},{2,19},{3,2},{18,3},{19,18},{4,21},{5,... | collective-permute-start | bytes 1572872 | tf_op jit(solution)/shard_map/ppermute | solution.py:241
  106.1 6.6 %collective-permute-done.30 = f16[4,128,512]{2,1,0:T(8,128)(2,1)S(1)} collective-permute-done((f16[4,128,512]{2,1,0:T(8,128)(2,1)S(1)}, f16[4,128,512]{2,1,0:T(8,128)(2,1)S(1)}, u32[]{:S(2)}, u32[]{:S(2)}) %collective-permute-start.30) | collective-permute-done | bytes 524320 | tf_op jit(solution)/shard_map/ppermute | solution.py:241
  112.7 13.8 %collective-permute-start.25 = (f16[4,128,512]{2,1,0:T(8,128)(2,1)}, f16[4,128,512]{2,1,0:T(8,128)(2,1)}, u32[]{:S(2)}, u32[]{:S(2)}) collective-permute-start(f16[4,128,512]{2,1,0:T(8,128)(2,1)} %get-tuple-element.38), channel_id=1, source_target_pairs={{0,64},{32,96},{64,0},{96,32},{1,65},{33,97},{65,1},{97,33},{2,66}... | collective-permute-start | bytes 1572872 | tf_op jit(solution)/shard_map/ppermute | solution.py:241
  127.7 3.5 %all-to-all-start = ((f16[4,128,512]{2,1,0:T(8,128)(2,1)}), f16[4,128,512]{2,1,0:T(8,128)(2,1)S(1)}, u32[]{:S(2)}, u32[]{:S(2)}) async-start(f16[4,128,512]{2,1,0:T(8,128)(2,1)} %multiply_convert_fusion.2), calls=%async_computation | async-start | bytes 1048576 | tf_op jit(solution)/shard_map/all_to_all | solution.py:336
  131.2 8.5 %collective-permute-done.25 = f16[4,128,512]{2,1,0:T(8,128)(2,1)} collective-permute-done((f16[4,128,512]{2,1,0:T(8,128)(2,1)}, f16[4,128,512]{2,1,0:T(8,128)(2,1)}, u32[]{:S(2)}, u32[]{:S(2)}) %collective-permute-start.25) | collective-permute-done | bytes 524320 | tf_op jit(solution)/shard_map/ppermute | solution.py:241
  141.4 3.2 %collective-permute-start.29 = (f16[128,512]{1,0:T(8,128)(2,1)S(1)}, f16[128,512]{1,0:T(8,128)(2,1)S(1)}, u32[]{:S(2)}, u32[]{:S(2)}) collective-permute-start(f16[128,512]{1,0:T(8,128)(2,1)S(1)} %get-tuple-element.43), channel_id=1, source_target_pairs={{0,17},{1,0},{16,1},{17,16},{2,19},{3,2},{18,3},{19,18},{4,21},{5,... | collective-permute-start | bytes 393224 | tf_op jit(solution)/shard_map/ppermute | solution.py:241
  144.6 3.9 %collective-permute-done.27 = f16[128,512]{1,0:T(8,128)(2,1)S(1)} collective-permute-done((f16[128,512]{1,0:T(8,128)(2,1)S(1)}, f16[128,512]{1,0:T(8,128)(2,1)S(1)}, u32[]{:S(2)}, u32[]{:S(2)}) %collective-permute-start.27) | collective-permute-done | bytes 131104 | tf_op jit(solution)/shard_map/ppermute | solution.py:241
  148.6 2.5 %collective-permute-done.28 = f16[128,512]{1,0:T(8,128)(2,1)S(1)} collective-permute-done((f16[128,512]{1,0:T(8,128)(2,1)S(1)}, f16[128,512]{1,0:T(8,128)(2,1)S(1)}, u32[]{:S(2)}, u32[]{:S(2)}) %collective-permute-start.28) | collective-permute-done | bytes 131104 | tf_op jit(solution)/shard_map/ppermute | solution.py:241
  153.3 8.4 %collective-permute-done.33 = f16[256,512]{1,0:T(8,128)(2,1)S(1)} collective-permute-done((f16[256,512]{1,0:T(8,128)(2,1)S(1)}, f16[256,512]{1,0:T(8,128)(2,1)S(1)}, u32[]{:S(2)}, u32[]{:S(2)}) %collective-permute-start.33) | collective-permute-done | bytes 262176 | tf_op jit(solution)/shard_map/ppermute | solution.py:340
  (108 shorter events, 34.3 us)
Async XLA Ops:
  6.7 17.1 %collective-permute-start.1 = (bf16[2,528,256]{2,1,0:T(8,128)(2,1)}, bf16[2,528,256]{2,1,0:T(8,128)(2,1)S(1)}, u32[]{:S(2)}, u32[]{:S(2)}) collective-permute-start(bf16[2,528,256]{2,1,0:T(8,128)(2,1)} %get-tuple-element.19), channel_id=1, source_target_pairs={{8,0},{16,8},{24,16},{32,24},{40,32},{48,40},{56,48},{64,56},{72,6... | collective-permute-start | bytes 1622024 | tf_op jit(solution)/shard_map/ppermute | solution.py:290
  10.6 13.9 %collective-permute-start = (bf16[2,528,256]{2,1,0:T(8,128)(2,1)S(1)}, bf16[2,528,256]{2,1,0:T(8,128)(2,1)S(1)}, u32[]{:S(2)}, u32[]{:S(2)}) collective-permute-start(bf16[2,528,256]{2,1,0:T(8,128)(2,1)S(1)} %get-tuple-element.20), channel_id=1, source_target_pairs={{0,8},{8,16},{16,24},{24,32},{32,40},{40,48},{48,56},{56,64},{64,7... | collective-permute-start | bytes 1622024 | tf_op jit(solution)/shard_map/ppermute | solution.py:289
  23.2 14.6 %collective-permute-start.9 = (bf16[512,512]{1,0:T(8,128)(2,1)S(1)}, bf16[512,512]{1,0:T(8,128)(2,1)S(1)}, u32[]{:S(2)}, u32[]{:S(2)}) collective-permute-start(bf16[512,512]{1,0:T(8,128)(2,1)S(1)} %get-tuple-element.29), channel_id=1, source_target_pairs={{0,1},{1,0},{2,3},{3,2},{4,5},{5,4},{6,7},{7,6},{8,9},{9,8},{10,11... | collective-permute-start | bytes 1572872 | tf_op jit(solution)/shard_map/ppermute | solution.py:314
  24.5 14.7 %collective-permute-start.3 = (bf16[512,512]{1,0:T(8,128)(2,1)S(1)}, bf16[512,512]{1,0:T(8,128)(2,1)S(1)}, u32[]{:S(2)}, u32[]{:S(2)}) collective-permute-start(bf16[512,512]{1,0:T(8,128)(2,1)S(1)} %get-tuple-element.23.refs_1_), channel_id=1, source_target_pairs={{0,2},{2,4},{4,6},{6,0},{1,3},{3,5},{5,7},{7,1},{8,10},{10,12},{12... | collective-permute-start | bytes 1572872 | tf_op jit(solution)/shard_map/ppermute | solution.py:252
  24.7 15.9 %collective-permute-start.2 = (bf16[512,512]{1,0:T(8,128)(2,1)S(1)}, bf16[512,512]{1,0:T(8,128)(2,1)S(1)}, u32[]{:S(2)}, u32[]{:S(2)}) collective-permute-start(bf16[512,512]{1,0:T(8,128)(2,1)S(1)} %get-tuple-element.23.refs_1_), channel_id=1, source_target_pairs={{2,0},{4,2},{6,4},{0,6},{3,1},{5,3},{7,5},{1,7},{10,8},{12,10},{14... | collective-permute-start | bytes 1572872 | tf_op jit(solution)/shard_map/ppermute | solution.py:251
  26.5 16.4 %collective-permute-start.10 = (bf16[512,512]{1,0:T(8,128)(2,1)S(1)}, bf16[512,512]{1,0:T(8,128)(2,1)}, u32[]{:S(2)}, u32[]{:S(2)}) collective-permute-start(bf16[512,512]{1,0:T(8,128)(2,1)S(1)} %get-tuple-element.23.refs_1_), channel_id=1, source_target_pairs={{0,8},{8,0},{1,9},{9,1},{2,10},{10,2},{3,11},{11,3},{4,12},{12,4},... | collective-permute-start | bytes 1572872 | tf_op jit(solution)/shard_map/ppermute | solution.py:258
  37.8 18.0 %collective-permute-start.11 = (bf16[512,512]{1,0:T(8,128)(2,1)S(1)}, bf16[512,512]{1,0:T(8,128)(2,1)}, u32[]{:S(2)}, u32[]{:S(2)}) collective-permute-start(bf16[512,512]{1,0:T(8,128)(2,1)S(1)} %collective-permute-done.9.refs_2_), channel_id=1, source_target_pairs={{0,8},{8,0},{1,9},{9,1},{2,10},{10,2},{3,11},{11,3},{4,12},{12,4},... | collective-permute-start | bytes 1572872 | tf_op jit(solution)/shard_map/ppermute | solution.py:258
  40.6 15.8 %collective-permute-start.15 = (bf16[512,512]{1,0:T(8,128)(2,1)S(1)}, bf16[512,512]{1,0:T(8,128)(2,1)}, u32[]{:S(2)}, u32[]{:S(2)}) collective-permute-start(bf16[512,512]{1,0:T(8,128)(2,1)S(1)} %collective-permute-done.9.refs_2_), channel_id=1, source_target_pairs={{0,2},{2,4},{4,6},{6,0},{1,3},{3,5},{5,7},{7,1},{8,10},{10,12},{12... | collective-permute-start | bytes 1572872 | tf_op jit(solution)/shard_map/ppermute | solution.py:252
  41.4 17.3 %collective-permute-start.12 = (bf16[512,512]{1,0:T(8,128)(2,1)S(1)}, bf16[512,512]{1,0:T(8,128)(2,1)S(1)}, u32[]{:S(2)}, u32[]{:S(2)}) collective-permute-start(bf16[512,512]{1,0:T(8,128)(2,1)S(1)} %collective-permute-done.9.refs_2_), channel_id=1, source_target_pairs={{2,0},{4,2},{6,4},{0,6},{3,1},{5,3},{7,5},{1,7},{10,8},{12,10},{14... | collective-permute-start | bytes 1572872 | tf_op jit(solution)/shard_map/ppermute | solution.py:251
  42.8 13.6 %collective-permute-start.13 = (bf16[256,512]{1,0:T(8,128)(2,1)S(1)}, bf16[256,512]{1,0:T(8,128)(2,1)S(1)}, u32[]{:S(2)}, u32[]{:S(2)}) collective-permute-start(bf16[256,512]{1,0:T(8,128)(2,1)S(1)} %slice.135), channel_id=1, source_target_pairs={{0,8},{8,0},{1,9},{9,1},{2,10},{10,2},{3,11},{11,3},{4,12},{12,4},... | collective-permute-start | bytes 786440 | tf_op jit(solution)/shard_map/ppermute | solution.py:259
  42.9 15.9 %collective-permute-start.16 = (bf16[512,512]{1,0:T(8,128)(2,1)}, bf16[512,512]{1,0:T(8,128)(2,1)S(1)}, u32[]{:S(2)}, u32[]{:S(2)}) collective-permute-start(bf16[512,512]{1,0:T(8,128)(2,1)} %copy-done.3), channel_id=1, source_target_pairs={{0,8},{8,0},{1,9},{9,1},{2,10},{10,2},{3,11},{11,3},{4,12},{12,4},... | collective-permute-start | bytes 1572872 | tf_op jit(solution)/shard_map/ppermute | solution.py:260
  55.8 13.9 %collective-permute-start.4 = (bf16[512,512]{1,0:T(8,128)(2,1)S(1)}, bf16[512,512]{1,0:T(8,128)(2,1)S(1)}, u32[]{:S(2)}, u32[]{:S(2)}) collective-permute-start(bf16[512,512]{1,0:T(8,128)(2,1)S(1)} %get-tuple-element.28), channel_id=1, source_target_pairs={{0,1},{1,0},{2,3},{3,2},{4,5},{5,4},{6,7},{7,6},{8,9},{9,8},{10,11... | collective-permute-start | bytes 1572872 | tf_op jit(solution)/shard_map/ppermute | solution.py:326
  56.4 14.3 %collective-permute-start.8 = (bf16[512,512]{1,0:T(8,128)(2,1)S(1)}, bf16[512,512]{1,0:T(8,128)(2,1)S(1)}, u32[]{:S(2)}, u32[]{:S(2)}) collective-permute-start(bf16[512,512]{1,0:T(8,128)(2,1)S(1)} %get-tuple-element.27.refs_1_), channel_id=1, source_target_pairs={{0,2},{2,4},{4,6},{6,0},{1,3},{3,5},{5,7},{7,1},{8,10},{10,12},{12... | collective-permute-start | bytes 1572872 | tf_op jit(solution)/shard_map/ppermute | solution.py:252
  58.7 15.2 %collective-permute-start.7 = (bf16[512,512]{1,0:T(8,128)(2,1)S(1)}, bf16[512,512]{1,0:T(8,128)(2,1)S(1)}, u32[]{:S(2)}, u32[]{:S(2)}) collective-permute-start(bf16[512,512]{1,0:T(8,128)(2,1)S(1)} %get-tuple-element.27.refs_1_), channel_id=1, source_target_pairs={{2,0},{4,2},{6,4},{0,6},{3,1},{5,3},{7,5},{1,7},{10,8},{12,10},{14... | collective-permute-start | bytes 1572872 | tf_op jit(solution)/shard_map/ppermute | solution.py:251
  74.2 14.4 %collective-permute-start.18 = (bf16[512,512]{1,0:T(8,128)(2,1)S(1)}, bf16[512,512]{1,0:T(8,128)(2,1)S(1)}, u32[]{:S(2)}, u32[]{:S(2)}) collective-permute-start(bf16[512,512]{1,0:T(8,128)(2,1)S(1)} %collective-permute-done.4.refs_2_), channel_id=1, source_target_pairs={{2,0},{4,2},{6,4},{0,6},{3,1},{5,3},{7,5},{1,7},{10,8},{12,10},{14... | collective-permute-start | bytes 1572872 | tf_op jit(solution)/shard_map/ppermute | solution.py:251
  75.9 14.2 %collective-permute-start.6 = (bf16[512,512]{1,0:T(8,128)(2,1)S(1)}, bf16[512,512]{1,0:T(8,128)(2,1)S(1)}, u32[]{:S(2)}, u32[]{:S(2)}) collective-permute-start(bf16[512,512]{1,0:T(8,128)(2,1)S(1)} %collective-permute-done.4.refs_2_), channel_id=1, source_target_pairs={{0,8},{8,0},{1,9},{9,1},{2,10},{10,2},{3,11},{11,3},{4,12},{12,4},... | collective-permute-start | bytes 1572872 | tf_op jit(solution)/shard_map/ppermute | solution.py:258
  76.5 13.7 %collective-permute-start.22 = (bf16[512,512]{1,0:T(8,128)(2,1)S(1)}, bf16[512,512]{1,0:T(8,128)(2,1)S(1)}, u32[]{:S(2)}, u32[]{:S(2)}) collective-permute-start(bf16[512,512]{1,0:T(8,128)(2,1)S(1)} %collective-permute-done.8.refs_9_), channel_id=1, source_target_pairs={{0,8},{8,0},{1,9},{9,1},{2,10},{10,2},{3,11},{11,3},{4,12},{12,4},... | collective-permute-start | bytes 1572872 | tf_op jit(solution)/shard_map/ppermute | solution.py:260
  97.0 15.8 %collective-permute-start.30 = (f16[4,128,512]{2,1,0:T(8,128)(2,1)S(1)}, f16[4,128,512]{2,1,0:T(8,128)(2,1)S(1)}, u32[]{:S(2)}, u32[]{:S(2)}) collective-permute-start(f16[4,128,512]{2,1,0:T(8,128)(2,1)S(1)} %get-tuple-element.39), channel_id=1, source_target_pairs={{0,1},{1,16},{16,17},{17,0},{2,3},{3,18},{18,19},{19,2},{4,5},{5,2... | collective-permute-start | bytes 1572872 | tf_op jit(solution)/shard_map/ppermute | solution.py:241
  98.2 28.3 %collective-permute-start.32 = (f16[4,128,512]{2,1,0:T(8,128)(2,1)S(1)}, f16[4,128,512]{2,1,0:T(8,128)(2,1)S(1)}, u32[]{:S(2)}, u32[]{:S(2)}) collective-permute-start(f16[4,128,512]{2,1,0:T(8,128)(2,1)S(1)} %get-tuple-element.40), channel_id=1, source_target_pairs={{0,17},{1,0},{16,1},{17,16},{2,19},{3,2},{18,3},{19,18},{4,21},{5,... | collective-permute-start | bytes 1572872 | tf_op jit(solution)/shard_map/ppermute | solution.py:241
  100.3 26.3 %collective-permute-start.31 = (f16[4,128,512]{2,1,0:T(8,128)(2,1)S(1)}, f16[4,128,512]{2,1,0:T(8,128)(2,1)S(1)}, u32[]{:S(2)}, u32[]{:S(2)}) collective-permute-start(f16[4,128,512]{2,1,0:T(8,128)(2,1)S(1)} %get-tuple-element.41), channel_id=1, source_target_pairs={{0,16},{1,17},{16,0},{17,1},{2,18},{3,19},{18,2},{19,3},{4,20},{5,... | collective-permute-start | bytes 1572872 | tf_op jit(solution)/shard_map/ppermute | solution.py:241
  104.1 27.1 %collective-permute-start.24 = (f16[4,128,512]{2,1,0:T(8,128)(2,1)}, f16[4,128,512]{2,1,0:T(8,128)(2,1)S(1)}, u32[]{:S(2)}, u32[]{:S(2)}) collective-permute-start(f16[4,128,512]{2,1,0:T(8,128)(2,1)} %get-tuple-element.36), channel_id=1, source_target_pairs={{0,32},{32,64},{64,96},{96,0},{1,33},{33,65},{65,97},{97,1},{2,34}... | collective-permute-start | bytes 1572872 | tf_op jit(solution)/shard_map/ppermute | solution.py:241
  106.0 25.2 %collective-permute-start.26 = (f16[4,128,512]{2,1,0:T(8,128)(2,1)}, f16[4,128,512]{2,1,0:T(8,128)(2,1)}, u32[]{:S(2)}, u32[]{:S(2)}) collective-permute-start(f16[4,128,512]{2,1,0:T(8,128)(2,1)} %get-tuple-element.37), channel_id=1, source_target_pairs={{0,96},{32,0},{64,32},{96,64},{1,97},{33,1},{65,33},{97,65},{2,98}... | collective-permute-start | bytes 1572872 | tf_op jit(solution)/shard_map/ppermute | solution.py:241
  112.7 27.0 %collective-permute-start.25 = (f16[4,128,512]{2,1,0:T(8,128)(2,1)}, f16[4,128,512]{2,1,0:T(8,128)(2,1)}, u32[]{:S(2)}, u32[]{:S(2)}) collective-permute-start(f16[4,128,512]{2,1,0:T(8,128)(2,1)} %get-tuple-element.38), channel_id=1, source_target_pairs={{0,64},{32,96},{64,0},{96,32},{1,65},{33,97},{65,1},{97,33},{2,66}... | collective-permute-start | bytes 1572872 | tf_op jit(solution)/shard_map/ppermute | solution.py:241
  127.7 23.5 %all-to-all-start = ((f16[4,128,512]{2,1,0:T(8,128)(2,1)}), f16[4,128,512]{2,1,0:T(8,128)(2,1)S(1)}, u32[]{:S(2)}, u32[]{:S(2)}) async-start(f16[4,128,512]{2,1,0:T(8,128)(2,1)} %multiply_convert_fusion.2), calls=%async_computation | async-start | bytes 1048576 | tf_op jit(solution)/shard_map/all_to_all | solution.py:336
  (22 other events, 138.8 us)

commit v7 on v6

--- a/solution.py
+++ b/solution.py
@@ -235,6 +235,29 @@
     )(info, *operands, *acc)
 
 
+def place(z, y, x):
+    return ((z % 4 * 2 + x % 4 // 2) * 4 + y % 4) * 2 + x % 2
+
+
+def to_places(pieces):
+    z, y = lax.axis_index("z"), lax.axis_index("y")
+    total = 0.0
+    for d in range(4):
+        pairs = []
+        for zi in range(4):
+            for yi in range(4):
+                moves = (zi - yi) % 4 == 2
+                if moves or d:
+                    pairs += [
+                        (place(zi, yi, xi), place(zi - moves, yi - moves, xi + d)) for xi in range(4)
+                    ]
+        came = lax.ppermute(pieces[d], ("z", "xh", "y", "xl"), pairs)
+        if d == 0:
+            came = jnp.where(lax.rem(y + 2, 4) == z, came, pieces[0])
+        total = total + came.astype(jnp.float32)
+    return total * 0.25
+
+
 def to_four(pieces, axis):
     total = pieces[0].astype(jnp.float32)
     for d in (1, 2, 3):
@@ -334,11 +357,10 @@
     along_x = to_four(along_x, XS).astype(HALF)
     along_z = to_four(along_z, "z").astype(HALF)
     along_x = mean_of_four(lax.all_to_all(along_x, "z", 0, 0, tiled=True))
-    along_z = to_four(along_z, XS)
-    summed = jnp.concatenate([along_z, along_x], axis=0)
     moves = [((i + 2) % 4 * 4 + i, (i + 1) % 4 * 4 + (i + 3) % 4) for i in range(4)]
-    moved = lax.ppermute(summed.astype(HALF), ("z", "y"), moves).astype(jnp.float32)
-    summed = jnp.where(lax.rem(y + 2, 4) == z, moved, summed)
+    moved = lax.ppermute(along_x.astype(HALF), ("z", "y"), moves).astype(jnp.float32)
+    along_x = jnp.where(lax.rem(y + 2, 4) == z, moved, along_x)
+    summed = jnp.concatenate([to_places(along_z), along_x], axis=0)
     total_sources = sources.shape[0] * count
     return field, summed * jnp.float32(16.0 / (LIFT * total_sources))
 

time: 163 us -> 164 us (level)
  waiting for transfers between devices: 66.4 us -> 56 us
  starting transfers between devices: 47.7 us -> 54.3 us
  local copies, waits for them, and re-layouts: 9.41 us -> 11.5 us
    ppermute x1 -> x5, starting transfers between devices: 1.92 us -> 11.8 us  [the longest x4 7.03 us: to_places(): came = lax.ppermute(pieces[d], ('z', 'xh', 'y', 'xl'), pairs)]
    ppermute x9 -> x6, waiting for transfers between devices: 21.6 us -> 13 us  [to_four(): came = lax.ppermute(pieces[d], axis, [(i, (i + d) % 4) for i in range(4)])]
    ppermute x9 -> x6, starting transfers between devices: 24.3 us -> 20.9 us  [to_four(): came = lax.ppermute(pieces[d], axis, [(i, (i + d) % 4) for i in range(4)])]
    ppermute x1 -> x5, waiting for transfers between devices: 8.44 us -> 6.72 us  [the longest x4 4.33 us: to_places(): came = lax.ppermute(pieces[d], ('z', 'xh', 'y', 'xl'), pairs)]
    unnamed x20 -> x24, local copies, waits for them, and re-layouts: 7.34 us -> 8.13 us
  transfers between devices with their start and end apart: 35 -> 36, of which waited for: 18 -> 16; matrix products, arithmetic and copies ran while one was open for 4% -> 5% of each run, Pallas kernels for 15% -> 15%
where the time goes in v7:
time: 164 us; the launch traced here: 162 us
  waiting for transfers between devices  56 us (34%)
  starting transfers between devices  54.3 us (33%)
  Pallas kernels  32.2 us (20%)
  local copies, waits for them, and re-layouts  11.5 us (7%)
  other arithmetic  6.57 us (4%)
    ppermute x6, starting transfers between devices, to_four(): came = lax.ppermute(pieces[d], axis, [(i, (i + d) % 4) for i in range(4)])  20.9 us
    pallas_call x2, Pallas kernels, stencil(): pl.pallas_call(kernel, grid_spec=pltpu.PrefetchScalarGridSpec(num_scalar_...  17.5 us
    ppermute x2, waiting for transfers between devices, body(): other = lax.ppermute(send, 'xl', SWAP)  14.2 us
    ppermute x6, waiting for transfers between devices, to_four(): came = lax.ppermute(pieces[d], axis, [(i, (i + d) % 4) for i in range(4)])  13 us
    ppermute x4, waiting for transfers between devices, along_y(): last = lax.ppermute(own, 'y', [(i, (i + 1) % 4) for i in range(4)])  12.7 us
    pallas_call x2, Pallas kernels, partial_gram(): pl.pallas_call(lambda *refs: gram_kernel(bool(acc), *refs), in_specs=[pl....  11.5 us
    unnamed x24, local copies, waits for them, and re-layouts  8.13 us
    ppermute x4, starting transfers between devices, to_places(): came = lax.ppermute(pieces[d], ('z', 'xh', 'y', 'xl'), pairs)  7.03 us
  transfers between devices with their start and end apart: 36, of which 16 were waited for; matrix products, arithmetic and copies ran while one was open for 5% of the time, Pallas kernels for 15%

profile of v7, /device:TPU:56, one launch (start us, length us, event | category | flops | bytes accessed | tf_op | source)
XLA Modules:
  0.0 162.4 jit_solution(13222349771924972810)
XLA Ops:
  0.6 2.2 %copy-done = f32[512,8,256]{2,1,0:T(8,128)S(1)} copy-done((f32[512,8,256]{2,1,0:T(8,128)S(1)}, f32[512,8,256]{2,1,0:T(8,128)}, u32[]{:S(2)}) %copy-start) | copy-done | bytes 4194328
  3.6 3.1 %shard_map.68 = (bf16[2,528,256]{2,1,0:T(8,128)(2,1)}, bf16[2,528,256]{2,1,0:T(8,128)(2,1)S(1)}) custom-call(f32[512,8,256]{2,1,0:T(8,128)S(1)} %copy-done, f32[4,8,256]{2,1,0:T(8,128)S(1)} %copy-done.5), custom_call_target="tpu_custom_call" | custom-call | flops 1000 | bytes 6291456 | tf_op jit(solution)/shard_map/pallas_call | solution.py:53
  6.7 3.9 %collective-permute-start.1 = (bf16[2,528,256]{2,1,0:T(8,128)(2,1)}, bf16[2,528,256]{2,1,0:T(8,128)(2,1)S(1)}, u32[]{:S(2)}, u32[]{:S(2)}) collective-permute-start(bf16[2,528,256]{2,1,0:T(8,128)(2,1)} %get-tuple-element.19), channel_id=1, source_target_pairs={{8,0},{16,8},{24,16},{32,24},{40,32},{48,40},{56,48},{64,56},{72,6... | collective-permute-start | bytes 1622024 | tf_op jit(solution)/shard_map/ppermute | solution.py:313
  13.7 2.2 %copy-done.1 = f32[512,8,256]{2,1,0:T(8,128)S(1)} copy-done((f32[512,8,256]{2,1,0:T(8,128)S(1)}, f32[512,8,256]{2,1,0:T(8,128)}, u32[]{:S(2)}) %copy-start.1) | copy-done | bytes 4194328
  15.9 7.3 %shard_map.69 = (f32[512,8,256]{2,1,0:T(8,128)}, bf16[512,512]{1,0:T(8,128)(2,1)S(1)}, bf16[512,512]{1,0:T(8,128)(2,1)S(1)}) custom-call(s32[6]{0:T(128)S(1)} %stack.39.info.refs_0_, f32[512,8,256]{2,1,0:T(8,128)S(1)} %copy-done.1, f32[5,8,256]{2,1,0:T(8,128)S(1)} %pad_maximum_fusion.2.coef_ref, f32[8,256]{1,0:T(8,128)S(1)} %fusion.emis_ref, ...), custom_call_target="tpu_custom_call" | custom-call | flops 1000 | bytes 104857600 | tf_op jit(solution)/shard_map/pallas_call | solution.py:155
  27.0 10.9 %collective-permute-done.9.refs_2_ = bf16[512,512]{1,0:T(8,128)(2,1)S(1)} collective-permute-done((bf16[512,512]{1,0:T(8,128)(2,1)S(1)}, bf16[512,512]{1,0:T(8,128)(2,1)S(1)}, u32[]{:S(2)}, u32[]{:S(2)}) %collective-permute-start.9) | collective-permute-done | bytes 524320 | tf_op jit(solution)/shard_map/ppermute | solution.py:337
  43.4 2.2 %copy-done.2 = f32[512,8,256]{2,1,0:T(8,128)S(1)} copy-done((f32[512,8,256]{2,1,0:T(8,128)S(1)}, f32[512,8,256]{2,1,0:T(8,128)}, u32[]{:S(2)}) %copy-start.2) | copy-done | bytes 4194328
  45.6 10.2 %shard_map.70 = (f32[512,8,256]{2,1,0:T(8,128)}, bf16[512,512]{1,0:T(8,128)(2,1)S(1)}, bf16[512,512]{1,0:T(8,128)(2,1)S(1)}) custom-call(s32[6]{0:T(128)S(1)} %stack.39.info.refs_0_, f32[512,8,256]{2,1,0:T(8,128)S(1)} %copy-done.2, bf16[2,528,256]{2,1,0:T(8,128)(2,1)S(1)} %collective-permute-done.up_ref, ...), custom_call_target="tpu_custom_call", output_to_operand_aliasing={{0}: (7, {})} | custom-call | flops 1000 | bytes 20971520 | tf_op jit(solution)/shard_map/pallas_call | solution.py:155
  56.4 2.3 %collective-permute-start.8 = (bf16[512,512]{1,0:T(8,128)(2,1)S(1)}, bf16[512,512]{1,0:T(8,128)(2,1)S(1)}, u32[]{:S(2)}, u32[]{:S(2)}) collective-permute-start(bf16[512,512]{1,0:T(8,128)(2,1)S(1)} %get-tuple-element.27.refs_1_), channel_id=1, source_target_pairs={{0,2},{2,4},{4,6},{6,0},{1,3},{3,5},{5,7},{7,1},{8,10},{10,12},{12... | collective-permute-start | bytes 1572872 | tf_op jit(solution)/shard_map/ppermute | solution.py:275
  60.4 6.1 %shard_map.71 = (f32[16,128,512]{2,1,0:T(8,128)S(1)}, f32[16,128,512]{2,1,0:T(8,128)S(1)}) custom-call(s32[6]{0:T(128)S(1)} %stack.39.info.refs_0_, bf16[512,512]{1,0:T(8,128)(2,1)S(1)} %get-tuple-element.23.refs_1_, bf16[512,512]{1,0:T(8,128)(2,1)S(1)} %collective-permute-done.9.refs_2_, bf16[512,512]{1,0:T(8,128)(2,1)} %collective-permute-done.10.refs_3_, ...), custom_call_target="tpu_custom_call" | custom-call | flops 1000 | bytes 8388608 | tf_op jit(solution)/shard_map/pallas_call | solution.py:227
  66.4 3.3 %collective-permute-done.4.refs_2_ = bf16[512,512]{1,0:T(8,128)(2,1)S(1)} collective-permute-done((bf16[512,512]{1,0:T(8,128)(2,1)S(1)}, bf16[512,512]{1,0:T(8,128)(2,1)S(1)}, u32[]{:S(2)}, u32[]{:S(2)}) %collective-permute-start.4) | collective-permute-done | bytes 524320 | tf_op jit(solution)/shard_map/ppermute | solution.py:349
  70.8 3.1 %collective-permute-done.7.refs_5_ = bf16[512,512]{1,0:T(8,128)(2,1)S(1)} collective-permute-done((bf16[512,512]{1,0:T(8,128)(2,1)S(1)}, bf16[512,512]{1,0:T(8,128)(2,1)S(1)}, u32[]{:S(2)}, u32[]{:S(2)}) %collective-permute-start.7) | collective-permute-done | bytes 524320 | tf_op jit(solution)/shard_map/ppermute | solution.py:274
  76.5 10.6 %collective-permute-done.21.refs_10_ = bf16[512,512]{1,0:T(8,128)(2,1)S(1)} collective-permute-done((bf16[512,512]{1,0:T(8,128)(2,1)S(1)}, bf16[512,512]{1,0:T(8,128)(2,1)S(1)}, u32[]{:S(2)}, u32[]{:S(2)}) %collective-permute-start.21) | collective-permute-done | bytes 524320 | tf_op jit(solution)/shard_map/ppermute | solution.py:275
  90.5 5.5 %shard_map.72 = (f32[16,128,512]{2,1,0:T(8,128)S(1)}, f32[16,128,512]{2,1,0:T(8,128)S(1)}) custom-call(s32[6]{0:T(128)S(1)} %stack.39.info.refs_0_, bf16[512,512]{1,0:T(8,128)(2,1)S(1)} %get-tuple-element.27.refs_1_, bf16[512,512]{1,0:T(8,128)(2,1)S(1)} %collective-permute-done.4.refs_2_, bf16[512,512]{1,0:T(8,128)(2,1)S(1)} %collective-permute-done.5.refs_3_, ...), custom_call_target="tpu_custom_call" | custom-call | flops 1000 | bytes 8388608 | tf_op jit(solution)/shard_map/pallas_call | solution.py:227
  99.4 2.0 %collective-permute-start.33 = (f16[4,128,512]{2,1,0:T(8,128)(2,1)}, f16[4,128,512]{2,1,0:T(8,128)(2,1)}, u32[]{:S(2)}, u32[]{:S(2)}) collective-permute-start(f16[4,128,512]{2,1,0:T(8,128)(2,1)} %get-tuple-element.40), channel_id=1, source_target_pairs={{0,17},{1,0},{16,1},{17,16},{2,19},{3,2},{18,3},{19,18},{4,21},{5,... | collective-permute-start | bytes 1572872 | tf_op jit(solution)/shard_map/ppermute | solution.py:264
  107.3 6.6 %collective-permute-done.31 = f16[4,128,512]{2,1,0:T(8,128)(2,1)S(1)} collective-permute-done((f16[4,128,512]{2,1,0:T(8,128)(2,1)S(1)}, f16[4,128,512]{2,1,0:T(8,128)(2,1)S(1)}, u32[]{:S(2)}, u32[]{:S(2)}) %collective-permute-start.31) | collective-permute-done | bytes 524320 | tf_op jit(solution)/shard_map/ppermute | solution.py:264
  113.9 13.8 %collective-permute-start.25 = (f16[4,128,512]{2,1,0:T(8,128)(2,1)}, f16[4,128,512]{2,1,0:T(8,128)(2,1)}, u32[]{:S(2)}, u32[]{:S(2)}) collective-permute-start(f16[4,128,512]{2,1,0:T(8,128)(2,1)} %get-tuple-element.38), channel_id=1, source_target_pairs={{0,64},{32,96},{64,0},{96,32},{1,65},{33,97},{65,1},{97,33},{2,66}... | collective-permute-start | bytes 1572872 | tf_op jit(solution)/shard_map/ppermute | solution.py:264
  127.8 2.5 %multiply_convert_fusion.2 = f16[4,128,512]{2,1,0:T(8,128)(2,1)} fusion(f16[4,128,512]{2,1,0:T(8,128)(2,1)} %collective-permute-done.33, f16[4,128,512]{2,1,0:T(8,128)(2,1)} %collective-permute-done.32, f16[4,128,512]{2,1,0:T(8,128)(2,1)S(1)} %collective-permute-done.31, f16[16,128,512]{2,1,0:T(8,128)(2,1)} %copy-done.7), kind=kLoop, calls=%fused_computation.5 | loop fusion | flops 2359296 | bytes 2621440 | tf_op jit(solution)/shard_map/convert_element_type | solution.py:357
  130.2 3.5 %all-to-all-start = ((f16[4,128,512]{2,1,0:T(8,128)(2,1)}), f16[4,128,512]{2,1,0:T(8,128)(2,1)S(1)}, u32[]{:S(2)}, u32[]{:S(2)}) async-start(f16[4,128,512]{2,1,0:T(8,128)(2,1)} %multiply_convert_fusion.2), calls=%async_computation | async-start | bytes 1048576 | tf_op jit(solution)/shard_map/all_to_all | solution.py:359
  134.5 6.4 %collective-permute-done.25 = f16[4,128,512]{2,1,0:T(8,128)(2,1)} collective-permute-done((f16[4,128,512]{2,1,0:T(8,128)(2,1)}, f16[4,128,512]{2,1,0:T(8,128)(2,1)}, u32[]{:S(2)}, u32[]{:S(2)}) %collective-permute-start.25) | collective-permute-done | bytes 524320 | tf_op jit(solution)/shard_map/ppermute | solution.py:264
  144.6 3.2 %collective-permute-start.30 = (f16[128,512]{1,0:T(8,128)(2,1)S(1)}, f16[128,512]{1,0:T(8,128)(2,1)S(1)}, u32[]{:S(2)}, u32[]{:S(2)}) collective-permute-start(f16[128,512]{1,0:T(8,128)(2,1)S(1)} %get-tuple-element.43), channel_id=1, source_target_pairs={{0,17},{1,0},{16,1},{17,16},{2,19},{3,2},{18,3},{19,18},{4,115},{5... | collective-permute-start | bytes 393224 | tf_op jit(solution)/shard_map/ppermute | solution.py:254
  149.9 4.8 %collective-permute-start.34 = (f16[128,512]{1,0:T(8,128)(2,1)S(1)}, f16[128,512]{1,0:T(8,128)(2,1)S(1)}, u32[]{:S(2)}, u32[]{:S(2)}) collective-permute-start(f16[128,512]{1,0:T(8,128)(2,1)S(1)} %multiply_convert_fusion.4), channel_id=1, source_target_pairs={{64,38},{98,64},{4,98},{38,4},{65,39},{99,65},{5,99},{39,5},{72,46... | collective-permute-start | bytes 393224 | tf_op jit(solution)/shard_map/ppermute | solution.py:361
  154.7 4.3 %collective-permute-done.27 = f16[128,512]{1,0:T(8,128)(2,1)S(1)} collective-permute-done((f16[128,512]{1,0:T(8,128)(2,1)S(1)}, f16[128,512]{1,0:T(8,128)(2,1)S(1)}, u32[]{:S(2)}, u32[]{:S(2)}) %collective-permute-start.27) | collective-permute-done | bytes 131104 | tf_op jit(solution)/shard_map/ppermute | solution.py:254
  159.1 2.4 %collective-permute-done.34 = f16[128,512]{1,0:T(8,128)(2,1)S(1)} collective-permute-done((f16[128,512]{1,0:T(8,128)(2,1)S(1)}, f16[128,512]{1,0:T(8,128)(2,1)S(1)}, u32[]{:S(2)}, u32[]{:S(2)}) %collective-permute-start.34) | collective-permute-done | bytes 131104 | tf_op jit(solution)/shard_map/ppermute | solution.py:361
  (114 shorter events, 39.0 us)
Async XLA Ops:
  6.7 17.1 %collective-permute-start.1 = (bf16[2,528,256]{2,1,0:T(8,128)(2,1)}, bf16[2,528,256]{2,1,0:T(8,128)(2,1)S(1)}, u32[]{:S(2)}, u32[]{:S(2)}) collective-permute-start(bf16[2,528,256]{2,1,0:T(8,128)(2,1)} %get-tuple-element.19), channel_id=1, source_target_pairs={{8,0},{16,8},{24,16},{32,24},{40,32},{48,40},{56,48},{64,56},{72,6... | collective-permute-start | bytes 1622024 | tf_op jit(solution)/shard_map/ppermute | solution.py:313
  10.6 13.9 %collective-permute-start = (bf16[2,528,256]{2,1,0:T(8,128)(2,1)S(1)}, bf16[2,528,256]{2,1,0:T(8,128)(2,1)S(1)}, u32[]{:S(2)}, u32[]{:S(2)}) collective-permute-start(bf16[2,528,256]{2,1,0:T(8,128)(2,1)S(1)} %get-tuple-element.20), channel_id=1, source_target_pairs={{0,8},{8,16},{16,24},{24,32},{32,40},{40,48},{48,56},{56,64},{64,7... | collective-permute-start | bytes 1622024 | tf_op jit(solution)/shard_map/ppermute | solution.py:312
  23.2 14.6 %collective-permute-start.9 = (bf16[512,512]{1,0:T(8,128)(2,1)S(1)}, bf16[512,512]{1,0:T(8,128)(2,1)S(1)}, u32[]{:S(2)}, u32[]{:S(2)}) collective-permute-start(bf16[512,512]{1,0:T(8,128)(2,1)S(1)} %get-tuple-element.29), channel_id=1, source_target_pairs={{0,1},{1,0},{2,3},{3,2},{4,5},{5,4},{6,7},{7,6},{8,9},{9,8},{10,11... | collective-permute-start | bytes 1572872 | tf_op jit(solution)/shard_map/ppermute | solution.py:337
  24.5 14.7 %collective-permute-start.3 = (bf16[512,512]{1,0:T(8,128)(2,1)S(1)}, bf16[512,512]{1,0:T(8,128)(2,1)S(1)}, u32[]{:S(2)}, u32[]{:S(2)}) collective-permute-start(bf16[512,512]{1,0:T(8,128)(2,1)S(1)} %get-tuple-element.23.refs_1_), channel_id=1, source_target_pairs={{0,2},{2,4},{4,6},{6,0},{1,3},{3,5},{5,7},{7,1},{8,10},{10,12},{12... | collective-permute-start | bytes 1572872 | tf_op jit(solution)/shard_map/ppermute | solution.py:275
  24.7 15.9 %collective-permute-start.2 = (bf16[512,512]{1,0:T(8,128)(2,1)S(1)}, bf16[512,512]{1,0:T(8,128)(2,1)S(1)}, u32[]{:S(2)}, u32[]{:S(2)}) collective-permute-start(bf16[512,512]{1,0:T(8,128)(2,1)S(1)} %get-tuple-element.23.refs_1_), channel_id=1, source_target_pairs={{2,0},{4,2},{6,4},{0,6},{3,1},{5,3},{7,5},{1,7},{10,8},{12,10},{14... | collective-permute-start | bytes 1572872 | tf_op jit(solution)/shard_map/ppermute | solution.py:274
  26.5 16.4 %collective-permute-start.10 = (bf16[512,512]{1,0:T(8,128)(2,1)S(1)}, bf16[512,512]{1,0:T(8,128)(2,1)}, u32[]{:S(2)}, u32[]{:S(2)}) collective-permute-start(bf16[512,512]{1,0:T(8,128)(2,1)S(1)} %get-tuple-element.23.refs_1_), channel_id=1, source_target_pairs={{0,8},{8,0},{1,9},{9,1},{2,10},{10,2},{3,11},{11,3},{4,12},{12,4},... | collective-permute-start | bytes 1572872 | tf_op jit(solution)/shard_map/ppermute | solution.py:281
  37.8 18.0 %collective-permute-start.11 = (bf16[512,512]{1,0:T(8,128)(2,1)S(1)}, bf16[512,512]{1,0:T(8,128)(2,1)}, u32[]{:S(2)}, u32[]{:S(2)}) collective-permute-start(bf16[512,512]{1,0:T(8,128)(2,1)S(1)} %collective-permute-done.9.refs_2_), channel_id=1, source_target_pairs={{0,8},{8,0},{1,9},{9,1},{2,10},{10,2},{3,11},{11,3},{4,12},{12,4},... | collective-permute-start | bytes 1572872 | tf_op jit(solution)/shard_map/ppermute | solution.py:281
  40.6 15.8 %collective-permute-start.15 = (bf16[512,512]{1,0:T(8,128)(2,1)S(1)}, bf16[512,512]{1,0:T(8,128)(2,1)}, u32[]{:S(2)}, u32[]{:S(2)}) collective-permute-start(bf16[512,512]{1,0:T(8,128)(2,1)S(1)} %collective-permute-done.9.refs_2_), channel_id=1, source_target_pairs={{0,2},{2,4},{4,6},{6,0},{1,3},{3,5},{5,7},{7,1},{8,10},{10,12},{12... | collective-permute-start | bytes 1572872 | tf_op jit(solution)/shard_map/ppermute | solution.py:275
  41.4 17.3 %collective-permute-start.12 = (bf16[512,512]{1,0:T(8,128)(2,1)S(1)}, bf16[512,512]{1,0:T(8,128)(2,1)S(1)}, u32[]{:S(2)}, u32[]{:S(2)}) collective-permute-start(bf16[512,512]{1,0:T(8,128)(2,1)S(1)} %collective-permute-done.9.refs_2_), channel_id=1, source_target_pairs={{2,0},{4,2},{6,4},{0,6},{3,1},{5,3},{7,5},{1,7},{10,8},{12,10},{14... | collective-permute-start | bytes 1572872 | tf_op jit(solution)/shard_map/ppermute | solution.py:274
  42.9 15.9 %collective-permute-start.16 = (bf16[512,512]{1,0:T(8,128)(2,1)}, bf16[512,512]{1,0:T(8,128)(2,1)S(1)}, u32[]{:S(2)}, u32[]{:S(2)}) collective-permute-start(bf16[512,512]{1,0:T(8,128)(2,1)} %copy-done.3), channel_id=1, source_target_pairs={{0,8},{8,0},{1,9},{9,1},{2,10},{10,2},{3,11},{11,3},{4,12},{12,4},... | collective-permute-start | bytes 1572872 | tf_op jit(solution)/shard_map/ppermute | solution.py:283
  55.8 13.9 %collective-permute-start.4 = (bf16[512,512]{1,0:T(8,128)(2,1)S(1)}, bf16[512,512]{1,0:T(8,128)(2,1)S(1)}, u32[]{:S(2)}, u32[]{:S(2)}) collective-permute-start(bf16[512,512]{1,0:T(8,128)(2,1)S(1)} %get-tuple-element.28), channel_id=1, source_target_pairs={{0,1},{1,0},{2,3},{3,2},{4,5},{5,4},{6,7},{7,6},{8,9},{9,8},{10,11... | collective-permute-start | bytes 1572872 | tf_op jit(solution)/shard_map/ppermute | solution.py:349
  56.4 14.3 %collective-permute-start.8 = (bf16[512,512]{1,0:T(8,128)(2,1)S(1)}, bf16[512,512]{1,0:T(8,128)(2,1)S(1)}, u32[]{:S(2)}, u32[]{:S(2)}) collective-permute-start(bf16[512,512]{1,0:T(8,128)(2,1)S(1)} %get-tuple-element.27.refs_1_), channel_id=1, source_target_pairs={{0,2},{2,4},{4,6},{6,0},{1,3},{3,5},{5,7},{7,1},{8,10},{10,12},{12... | collective-permute-start | bytes 1572872 | tf_op jit(solution)/shard_map/ppermute | solution.py:275
  58.7 15.2 %collective-permute-start.7 = (bf16[512,512]{1,0:T(8,128)(2,1)S(1)}, bf16[512,512]{1,0:T(8,128)(2,1)S(1)}, u32[]{:S(2)}, u32[]{:S(2)}) collective-permute-start(bf16[512,512]{1,0:T(8,128)(2,1)S(1)} %get-tuple-element.27.refs_1_), channel_id=1, source_target_pairs={{2,0},{4,2},{6,4},{0,6},{3,1},{5,3},{7,5},{1,7},{10,8},{12,10},{14... | collective-permute-start | bytes 1572872 | tf_op jit(solution)/shard_map/ppermute | solution.py:274
  74.2 14.4 %collective-permute-start.18 = (bf16[512,512]{1,0:T(8,128)(2,1)S(1)}, bf16[512,512]{1,0:T(8,128)(2,1)S(1)}, u32[]{:S(2)}, u32[]{:S(2)}) collective-permute-start(bf16[512,512]{1,0:T(8,128)(2,1)S(1)} %collective-permute-done.4.refs_2_), channel_id=1, source_target_pairs={{2,0},{4,2},{6,4},{0,6},{3,1},{5,3},{7,5},{1,7},{10,8},{12,10},{14... | collective-permute-start | bytes 1572872 | tf_op jit(solution)/shard_map/ppermute | solution.py:274
  75.9 14.2 %collective-permute-start.6 = (bf16[512,512]{1,0:T(8,128)(2,1)S(1)}, bf16[512,512]{1,0:T(8,128)(2,1)S(1)}, u32[]{:S(2)}, u32[]{:S(2)}) collective-permute-start(bf16[512,512]{1,0:T(8,128)(2,1)S(1)} %collective-permute-done.4.refs_2_), channel_id=1, source_target_pairs={{0,8},{8,0},{1,9},{9,1},{2,10},{10,2},{3,11},{11,3},{4,12},{12,4},... | collective-permute-start | bytes 1572872 | tf_op jit(solution)/shard_map/ppermute | solution.py:281
  98.3 15.7 %collective-permute-start.31 = (f16[4,128,512]{2,1,0:T(8,128)(2,1)S(1)}, f16[4,128,512]{2,1,0:T(8,128)(2,1)S(1)}, u32[]{:S(2)}, u32[]{:S(2)}) collective-permute-start(f16[4,128,512]{2,1,0:T(8,128)(2,1)S(1)} %get-tuple-element.39), channel_id=1, source_target_pairs={{0,1},{1,16},{16,17},{17,0},{2,3},{3,18},{18,19},{19,2},{4,5},{5,2... | collective-permute-start | bytes 1572872 | tf_op jit(solution)/shard_map/ppermute | solution.py:264
  99.4 28.3 %collective-permute-start.33 = (f16[4,128,512]{2,1,0:T(8,128)(2,1)}, f16[4,128,512]{2,1,0:T(8,128)(2,1)}, u32[]{:S(2)}, u32[]{:S(2)}) collective-permute-start(f16[4,128,512]{2,1,0:T(8,128)(2,1)} %get-tuple-element.40), channel_id=1, source_target_pairs={{0,17},{1,0},{16,1},{17,16},{2,19},{3,2},{18,3},{19,18},{4,21},{5,... | collective-permute-start | bytes 1572872 | tf_op jit(solution)/shard_map/ppermute | solution.py:264
  101.5 26.3 %collective-permute-start.32 = (f16[4,128,512]{2,1,0:T(8,128)(2,1)}, f16[4,128,512]{2,1,0:T(8,128)(2,1)}, u32[]{:S(2)}, u32[]{:S(2)}) collective-permute-start(f16[4,128,512]{2,1,0:T(8,128)(2,1)} %get-tuple-element.41), channel_id=1, source_target_pairs={{0,16},{1,17},{16,0},{17,1},{2,18},{3,19},{18,2},{19,3},{4,20},{5,... | collective-permute-start | bytes 1572872 | tf_op jit(solution)/shard_map/ppermute | solution.py:264
  105.3 28.4 %collective-permute-start.24 = (f16[4,128,512]{2,1,0:T(8,128)(2,1)}, f16[4,128,512]{2,1,0:T(8,128)(2,1)S(1)}, u32[]{:S(2)}, u32[]{:S(2)}) collective-permute-start(f16[4,128,512]{2,1,0:T(8,128)(2,1)} %get-tuple-element.36), channel_id=1, source_target_pairs={{0,32},{32,64},{64,96},{96,0},{1,33},{33,65},{65,97},{97,1},{2,34}... | collective-permute-start | bytes 1572872 | tf_op jit(solution)/shard_map/ppermute | solution.py:264
  107.2 26.5 %collective-permute-start.26 = (f16[4,128,512]{2,1,0:T(8,128)(2,1)}, f16[4,128,512]{2,1,0:T(8,128)(2,1)}, u32[]{:S(2)}, u32[]{:S(2)}) collective-permute-start(f16[4,128,512]{2,1,0:T(8,128)(2,1)} %get-tuple-element.37), channel_id=1, source_target_pairs={{0,96},{32,0},{64,32},{96,64},{1,97},{33,1},{65,33},{97,65},{2,98}... | collective-permute-start | bytes 1572872 | tf_op jit(solution)/shard_map/ppermute | solution.py:264
  113.9 27.0 %collective-permute-start.25 = (f16[4,128,512]{2,1,0:T(8,128)(2,1)}, f16[4,128,512]{2,1,0:T(8,128)(2,1)}, u32[]{:S(2)}, u32[]{:S(2)}) collective-permute-start(f16[4,128,512]{2,1,0:T(8,128)(2,1)} %get-tuple-element.38), channel_id=1, source_target_pairs={{0,64},{32,96},{64,0},{96,32},{1,65},{33,97},{65,1},{97,33},{2,66}... | collective-permute-start | bytes 1572872 | tf_op jit(solution)/shard_map/ppermute | solution.py:264
  130.2 19.5 %all-to-all-start = ((f16[4,128,512]{2,1,0:T(8,128)(2,1)}), f16[4,128,512]{2,1,0:T(8,128)(2,1)S(1)}, u32[]{:S(2)}, u32[]{:S(2)}) async-start(f16[4,128,512]{2,1,0:T(8,128)(2,1)} %multiply_convert_fusion.2), calls=%async_computation | async-start | bytes 1048576 | tf_op jit(solution)/shard_map/all_to_all | solution.py:359
  142.7 16.3 %collective-permute-start.27 = (f16[128,512]{1,0:T(8,128)(2,1)S(1)}, f16[128,512]{1,0:T(8,128)(2,1)S(1)}, u32[]{:S(2)}, u32[]{:S(2)}) collective-permute-start(f16[128,512]{1,0:T(8,128)(2,1)S(1)} %get-tuple-element.42), channel_id=1, source_target_pairs={{4,98},{5,99},{20,114},{21,115},{38,4},{39,5},{54,20},{55,21},{64,... | collective-permute-start | bytes 393224 | tf_op jit(solution)/shard_map/ppermute | solution.py:254
  144.6 14.4 %collective-permute-start.30 = (f16[128,512]{1,0:T(8,128)(2,1)S(1)}, f16[128,512]{1,0:T(8,128)(2,1)S(1)}, u32[]{:S(2)}, u32[]{:S(2)}) collective-permute-start(f16[128,512]{1,0:T(8,128)(2,1)S(1)} %get-tuple-element.43), channel_id=1, source_target_pairs={{0,17},{1,0},{16,1},{17,16},{2,19},{3,2},{18,3},{19,18},{4,115},{5... | collective-permute-start | bytes 393224 | tf_op jit(solution)/shard_map/ppermute | solution.py:254
  (25 other events, 177.2 us)

commit v8 on v6

--- a/solution.py
+++ b/solution.py
@@ -335,10 +335,12 @@
     along_z = to_four(along_z, "z").astype(HALF)
     along_x = mean_of_four(lax.all_to_all(along_x, "z", 0, 0, tiled=True))
     along_z = to_four(along_z, XS)
-    summed = jnp.concatenate([along_z, along_x], axis=0)
     moves = [((i + 2) % 4 * 4 + i, (i + 1) % 4 * 4 + (i + 3) % 4) for i in range(4)]
-    moved = lax.ppermute(summed.astype(HALF), ("z", "y"), moves).astype(jnp.float32)
-    summed = jnp.where(lax.rem(y + 2, 4) == z, moved, summed)
+    halves = []
+    for part in (along_z, along_x):
+        moved = lax.ppermute(part.astype(HALF), ("z", "y"), moves).astype(jnp.float32)
+        halves.append(jnp.where(lax.rem(y + 2, 4) == z, moved, part))
+    summed = jnp.concatenate(halves, axis=0)
     total_sources = sources.shape[0] * count
     return field, summed * jnp.float32(16.0 / (LIFT * total_sources))
 

time: 163 us -> 167 us (1.025); the launches traced: 163 us -> 163 us
  waiting for transfers between devices: 66.4 us -> 60 us
  starting transfers between devices: 47.7 us -> 53.8 us
    ppermute x1 -> x2, starting transfers between devices: 1.92 us -> 7.96 us  [body(): lax.ppermute(part.astype(HALF), ('z', 'y'), moves).astype(jnp.float32)]
    ppermute x1 -> x2, waiting for transfers between devices: 8.44 us -> 2.83 us  [body(): lax.ppermute(part.astype(HALF), ('z', 'y'), moves).astype(jnp.float32)]
    unnamed x20 -> x22, local copies, waits for them, and re-layouts: 7.34 us -> 8.12 us
  transfers between devices with their start and end apart: 35 -> 36, of which waited for: 18 -> 19; matrix products, arithmetic and copies ran while one was open for 4% -> 4% of each run, Pallas kernels for 15% -> 14%
where the time goes in v8:
time: 167 us; the launch traced here: 163 us
  waiting for transfers between devices  60 us (36%)
  starting transfers between devices  53.8 us (32%)
  Pallas kernels  32.2 us (19%)
  local copies, waits for them, and re-layouts  10.2 us (6%)
  other arithmetic  5.3 us (3%)
    ppermute x9, starting transfers between devices, to_four(): came = lax.ppermute(pieces[d], axis, [(i, (i + d) % 4) for i in range(4)])  24.3 us
    ppermute x9, waiting for transfers between devices, to_four(): came = lax.ppermute(pieces[d], axis, [(i, (i + d) % 4) for i in range(4)])  20.8 us
    pallas_call x2, Pallas kernels, stencil(): pl.pallas_call(kernel, grid_spec=pltpu.PrefetchScalarGridSpec(num_scalar_...  17.5 us
    ppermute x2, waiting for transfers between devices, body(): other = lax.ppermute(send, 'xl', SWAP)  14.2 us
    ppermute x4, waiting for transfers between devices, along_y(): last = lax.ppermute(own, 'y', [(i, (i + 1) % 4) for i in range(4)])  12.7 us
    pallas_call x2, Pallas kernels, partial_gram(): pl.pallas_call(lambda *refs: gram_kernel(bool(acc), *refs), in_specs=[pl....  11.5 us
    unnamed x22, local copies, waits for them, and re-layouts  8.12 us
    ppermute x2, starting transfers between devices, body(): lax.ppermute(part.astype(HALF), ('z', 'y'), moves).astype(jnp.float32)  7.96 us
  transfers between devices with their start and end apart: 36, of which 19 were waited for; matrix products, arithmetic and copies ran while one was open for 4% of the time, Pallas kernels for 14%

profile of v8, /device:TPU:56, one launch (start us, length us, event | category | flops | bytes accessed | tf_op | source)
XLA Modules:
  0.0 163.3 jit_solution(11234180981609846818)
XLA Ops:
  0.6 2.2 %copy-done = f32[512,8,256]{2,1,0:T(8,128)S(1)} copy-done((f32[512,8,256]{2,1,0:T(8,128)S(1)}, f32[512,8,256]{2,1,0:T(8,128)}, u32[]{:S(2)}) %copy-start) | copy-done | bytes 4194328
  3.6 3.1 %shard_map.68 = (bf16[2,528,256]{2,1,0:T(8,128)(2,1)}, bf16[2,528,256]{2,1,0:T(8,128)(2,1)S(1)}) custom-call(f32[512,8,256]{2,1,0:T(8,128)S(1)} %copy-done, f32[4,8,256]{2,1,0:T(8,128)S(1)} %copy-done.5), custom_call_target="tpu_custom_call" | custom-call | flops 1000 | bytes 6291456 | tf_op jit(solution)/shard_map/pallas_call | solution.py:53
  6.7 3.9 %collective-permute-start.1 = (bf16[2,528,256]{2,1,0:T(8,128)(2,1)}, bf16[2,528,256]{2,1,0:T(8,128)(2,1)S(1)}, u32[]{:S(2)}, u32[]{:S(2)}) collective-permute-start(bf16[2,528,256]{2,1,0:T(8,128)(2,1)} %get-tuple-element.19), channel_id=1, source_target_pairs={{8,0},{16,8},{24,16},{32,24},{40,32},{48,40},{56,48},{64,56},{72,6... | collective-permute-start | bytes 1622024 | tf_op jit(solution)/shard_map/ppermute | solution.py:290
  13.7 2.2 %copy-done.1 = f32[512,8,256]{2,1,0:T(8,128)S(1)} copy-done((f32[512,8,256]{2,1,0:T(8,128)S(1)}, f32[512,8,256]{2,1,0:T(8,128)}, u32[]{:S(2)}) %copy-start.1) | copy-done | bytes 4194328
  15.9 7.3 %shard_map.69 = (f32[512,8,256]{2,1,0:T(8,128)}, bf16[512,512]{1,0:T(8,128)(2,1)S(1)}, bf16[512,512]{1,0:T(8,128)(2,1)S(1)}) custom-call(s32[6]{0:T(128)S(1)} %stack.39.info.refs_0_, f32[512,8,256]{2,1,0:T(8,128)S(1)} %copy-done.1, f32[5,8,256]{2,1,0:T(8,128)S(1)} %pad_maximum_fusion.2.coef_ref, f32[8,256]{1,0:T(8,128)S(1)} %fusion.emis_ref, ...), custom_call_target="tpu_custom_call" | custom-call | flops 1000 | bytes 104857600 | tf_op jit(solution)/shard_map/pallas_call | solution.py:155
  27.0 10.9 %collective-permute-done.9.refs_2_ = bf16[512,512]{1,0:T(8,128)(2,1)S(1)} collective-permute-done((bf16[512,512]{1,0:T(8,128)(2,1)S(1)}, bf16[512,512]{1,0:T(8,128)(2,1)S(1)}, u32[]{:S(2)}, u32[]{:S(2)}) %collective-permute-start.9) | collective-permute-done | bytes 524320 | tf_op jit(solution)/shard_map/ppermute | solution.py:314
  43.4 2.2 %copy-done.2 = f32[512,8,256]{2,1,0:T(8,128)S(1)} copy-done((f32[512,8,256]{2,1,0:T(8,128)S(1)}, f32[512,8,256]{2,1,0:T(8,128)}, u32[]{:S(2)}) %copy-start.2) | copy-done | bytes 4194328
  45.6 10.2 %shard_map.70 = (f32[512,8,256]{2,1,0:T(8,128)}, bf16[512,512]{1,0:T(8,128)(2,1)S(1)}, bf16[512,512]{1,0:T(8,128)(2,1)S(1)}) custom-call(s32[6]{0:T(128)S(1)} %stack.39.info.refs_0_, f32[512,8,256]{2,1,0:T(8,128)S(1)} %copy-done.2, bf16[2,528,256]{2,1,0:T(8,128)(2,1)S(1)} %collective-permute-done.up_ref, ...), custom_call_target="tpu_custom_call", output_to_operand_aliasing={{0}: (7, {})} | custom-call | flops 1000 | bytes 20971520 | tf_op jit(solution)/shard_map/pallas_call | solution.py:155
  56.4 2.3 %collective-permute-start.8 = (bf16[512,512]{1,0:T(8,128)(2,1)S(1)}, bf16[512,512]{1,0:T(8,128)(2,1)S(1)}, u32[]{:S(2)}, u32[]{:S(2)}) collective-permute-start(bf16[512,512]{1,0:T(8,128)(2,1)S(1)} %get-tuple-element.27.refs_1_), channel_id=1, source_target_pairs={{0,2},{2,4},{4,6},{6,0},{1,3},{3,5},{5,7},{7,1},{8,10},{10,12},{12... | collective-permute-start | bytes 1572872 | tf_op jit(solution)/shard_map/ppermute | solution.py:252
  60.4 6.1 %shard_map.71 = (f32[16,128,512]{2,1,0:T(8,128)S(1)}, f32[16,128,512]{2,1,0:T(8,128)S(1)}) custom-call(s32[6]{0:T(128)S(1)} %stack.39.info.refs_0_, bf16[512,512]{1,0:T(8,128)(2,1)S(1)} %get-tuple-element.23.refs_1_, bf16[512,512]{1,0:T(8,128)(2,1)S(1)} %collective-permute-done.9.refs_2_, bf16[512,512]{1,0:T(8,128)(2,1)} %collective-permute-done.10.refs_3_, ...), custom_call_target="tpu_custom_call" | custom-call | flops 1000 | bytes 8388608 | tf_op jit(solution)/shard_map/pallas_call | solution.py:227
  66.5 3.3 %collective-permute-done.4.refs_2_ = bf16[512,512]{1,0:T(8,128)(2,1)S(1)} collective-permute-done((bf16[512,512]{1,0:T(8,128)(2,1)S(1)}, bf16[512,512]{1,0:T(8,128)(2,1)S(1)}, u32[]{:S(2)}, u32[]{:S(2)}) %collective-permute-start.4) | collective-permute-done | bytes 524320 | tf_op jit(solution)/shard_map/ppermute | solution.py:326
  70.8 3.1 %collective-permute-done.7.refs_5_ = bf16[512,512]{1,0:T(8,128)(2,1)S(1)} collective-permute-done((bf16[512,512]{1,0:T(8,128)(2,1)S(1)}, bf16[512,512]{1,0:T(8,128)(2,1)S(1)}, u32[]{:S(2)}, u32[]{:S(2)}) %collective-permute-start.7) | collective-permute-done | bytes 524320 | tf_op jit(solution)/shard_map/ppermute | solution.py:251
  76.5 10.6 %collective-permute-done.21.refs_10_ = bf16[512,512]{1,0:T(8,128)(2,1)S(1)} collective-permute-done((bf16[512,512]{1,0:T(8,128)(2,1)S(1)}, bf16[512,512]{1,0:T(8,128)(2,1)S(1)}, u32[]{:S(2)}, u32[]{:S(2)}) %collective-permute-start.21) | collective-permute-done | bytes 524320 | tf_op jit(solution)/shard_map/ppermute | solution.py:252
  90.5 5.5 %shard_map.72 = (f32[16,128,512]{2,1,0:T(8,128)S(1)}, f32[16,128,512]{2,1,0:T(8,128)S(1)}) custom-call(s32[6]{0:T(128)S(1)} %stack.39.info.refs_0_, bf16[512,512]{1,0:T(8,128)(2,1)S(1)} %get-tuple-element.27.refs_1_, bf16[512,512]{1,0:T(8,128)(2,1)S(1)} %collective-permute-done.4.refs_2_, bf16[512,512]{1,0:T(8,128)(2,1)S(1)} %collective-permute-done.5.refs_3_, ...), custom_call_target="tpu_custom_call" | custom-call | flops 1000 | bytes 8388608 | tf_op jit(solution)/shard_map/pallas_call | solution.py:227
  98.2 2.0 %collective-permute-start.33 = (f16[4,128,512]{2,1,0:T(8,128)(2,1)S(1)}, f16[4,128,512]{2,1,0:T(8,128)(2,1)S(1)}, u32[]{:S(2)}, u32[]{:S(2)}) collective-permute-start(f16[4,128,512]{2,1,0:T(8,128)(2,1)S(1)} %get-tuple-element.40), channel_id=1, source_target_pairs={{0,17},{1,0},{16,1},{17,16},{2,19},{3,2},{18,3},{19,18},{4,21},{5,... | collective-permute-start | bytes 1572872 | tf_op jit(solution)/shard_map/ppermute | solution.py:241
  106.2 6.6 %collective-permute-done.31 = f16[4,128,512]{2,1,0:T(8,128)(2,1)S(1)} collective-permute-done((f16[4,128,512]{2,1,0:T(8,128)(2,1)S(1)}, f16[4,128,512]{2,1,0:T(8,128)(2,1)S(1)}, u32[]{:S(2)}, u32[]{:S(2)}) %collective-permute-start.31) | collective-permute-done | bytes 524320 | tf_op jit(solution)/shard_map/ppermute | solution.py:241
  112.7 13.8 %collective-permute-start.25 = (f16[4,128,512]{2,1,0:T(8,128)(2,1)}, f16[4,128,512]{2,1,0:T(8,128)(2,1)}, u32[]{:S(2)}, u32[]{:S(2)}) collective-permute-start(f16[4,128,512]{2,1,0:T(8,128)(2,1)} %get-tuple-element.38), channel_id=1, source_target_pairs={{0,64},{32,96},{64,0},{96,32},{1,65},{33,97},{65,1},{97,33},{2,66}... | collective-permute-start | bytes 1572872 | tf_op jit(solution)/shard_map/ppermute | solution.py:241
  127.7 3.5 %all-to-all-start = ((f16[4,128,512]{2,1,0:T(8,128)(2,1)}), f16[4,128,512]{2,1,0:T(8,128)(2,1)S(1)}, u32[]{:S(2)}, u32[]{:S(2)}) async-start(f16[4,128,512]{2,1,0:T(8,128)(2,1)} %multiply_convert_fusion.2), calls=%async_computation | async-start | bytes 1048576 | tf_op jit(solution)/shard_map/all_to_all | solution.py:336
  132.0 7.8 %collective-permute-done.25 = f16[4,128,512]{2,1,0:T(8,128)(2,1)} collective-permute-done((f16[4,128,512]{2,1,0:T(8,128)(2,1)}, f16[4,128,512]{2,1,0:T(8,128)(2,1)}, u32[]{:S(2)}, u32[]{:S(2)}) %collective-permute-start.25) | collective-permute-done | bytes 524320 | tf_op jit(solution)/shard_map/ppermute | solution.py:241
  141.6 3.2 %collective-permute-start.29 = (f16[128,512]{1,0:T(8,128)(2,1)S(1)}, f16[128,512]{1,0:T(8,128)(2,1)S(1)}, u32[]{:S(2)}, u32[]{:S(2)}) collective-permute-start(f16[128,512]{1,0:T(8,128)(2,1)S(1)} %get-tuple-element.43), channel_id=1, source_target_pairs={{0,17},{1,0},{16,1},{17,16},{2,19},{3,2},{18,3},{19,18},{4,21},{5,... | collective-permute-start | bytes 393224 | tf_op jit(solution)/shard_map/ppermute | solution.py:241
  144.8 3.8 %collective-permute-done.27 = f16[128,512]{1,0:T(8,128)(2,1)S(1)} collective-permute-done((f16[128,512]{1,0:T(8,128)(2,1)S(1)}, f16[128,512]{1,0:T(8,128)(2,1)S(1)}, u32[]{:S(2)}, u32[]{:S(2)}) %collective-permute-start.27) | collective-permute-done | bytes 131104 | tf_op jit(solution)/shard_map/ppermute | solution.py:241
  148.7 2.5 %collective-permute-done.28 = f16[128,512]{1,0:T(8,128)(2,1)S(1)} collective-permute-done((f16[128,512]{1,0:T(8,128)(2,1)S(1)}, f16[128,512]{1,0:T(8,128)(2,1)S(1)}, u32[]{:S(2)}, u32[]{:S(2)}) %collective-permute-start.28) | collective-permute-done | bytes 131104 | tf_op jit(solution)/shard_map/ppermute | solution.py:241
  153.4 6.0 %collective-permute-start.34 = (f16[128,512]{1,0:T(8,128)(2,1)S(1)}, f16[128,512]{1,0:T(8,128)(2,1)S(1)}, u32[]{:S(2)}, u32[]{:S(2)}) collective-permute-start(f16[128,512]{1,0:T(8,128)(2,1)S(1)} %multiply_convert_fusion.4), channel_id=1, source_target_pairs={{64,38},{98,64},{4,98},{38,4},{65,39},{99,65},{5,99},{39,5},{72,46... | collective-permute-start | bytes 393224 | tf_op jit(solution)/shard_map/ppermute | solution.py:341
  160.4 2.0 %collective-permute-done.34 = f16[128,512]{1,0:T(8,128)(2,1)S(1)} collective-permute-done((f16[128,512]{1,0:T(8,128)(2,1)S(1)}, f16[128,512]{1,0:T(8,128)(2,1)S(1)}, u32[]{:S(2)}, u32[]{:S(2)}) %collective-permute-start.34) | collective-permute-done | bytes 131104 | tf_op jit(solution)/shard_map/ppermute | solution.py:341
  (113 shorter events, 38.1 us)
Async XLA Ops:
  6.7 17.1 %collective-permute-start.1 = (bf16[2,528,256]{2,1,0:T(8,128)(2,1)}, bf16[2,528,256]{2,1,0:T(8,128)(2,1)S(1)}, u32[]{:S(2)}, u32[]{:S(2)}) collective-permute-start(bf16[2,528,256]{2,1,0:T(8,128)(2,1)} %get-tuple-element.19), channel_id=1, source_target_pairs={{8,0},{16,8},{24,16},{32,24},{40,32},{48,40},{56,48},{64,56},{72,6... | collective-permute-start | bytes 1622024 | tf_op jit(solution)/shard_map/ppermute | solution.py:290
  10.6 13.9 %collective-permute-start = (bf16[2,528,256]{2,1,0:T(8,128)(2,1)S(1)}, bf16[2,528,256]{2,1,0:T(8,128)(2,1)S(1)}, u32[]{:S(2)}, u32[]{:S(2)}) collective-permute-start(bf16[2,528,256]{2,1,0:T(8,128)(2,1)S(1)} %get-tuple-element.20), channel_id=1, source_target_pairs={{0,8},{8,16},{16,24},{24,32},{32,40},{40,48},{48,56},{56,64},{64,7... | collective-permute-start | bytes 1622024 | tf_op jit(solution)/shard_map/ppermute | solution.py:289
  23.2 14.6 %collective-permute-start.9 = (bf16[512,512]{1,0:T(8,128)(2,1)S(1)}, bf16[512,512]{1,0:T(8,128)(2,1)S(1)}, u32[]{:S(2)}, u32[]{:S(2)}) collective-permute-start(bf16[512,512]{1,0:T(8,128)(2,1)S(1)} %get-tuple-element.29), channel_id=1, source_target_pairs={{0,1},{1,0},{2,3},{3,2},{4,5},{5,4},{6,7},{7,6},{8,9},{9,8},{10,11... | collective-permute-start | bytes 1572872 | tf_op jit(solution)/shard_map/ppermute | solution.py:314
  24.5 14.7 %collective-permute-start.3 = (bf16[512,512]{1,0:T(8,128)(2,1)S(1)}, bf16[512,512]{1,0:T(8,128)(2,1)S(1)}, u32[]{:S(2)}, u32[]{:S(2)}) collective-permute-start(bf16[512,512]{1,0:T(8,128)(2,1)S(1)} %get-tuple-element.23.refs_1_), channel_id=1, source_target_pairs={{0,2},{2,4},{4,6},{6,0},{1,3},{3,5},{5,7},{7,1},{8,10},{10,12},{12... | collective-permute-start | bytes 1572872 | tf_op jit(solution)/shard_map/ppermute | solution.py:252
  24.7 15.9 %collective-permute-start.2 = (bf16[512,512]{1,0:T(8,128)(2,1)S(1)}, bf16[512,512]{1,0:T(8,128)(2,1)S(1)}, u32[]{:S(2)}, u32[]{:S(2)}) collective-permute-start(bf16[512,512]{1,0:T(8,128)(2,1)S(1)} %get-tuple-element.23.refs_1_), channel_id=1, source_target_pairs={{2,0},{4,2},{6,4},{0,6},{3,1},{5,3},{7,5},{1,7},{10,8},{12,10},{14... | collective-permute-start | bytes 1572872 | tf_op jit(solution)/shard_map/ppermute | solution.py:251
  26.5 16.4 %collective-permute-start.10 = (bf16[512,512]{1,0:T(8,128)(2,1)S(1)}, bf16[512,512]{1,0:T(8,128)(2,1)}, u32[]{:S(2)}, u32[]{:S(2)}) collective-permute-start(bf16[512,512]{1,0:T(8,128)(2,1)S(1)} %get-tuple-element.23.refs_1_), channel_id=1, source_target_pairs={{0,8},{8,0},{1,9},{9,1},{2,10},{10,2},{3,11},{11,3},{4,12},{12,4},... | collective-permute-start | bytes 1572872 | tf_op jit(solution)/shard_map/ppermute | solution.py:258
  37.9 18.0 %collective-permute-start.11 = (bf16[512,512]{1,0:T(8,128)(2,1)S(1)}, bf16[512,512]{1,0:T(8,128)(2,1)}, u32[]{:S(2)}, u32[]{:S(2)}) collective-permute-start(bf16[512,512]{1,0:T(8,128)(2,1)S(1)} %collective-permute-done.9.refs_2_), channel_id=1, source_target_pairs={{0,8},{8,0},{1,9},{9,1},{2,10},{10,2},{3,11},{11,3},{4,12},{12,4},... | collective-permute-start | bytes 1572872 | tf_op jit(solution)/shard_map/ppermute | solution.py:258
  40.6 15.8 %collective-permute-start.15 = (bf16[512,512]{1,0:T(8,128)(2,1)S(1)}, bf16[512,512]{1,0:T(8,128)(2,1)}, u32[]{:S(2)}, u32[]{:S(2)}) collective-permute-start(bf16[512,512]{1,0:T(8,128)(2,1)S(1)} %collective-permute-done.9.refs_2_), channel_id=1, source_target_pairs={{0,2},{2,4},{4,6},{6,0},{1,3},{3,5},{5,7},{7,1},{8,10},{10,12},{12... | collective-permute-start | bytes 1572872 | tf_op jit(solution)/shard_map/ppermute | solution.py:252
  41.4 17.3 %collective-permute-start.12 = (bf16[512,512]{1,0:T(8,128)(2,1)S(1)}, bf16[512,512]{1,0:T(8,128)(2,1)S(1)}, u32[]{:S(2)}, u32[]{:S(2)}) collective-permute-start(bf16[512,512]{1,0:T(8,128)(2,1)S(1)} %collective-permute-done.9.refs_2_), channel_id=1, source_target_pairs={{2,0},{4,2},{6,4},{0,6},{3,1},{5,3},{7,5},{1,7},{10,8},{12,10},{14... | collective-permute-start | bytes 1572872 | tf_op jit(solution)/shard_map/ppermute | solution.py:251
  42.8 13.6 %collective-permute-start.13 = (bf16[256,512]{1,0:T(8,128)(2,1)S(1)}, bf16[256,512]{1,0:T(8,128)(2,1)S(1)}, u32[]{:S(2)}, u32[]{:S(2)}) collective-permute-start(bf16[256,512]{1,0:T(8,128)(2,1)S(1)} %slice.135), channel_id=1, source_target_pairs={{0,8},{8,0},{1,9},{9,1},{2,10},{10,2},{3,11},{11,3},{4,12},{12,4},... | collective-permute-start | bytes 786440 | tf_op jit(solution)/shard_map/ppermute | solution.py:259
  42.9 15.9 %collective-permute-start.16 = (bf16[512,512]{1,0:T(8,128)(2,1)}, bf16[512,512]{1,0:T(8,128)(2,1)S(1)}, u32[]{:S(2)}, u32[]{:S(2)}) collective-permute-start(bf16[512,512]{1,0:T(8,128)(2,1)} %copy-done.3), channel_id=1, source_target_pairs={{0,8},{8,0},{1,9},{9,1},{2,10},{10,2},{3,11},{11,3},{4,12},{12,4},... | collective-permute-start | bytes 1572872 | tf_op jit(solution)/shard_map/ppermute | solution.py:260
  55.8 13.9 %collective-permute-start.4 = (bf16[512,512]{1,0:T(8,128)(2,1)S(1)}, bf16[512,512]{1,0:T(8,128)(2,1)S(1)}, u32[]{:S(2)}, u32[]{:S(2)}) collective-permute-start(bf16[512,512]{1,0:T(8,128)(2,1)S(1)} %get-tuple-element.28), channel_id=1, source_target_pairs={{0,1},{1,0},{2,3},{3,2},{4,5},{5,4},{6,7},{7,6},{8,9},{9,8},{10,11... | collective-permute-start | bytes 1572872 | tf_op jit(solution)/shard_map/ppermute | solution.py:326
  56.4 14.3 %collective-permute-start.8 = (bf16[512,512]{1,0:T(8,128)(2,1)S(1)}, bf16[512,512]{1,0:T(8,128)(2,1)S(1)}, u32[]{:S(2)}, u32[]{:S(2)}) collective-permute-start(bf16[512,512]{1,0:T(8,128)(2,1)S(1)} %get-tuple-element.27.refs_1_), channel_id=1, source_target_pairs={{0,2},{2,4},{4,6},{6,0},{1,3},{3,5},{5,7},{7,1},{8,10},{10,12},{12... | collective-permute-start | bytes 1572872 | tf_op jit(solution)/shard_map/ppermute | solution.py:252
  58.7 15.2 %collective-permute-start.7 = (bf16[512,512]{1,0:T(8,128)(2,1)S(1)}, bf16[512,512]{1,0:T(8,128)(2,1)S(1)}, u32[]{:S(2)}, u32[]{:S(2)}) collective-permute-start(bf16[512,512]{1,0:T(8,128)(2,1)S(1)} %get-tuple-element.27.refs_1_), channel_id=1, source_target_pairs={{2,0},{4,2},{6,4},{0,6},{3,1},{5,3},{7,5},{1,7},{10,8},{12,10},{14... | collective-permute-start | bytes 1572872 | tf_op jit(solution)/shard_map/ppermute | solution.py:251
  74.2 14.4 %collective-permute-start.18 = (bf16[512,512]{1,0:T(8,128)(2,1)S(1)}, bf16[512,512]{1,0:T(8,128)(2,1)S(1)}, u32[]{:S(2)}, u32[]{:S(2)}) collective-permute-start(bf16[512,512]{1,0:T(8,128)(2,1)S(1)} %collective-permute-done.4.refs_2_), channel_id=1, source_target_pairs={{2,0},{4,2},{6,4},{0,6},{3,1},{5,3},{7,5},{1,7},{10,8},{12,10},{14... | collective-permute-start | bytes 1572872 | tf_op jit(solution)/shard_map/ppermute | solution.py:251
  76.0 14.2 %collective-permute-start.6 = (bf16[512,512]{1,0:T(8,128)(2,1)S(1)}, bf16[512,512]{1,0:T(8,128)(2,1)S(1)}, u32[]{:S(2)}, u32[]{:S(2)}) collective-permute-start(bf16[512,512]{1,0:T(8,128)(2,1)S(1)} %collective-permute-done.4.refs_2_), channel_id=1, source_target_pairs={{0,8},{8,0},{1,9},{9,1},{2,10},{10,2},{3,11},{11,3},{4,12},{12,4},... | collective-permute-start | bytes 1572872 | tf_op jit(solution)/shard_map/ppermute | solution.py:258
  76.5 13.7 %collective-permute-start.22 = (bf16[512,512]{1,0:T(8,128)(2,1)S(1)}, bf16[512,512]{1,0:T(8,128)(2,1)S(1)}, u32[]{:S(2)}, u32[]{:S(2)}) collective-permute-start(bf16[512,512]{1,0:T(8,128)(2,1)S(1)} %collective-permute-done.8.refs_9_), channel_id=1, source_target_pairs={{0,8},{8,0},{1,9},{9,1},{2,10},{10,2},{3,11},{11,3},{4,12},{12,4},... | collective-permute-start | bytes 1572872 | tf_op jit(solution)/shard_map/ppermute | solution.py:260
  97.0 15.8 %collective-permute-start.31 = (f16[4,128,512]{2,1,0:T(8,128)(2,1)S(1)}, f16[4,128,512]{2,1,0:T(8,128)(2,1)S(1)}, u32[]{:S(2)}, u32[]{:S(2)}) collective-permute-start(f16[4,128,512]{2,1,0:T(8,128)(2,1)S(1)} %get-tuple-element.39), channel_id=1, source_target_pairs={{0,1},{1,16},{16,17},{17,0},{2,3},{3,18},{18,19},{19,2},{4,5},{5,2... | collective-permute-start | bytes 1572872 | tf_op jit(solution)/shard_map/ppermute | solution.py:241
  98.2 28.3 %collective-permute-start.33 = (f16[4,128,512]{2,1,0:T(8,128)(2,1)S(1)}, f16[4,128,512]{2,1,0:T(8,128)(2,1)S(1)}, u32[]{:S(2)}, u32[]{:S(2)}) collective-permute-start(f16[4,128,512]{2,1,0:T(8,128)(2,1)S(1)} %get-tuple-element.40), channel_id=1, source_target_pairs={{0,17},{1,0},{16,1},{17,16},{2,19},{3,2},{18,3},{19,18},{4,21},{5,... | collective-permute-start | bytes 1572872 | tf_op jit(solution)/shard_map/ppermute | solution.py:241
  100.3 26.3 %collective-permute-start.32 = (f16[4,128,512]{2,1,0:T(8,128)(2,1)S(1)}, f16[4,128,512]{2,1,0:T(8,128)(2,1)S(1)}, u32[]{:S(2)}, u32[]{:S(2)}) collective-permute-start(f16[4,128,512]{2,1,0:T(8,128)(2,1)S(1)} %get-tuple-element.41), channel_id=1, source_target_pairs={{0,16},{1,17},{16,0},{17,1},{2,18},{3,19},{18,2},{19,3},{4,20},{5,... | collective-permute-start | bytes 1572872 | tf_op jit(solution)/shard_map/ppermute | solution.py:241
  104.1 27.0 %collective-permute-start.24 = (f16[4,128,512]{2,1,0:T(8,128)(2,1)}, f16[4,128,512]{2,1,0:T(8,128)(2,1)S(1)}, u32[]{:S(2)}, u32[]{:S(2)}) collective-permute-start(f16[4,128,512]{2,1,0:T(8,128)(2,1)} %get-tuple-element.36), channel_id=1, source_target_pairs={{0,32},{32,64},{64,96},{96,0},{1,33},{33,65},{65,97},{97,1},{2,34}... | collective-permute-start | bytes 1572872 | tf_op jit(solution)/shard_map/ppermute | solution.py:241
  106.1 25.1 %collective-permute-start.26 = (f16[4,128,512]{2,1,0:T(8,128)(2,1)}, f16[4,128,512]{2,1,0:T(8,128)(2,1)}, u32[]{:S(2)}, u32[]{:S(2)}) collective-permute-start(f16[4,128,512]{2,1,0:T(8,128)(2,1)} %get-tuple-element.37), channel_id=1, source_target_pairs={{0,96},{32,0},{64,32},{96,64},{1,97},{33,1},{65,33},{97,65},{2,98}... | collective-permute-start | bytes 1572872 | tf_op jit(solution)/shard_map/ppermute | solution.py:241
  112.7 27.0 %collective-permute-start.25 = (f16[4,128,512]{2,1,0:T(8,128)(2,1)}, f16[4,128,512]{2,1,0:T(8,128)(2,1)}, u32[]{:S(2)}, u32[]{:S(2)}) collective-permute-start(f16[4,128,512]{2,1,0:T(8,128)(2,1)} %get-tuple-element.38), channel_id=1, source_target_pairs={{0,64},{32,96},{64,0},{96,32},{1,65},{33,97},{65,1},{97,33},{2,66}... | collective-permute-start | bytes 1572872 | tf_op jit(solution)/shard_map/ppermute | solution.py:241
  127.7 25.6 %all-to-all-start = ((f16[4,128,512]{2,1,0:T(8,128)(2,1)}), f16[4,128,512]{2,1,0:T(8,128)(2,1)S(1)}, u32[]{:S(2)}, u32[]{:S(2)}) async-start(f16[4,128,512]{2,1,0:T(8,128)(2,1)} %multiply_convert_fusion.2), calls=%async_computation | async-start | bytes 1048576 | tf_op jit(solution)/shard_map/all_to_all | solution.py:336
  (24 other events, 147.2 us)
